TPU v7x, 512 devices: a whole 4x8x8 slice. The times are simulated.
512 devices in a mesh: bins: 64 (over y, z_hi, x), view: 8 (over z_lo, core).
Axes of the slice: x: 4, y: 8, z: 8 (z_hi: 2, z_lo: 4; z = z_hi * 4 + z_lo), core: 2. Of those that a mesh axis runs over, the one named last changes fastest.
Arguments:
- latent_shocks: bfloat16 [65536, 128], P('bins'), may hold values from -6 to 6
- shock_direction: bfloat16 [65536, 128], P('bins'), may hold values from -6 to 6
- coupling_matrix: bfloat16 [5120, 128], P('view'), may hold values from -0.5 to 0.5
- signal_assay_map: int32 [5120], P('view'), may hold values from 0 to 7
- assay_depth_shift: float32 [8, 65536], P(None, 'bins'), may hold values from -3 to -1
- persistence_span: float32 [128], replicated, may hold values from 30 to 131072
- carry_weight: float32 [65536], P('bins'), as said below
- segment_beginnings: int32 [3], replicated, may hold values from 1 to 65535, as said below
Outputs:
- curvature_product: float32 [65536, 128], P('bins')
Inputs may be any that keep to these rules, and one draw needn't show every extreme that they name: `segment_beginnings`: 3 distinct bins; the first is 1 and the last is 65535. `carry_weight`: most entries equal 1; the others lie between 0.5 and 0.8.
All inputs are finite; a program needn't handle non-finite values.
Results may differ from a plain program's by a relative error of at most 0.0003.
Values sent between devices are 32-bit elements; how exact they have to be, the bound alone decides.
No kernel may reach another device: no remote copies, remote signals or barrier semaphores. Data moves between devices by JAX's collectives and lax.ppermute only.
A program may use at most 128 MiB of HBM per device.

v0:
```python
import jax
import jax.numpy as jnp
from jax import lax
from jax.sharding import PartitionSpec as P


def entering(x, axis, combine, identity, reverse):
    peers, here = (lax.axis_size(axis), lax.axis_index(axis))
    everything = jax.tree.map(lambda part: lax.all_gather(part, axis), x)
    start = jax.tree.map(
        lambda part, zero: jnp.broadcast_to(jnp.asarray(zero, part.dtype), part.shape), x, identity
    )

    def hop(k, before):
        at = peers - 1 - k if reverse else k
        reached = at > here if reverse else at < here
        new = combine(before, jax.tree.map(lambda part: part[at], everything))
        return jax.tree.map(lambda a, b: jnp.where(reached, a, b), new, before)

    return lax.fori_loop(0, peers, hop, start)


def compose(early, late):
    head = early[0] * late[0]
    return (head,) + tuple((late[0] * older + newer for older, newer in zip(early[1:], late[1:])))


def shrink_times_boost(persistence_span, carry_weight, segment_beginnings, topmost_line):
    discard_multiplier = 1.0 / persistence_span
    line_indices = topmost_line + jnp.arange(carry_weight.shape[0], dtype=jnp.int32)
    is_start = jnp.any(line_indices[:, None] == segment_beginnings[None, :], axis=1)
    keeping_fraction = (1.0 - discard_multiplier)[None, :] * carry_weight[:, None]
    shrink_multiplier = jnp.where(
        is_start[:, None], jnp.zeros_like(keeping_fraction), keeping_fraction
    )
    return (shrink_multiplier, jnp.sqrt(discard_multiplier * (2.0 - discard_multiplier)))


def weigh_block(latent_b, moved_b, offset_b, coupling_matrix, member):
    contract = (((1,), (1,)), ((), ()))
    log_rate = lax.dot_general(
        latent_b, coupling_matrix, contract, preferred_element_type=jnp.float32
    )
    log_rate = log_rate + lax.dot_general(
        offset_b, member, (((0,), (0,)), ((), ())), precision=lax.Precision.HIGHEST
    )
    along = lax.dot_general(moved_b, coupling_matrix, contract, preferred_element_type=jnp.float32)
    weighted = (jnp.exp(log_rate) * along).astype(jnp.bfloat16)
    return jnp.dot(weighted, coupling_matrix, preferred_element_type=jnp.float32)


def track_terms(latent, moved, assay_depth_shift, coupling_matrix, member):
    row_count = latent.shape[0]
    block = 1024
    nblock = row_count // block
    latent_b = latent.astype(jnp.bfloat16).reshape(nblock, block, latent.shape[1])
    moved_b = moved.astype(jnp.bfloat16).reshape(nblock, block, moved.shape[1])
    offset_b = assay_depth_shift.reshape(assay_depth_shift.shape[0], nblock, block).transpose(
        1, 0, 2
    )
    result = lax.map(
        lambda items: weigh_block(items[0], items[1], items[2], coupling_matrix, member),
        (latent_b, moved_b, offset_b),
    )
    return result.reshape(row_count, latent.shape[1])


def finish(pulled, shrink_multiplier, boost_multiplier, tangent_f):
    flip_m, flip_p = lax.associative_scan(
        compose, (jnp.flip(shrink_multiplier, 0), jnp.flip(shrink_multiplier * pulled, 0))
    )
    suffix_m = jnp.flip(flip_m, 0)
    suffix_p = jnp.flip(flip_p, 0)
    entry_m, entry_p = entering(
        (suffix_m[0], suffix_p[0]),
        "bins",
        compose,
        (jnp.ones_like(suffix_p[0]), jnp.zeros_like(suffix_p[0])),
        True,
    )
    carried = suffix_p + suffix_m * entry_p[None, :]
    p_next = jnp.concatenate([carried[1:], entry_p[None, :]], axis=0)
    adjoint = pulled + p_next
    return boost_multiplier[None, :] * adjoint + tangent_f


def local(
    latent_shocks,
    shock_direction,
    coupling_matrix,
    signal_assay_map,
    assay_depth_shift,
    persistence_span,
    carry_weight,
    segment_beginnings,
):
    row_count = latent_shocks.shape[0]
    topmost_line = lax.axis_index("bins") * row_count
    shrink_multiplier, boost_multiplier = shrink_times_boost(
        persistence_span, carry_weight, segment_beginnings, topmost_line
    )
    tangent_f = shock_direction.astype(jnp.float32)
    prod_run, local_z, local_v = lax.associative_scan(
        compose,
        (
            shrink_multiplier,
            boost_multiplier[None, :] * latent_shocks.astype(jnp.float32),
            boost_multiplier[None, :] * tangent_f,
        ),
    )
    unit = jnp.ones_like(boost_multiplier)
    blank = jnp.zeros_like(boost_multiplier)
    entry_m, entry_z, entry_v = entering(
        (prod_run[-1], local_z[-1], local_v[-1]), "bins", compose, (unit, blank, blank), False
    )
    latent = local_z + prod_run * entry_z[None, :]
    moved = local_v + prod_run * entry_v[None, :]
    member = (
        signal_assay_map[None, :]
        == jnp.arange(assay_depth_shift.shape[0], dtype=jnp.int32)[:, None]
    ).astype(jnp.float32)
    partial_terms = track_terms(latent, moved, assay_depth_shift, coupling_matrix, member)
    pulled = lax.psum(partial_terms, "view")
    return finish(pulled, shrink_multiplier, boost_multiplier, tangent_f)


def solution(mesh):
    in_specs = (
        P("bins", None),
        P("bins", None),
        P("view", None),
        P("view"),
        P(None, "bins"),
        P(),
        P("bins"),
        P(),
    )
    out_specs = P("bins", None)
    return jax.shard_map(local, mesh=mesh, in_specs=in_specs, out_specs=out_specs, check_vma=False)
```

profile of v0, /device:TPU:2, one launch (start us, length us, event | category | flops | bytes accessed | tf_op | source)
XLA Modules:
  0.0 1214.6 jit_solution(1311620277974299498)
XLA Ops:
  6.5 0.7 broadcast_subtract_fusion
  7.2 0.7 compare_reduce_fusion
  8.0 1.0 multiply_select_fusion
  9.0 0.4 slice.767
  9.4 0.4 slice.763
  9.9 0.4 slice.762
  10.3 1.1 convert_multiply_fusion
  11.4 0.4 slice.903
  11.8 0.4 slice.859
  12.2 0.4 slice.858
  12.6 1.4 slice.835
  14.0 0.4 slice.765
  14.4 1.4 slice.764
  15.8 1.0 multiply_add_fusion.1
  16.8 0.3 slice.901
  17.5 0.3 slice.768
  17.8 0.3 slice.833
  21.5 0.7 add.660
  22.3 0.7 add.671
  23.0 0.7 add.699
  23.7 1.1 fusion.12
  24.9 1.2 pad.344
  26.1 217.5 %all-gather = f32[64,1,128]{2,1,0:T(1,128)S(1)} all-gather(f32[1,1,128]{2,1,0:T(1,128)S(1)} %add_bitcast_fusion.4), channel_id=1, replica_groups=mesh['bins'=64,'view'=8] {'bins'}, dimensions={0}, use_global_device_ids=true | all-gather | bytes 33280 | tf_op jit(solution)/shard_map/all_gather | solution.py:9
  243.8 1.2 pad.364
  245.0 220.3 %all-gather.2 = f32[64,1,128]{2,1,0:T(1,128)S(1)} all-gather(f32[1,1,128]{2,1,0:T(1,128)S(1)} %add_bitcast_fusion.2), channel_id=1, replica_groups=mesh['bins'=64,'view'=8] {'bins'}, dimensions={0}, use_global_device_ids=true | all-gather | bytes 33280 | tf_op jit(solution)/shard_map/all_gather | solution.py:9
  465.3 2.6 pad.324
  467.9 0.7 add_bitcast_fusion.3
  468.6 211.6 %all-gather.1 = f32[64,1,128]{2,1,0:T(1,128)S(1)} all-gather(f32[1,1,128]{2,1,0:T(1,128)S(1)} %add_bitcast_fusion.3), channel_id=1, replica_groups=mesh['bins'=64,'view'=8] {'bins'}, dimensions={0}, use_global_device_ids=true | all-gather | bytes 33280 | tf_op jit(solution)/shard_map/all_gather | solution.py:9
  680.2 2.8 while.36
  683.1 2.0 fusion.10
  685.1 2.7 fusion.30
  687.8 4.0 fusion.8
  691.9 1.7 slice.914
  693.6 1.7 slice.908
  695.4 0.4 slice.906
  695.8 0.3 slice.907
  696.1 68.4 %all-reduce.102.cloned.1.call-done = f32[1024,128]{1,0:T(8,128)} async-done(((f32[1024,128]{1,0:T(8,128)}), f32[1024,128]{1,0:T(8,128)}) %all-reduce.102.cloned.1.call-update) | async-done | bytes 524304 | tf_op jit(solution)/shard_map/psum | solution.py:123
  764.5 1.4 fusion.20
  765.9 0.4 slice.982
  766.3 0.4 slice.911
  766.7 0.4 slice.909
  767.5 0.3 slice.980
  768.2 0.3 slice.915
  769.5 0.3 slice.983
  771.9 212.1 %all-gather.4 = f32[64,1,128]{2,1,0:T(1,128)S(1)} all-gather(f32[1,1,128]{2,1,0:T(1,128)S(1)} %add_bitcast_fusion), channel_id=1, replica_groups=mesh['bins'=64,'view'=8] {'bins'}, dimensions={0}, use_global_device_ids=true | all-gather | bytes 33280 | tf_op jit(solution)/shard_map/all_gather | solution.py:9
  984.2 219.6 %all-gather.3 = f32[64,1,128]{2,1,0:T(1,128)S(1)} all-gather(f32[1,1,128]{2,1,0:T(1,128)S(1)} %add_bitcast_fusion.1), channel_id=1, replica_groups=mesh['bins'=64,'view'=8] {'bins'}, dimensions={0}, use_global_device_ids=true | all-gather | bytes 33280 | tf_op jit(solution)/shard_map/all_gather | solution.py:9
  1203.8 3.0 while.37
  1206.9 0.9 convert_add_fusion
  (530 shorter events, 8.9 us)
Async XLA Ops:
  6.5 676.5 %copy-start = (bf16[640,128]{1,0:T(8,128)(2,1)S(1)}, bf16[640,128]{1,0:T(8,128)(2,1)}, u32[]{:S(2)}) copy-start(bf16[640,128]{1,0:T(8,128)(2,1)} %param.14) | copy-start | bytes 491524
  6.5 758.0 %all-reduce.102.cloned.1.call-start = ((), (), s32[]{:S(2)}) async-start(), calls=%async_computation | async-start | bytes 1048576 | tf_op jit(solution)/shard_map/psum | solution.py:123
  9.4 6.3 copy-start.3
  9.9 5.9 copy-start.4
  24.9 655.3 %copy-start.1 = (f32[1024,128]{1,0:T(8,128)}, f32[1024,128]{1,0:T(8,128)S(1)}, u32[]{:S(2)}) copy-start(f32[1024,128]{1,0:T(8,128)S(1)} %pad.343) | copy-start | bytes 1572868
  26.1 656.9 %copy-start.2 = (f32[1024,128]{1,0:T(8,128)}, f32[1024,128]{1,0:T(8,128)S(1)}, u32[]{:S(2)}) copy-start(f32[1024,128]{1,0:T(8,128)S(1)} %pad.344) | copy-start | bytes 1572868
  243.7 439.4 %copy-start.8 = (f32[1024,128]{1,0:T(8,128)}, f32[1024,128]{1,0:T(8,128)S(1)}, u32[]{:S(2)}) copy-start(f32[1024,128]{1,0:T(8,128)S(1)} %pad.323) | copy-start | bytes 1572868
  243.8 439.3 %copy-start.6 = (f32[1024,128]{1,0:T(8,128)}, f32[1024,128]{1,0:T(8,128)S(1)}, u32[]{:S(2)}) copy-start(f32[1024,128]{1,0:T(8,128)S(1)} %pad.363) | copy-start | bytes 1572868
  245.0 438.0 %copy-start.7 = (f32[1024,128]{1,0:T(8,128)}, f32[1024,128]{1,0:T(8,128)S(1)}, u32[]{:S(2)}) copy-start(f32[1024,128]{1,0:T(8,128)S(1)} %pad.364) | copy-start | bytes 1572868
  467.9 217.2 %copy-start.10 = (f32[8,1024]{1,0:T(8,128)S(1)}, f32[8,1024]{1,0:T(8,128)}, u32[]{:S(2)}) copy-start(f32[8,1024]{1,0:T(8,128)} %param.16) | copy-start | bytes 98308
  467.9 217.2 %copy-start.12 = (s32[640]{0:T(1024)S(1)}, s32[640]{0:T(1024)}, u32[]{:S(2)}) copy-start(s32[640]{0:T(1024)} %param.15) | copy-start | bytes 7684
  691.9 72.6 %copy-start.11 = (f32[1024]{0:T(1024)S(1)}, f32[1024]{0:T(1024)}, u32[]{:S(2)}) copy-start(f32[1024]{0:T(1024)} %param.18) | copy-start | bytes 12292
  771.6 435.3 %copy-start.5 = (f32[1024,128]{1,0:T(8,128)S(1)}, f32[1024,128]{1,0:T(8,128)}, u32[]{:S(2)}) copy-start(f32[1024,128]{1,0:T(8,128)} %all-reduce.102.cloned.1.call-done) | copy-start | bytes 1572868
  771.6 435.3 %copy-start.9 = (bf16[1024,128]{1,0:T(8,128)(2,1)S(1)}, bf16[1024,128]{1,0:T(8,128)(2,1)}, u32[]{:S(2)}) copy-start(bf16[1024,128]{1,0:T(8,128)(2,1)} %param.13) | copy-start | bytes 786436
Sparse Core Ops, SparseCore 0:
  692.0 72.4 all-reduce.101
where the time goes:
time: 1220 us; the launch traced here: 1210 us
  blocking collectives  1080 us (89%)
  waiting for transfers between devices  68.4 us (6%)
  local copies, waits for them, and re-layouts  22.2 us (2%)
  between operations  15.8 us (1%)
  other arithmetic  15.2 us (1%)
    all_gather x5, blocking collectives, entering(): everything = jax.tree.map(lambda part: lax.all_gather(part, axis), x)  1080 us
    psum x1, waiting for transfers between devices, local(): pulled = lax.psum(partial_terms, 'view')  68.4 us
  transfers between devices with their start and end apart: 1, of which 1 were waited for; matrix products, arithmetic and copies ran while one was open for 0% of the time, Pallas kernels for 0%

commit v1 on v0

v1 whole, which is shorter than its diff:
```python
import jax
import jax.numpy as jnp
from jax import lax
from jax.experimental import pallas as pl
from jax.experimental.pallas import tpu as pltpu
from jax.sharding import Mesh, PartitionSpec as P

ROWS, K, CHUNKS, STEPS = 1024, 128, 8, 128
PEERS, NVIEW, TRACKS = 64, 8, 640
BLOCK = 256
PART = STEPS + 8
BINS, VIEW = ("y", "zh", "x"), ("zl", "core")
VMEM, SMEM = pltpu.VMEM, pltpu.SMEM


def spec(space):
    return pl.BlockSpec(memory_space=space)


def call(body, ins, outs, scratch=()):
    return pl.pallas_call(
        body,
        in_specs=[spec(s) for s in ins],
        out_specs=[spec(VMEM) for _ in outs],
        out_shape=[jax.ShapeDtypeStruct(shape, dtype) for shape, dtype in outs],
        scratch_shapes=list(scratch),
        compiler_params=pltpu.CompilerParams(vmem_limit_bytes=48 * 1024 * 1024),
    )


def factors(here_ref, begin_ref, span_ref, carry_ref):
    forget = 1.0 / span_ref[...]
    at = (
        here_ref[0] * ROWS
        + lax.broadcasted_iota(jnp.int32, (CHUNKS, STEPS), 0) * STEPS
        + lax.broadcasted_iota(jnp.int32, (CHUNKS, STEPS), 1)
    )
    begins = (at == begin_ref[0]) | (at == begin_ref[1]) | (at == begin_ref[2])
    carry = jnp.where(begins, 0.0, carry_ref[...])
    return 1.0 - forget, jnp.sqrt(forget * (2.0 - forget)), carry


def decay_at(keep, carry, i):
    return jnp.broadcast_to(carry[:, i : i + 1], (CHUNKS, K)) * keep


def rows(ref, i, stride=STEPS):
    return ref[pl.ds(i, CHUNKS, stride=stride), :]


def ends_kernel(here, begin, span, carry_ref, x, d, chunk, sent, xs, ds):
    keep, gain, carry = factors(here, begin, span, carry_ref)
    xs[...] = gain * x[...].astype(jnp.float32)
    ds[...] = gain * d[...].astype(jnp.float32)
    z, v, m = rows(xs, 0), rows(ds, 0), decay_at(keep, carry, 0)
    for i in range(1, STEPS):
        decay = decay_at(keep, carry, i)
        z = decay * z + rows(xs, i)
        v = decay * v + rows(ds, i)
        m = decay * m
    chunk[0] = m
    chunk[1] = z
    chunk[2] = v
    mt, zt, vt = m[0:1], z[0:1], v[0:1]
    for j in range(1, CHUNKS):
        mj = m[j : j + 1]
        mt, zt, vt = mj * mt, mj * zt + z[j : j + 1], mj * vt + v[j : j + 1]
    sent[...] = jnp.broadcast_to(jnp.concatenate([mt, zt, vt], axis=0)[None], sent.shape)


def prepare_kernel(shift, assay, coupling, shift_t, coupling_t):
    s = shift[...]
    hi = s.astype(jnp.bfloat16).astype(jnp.float32)
    mid = (s - hi).astype(jnp.bfloat16).astype(jnp.float32)
    low = s - hi - mid
    blank = jnp.zeros((K - 3 * NVIEW, ROWS), jnp.float32)
    shift_t[...] = jnp.concatenate([hi, mid, low, blank], axis=0).T.astype(jnp.bfloat16)
    member = (
        assay[...] == lax.broadcasted_iota(jnp.int32, (NVIEW, TRACKS), 0)
    ).astype(jnp.float32)
    blank = jnp.zeros((K - 3 * NVIEW, TRACKS), jnp.float32)
    coupling_t[0:K] = coupling[...].astype(jnp.float32).T.astype(jnp.bfloat16)
    coupling_t[K : 2 * K] = jnp.concatenate([member, member, member, blank], axis=0).astype(
        jnp.bfloat16
    )


def tracks_kernel(
    here, begin, span, carry_ref, x, d, chunk, got, shift_t, coupling_t, coupling,
    parts, sent, xs, ds, pulled,
):
    keep, gain, carry = factors(here, begin, span, carry_ref)
    xs[...] = gain * x[...].astype(jnp.float32)
    ds[...] = gain * d[...].astype(jnp.float32)
    ez = jnp.zeros((1, K), jnp.float32)
    ev = jnp.zeros((1, K), jnp.float32)
    for e in range(PEERS - 1):
        m, z, v = got[e, 0:1, :], got[e, 1:2, :], got[e, 2:3, :]
        earlier = e < here[0]
        ez = jnp.where(earlier, m * ez + z, ez)
        ev = jnp.where(earlier, m * ev + v, ev)
    zs, vs = [ez], [ev]
    for j in range(CHUNKS - 1):
        m = chunk[0, j : j + 1, :]
        zs.append(m * zs[-1] + chunk[1, j : j + 1, :])
        vs.append(m * vs[-1] + chunk[2, j : j + 1, :])
    z, v = jnp.concatenate(zs, axis=0), jnp.concatenate(vs, axis=0)
    for i in range(STEPS):
        decay = decay_at(keep, carry, i)
        z = decay * z + rows(xs, i)
        v = decay * v + rows(ds, i)
        xs[pl.ds(i, CHUNKS, stride=STEPS), :] = z
        ds[pl.ds(i, CHUNKS, stride=STEPS), :] = v
    for b in range(ROWS // BLOCK):
        at = pl.ds(b * BLOCK, BLOCK)
        latent = xs[at, :].astype(jnp.bfloat16)
        moved = ds[at, :].astype(jnp.bfloat16)
        log_rate = jnp.dot(
            jnp.concatenate([latent, shift_t[at, :]], axis=1),
            coupling_t[...],
            preferred_element_type=jnp.float32,
        )
        along = jnp.dot(moved, coupling_t[0:K, :], preferred_element_type=jnp.float32)
        weighted = (jnp.exp(log_rate) * along).astype(jnp.bfloat16)
        pulled[at, :] = jnp.dot(weighted, coupling[...], preferred_element_type=jnp.float32)
    for j in range(CHUNKS):
        parts[(j % 4) * 2 + j // 4] = pulled[pl.ds(j * STEPS, STEPS), :]
    r = jnp.zeros((CHUNKS, K), jnp.float32)
    for i in reversed(range(STEPS)):
        r = decay_at(keep, carry, i) * (rows(pulled, i) + r)
    total = r[CHUNKS - 1 : CHUNKS]
    for j in reversed(range(CHUNKS - 1)):
        total = chunk[0, j : j + 1, :] * total + r[j : j + 1]
    sent[...] = jnp.broadcast_to(total[None], sent.shape)


def sum_kernel(here, got, late, parts, out):
    total = parts[0]
    for j in range(1, NVIEW):
        total = total + parts[j]
    entry = jnp.zeros((1, K), jnp.float32)
    for e in reversed(range(1, PEERS)):
        entry = jnp.where(e > here[0], got[e, 0:1, :] * entry + late[e], entry)
    tail = jnp.concatenate([entry, jnp.zeros((PART - STEPS - 1, K), jnp.float32)], axis=0)
    for j in range(4):
        out[j, 0:STEPS, :] = total
        out[j, STEPS:PART, :] = tail


def finish_kernel(here, begin, span, carry_ref, d, chunk, parts, out, adjoint):
    keep, gain, carry = factors(here, begin, span, carry_ref)
    r = jnp.zeros((CHUNKS, K), jnp.float32)
    for i in reversed(range(STEPS)):
        r = decay_at(keep, carry, i) * (rows(parts, i, PART) + r)
    entry = parts[STEPS : STEPS + 1, :]
    for j in range(1, CHUNKS):
        entry = entry + parts[j * PART + STEPS : j * PART + STEPS + 1, :]
    entries = [entry]
    for j in reversed(range(1, CHUNKS)):
        entries.append(chunk[0, j : j + 1, :] * entries[-1] + r[j : j + 1])
    r = jnp.concatenate(entries[::-1], axis=0)
    for i in reversed(range(STEPS)):
        a = rows(parts, i, PART) + r
        adjoint[pl.ds(i, CHUNKS, stride=STEPS), :] = a
        r = decay_at(keep, carry, i) * a
    out[...] = gain * adjoint[...] + d[...].astype(jnp.float32)


def local(x, d, coupling, assay, shift, span, carry, begin):
    f32, bf16 = jnp.float32, jnp.bfloat16
    here = lax.axis_index(BINS)[None]
    span = span.reshape(1, K)
    carry = carry.reshape(CHUNKS, STEPS)
    assay = assay.reshape(1, TRACKS)
    wide = VMEM((ROWS, K), f32)
    head = (here, begin, span, carry)
    heads = [SMEM, SMEM, VMEM, VMEM]
    chunk, sent = call(
        ends_kernel, heads + [VMEM] * 2, [((3, CHUNKS, K), f32), ((PEERS, 3, K), f32)], [wide] * 2
    )(*head, x, d)
    got = lax.all_to_all(sent, BINS, 0, 0, tiled=True)
    shift_t, coupling_t = call(
        prepare_kernel, [VMEM] * 3, [((ROWS, K), bf16), ((2 * K, TRACKS), bf16)]
    )(shift, assay, coupling)
    parts, sent = call(
        tracks_kernel,
        heads + [VMEM] * 7,
        [((NVIEW, STEPS, K), f32), ((PEERS, 1, K), f32)],
        [wide] * 3,
    )(*head, x, d, chunk, got, shift_t, coupling_t, coupling)
    late = lax.all_to_all(sent, BINS, 0, 0, tiled=True)
    parts = lax.all_to_all(parts, VIEW, 0, 0, tiled=True)
    (mine,) = call(sum_kernel, [SMEM] + [VMEM] * 3, [((4, PART, K), f32)])(here, got, late, parts)
    column = lax.all_to_all(mine, "zl", 0, 0, tiled=True)
    parts = lax.all_gather(column, "core").reshape(CHUNKS * PART, K)
    (out,) = call(finish_kernel, heads + [VMEM] * 3, [((ROWS, K), f32)], [wide])(
        *head, d, chunk, parts
    )
    return out


def solution(mesh):
    fine = Mesh(mesh.devices.reshape(8, 2, 4, 4, 2), ("y", "zh", "x", "zl", "core"))
    in_specs = (
        P(BINS, None),
        P(BINS, None),
        P(VIEW, None),
        P(VIEW),
        P(None, BINS),
        P(),
        P(BINS),
        P(),
    )
    return jax.shard_map(
        local, mesh=fine, in_specs=in_specs, out_specs=P(BINS, None), check_vma=False
    )
```

time: 1220 us -> 98.3 us (0.08)
  the two profiles are of different devices: /device:TPU:2 before, /device:TPU:1 now
where the time goes in v1:
time: 98.3 us; the launch traced here: 97.9 us
  blocking collectives  53.8 us (55%)
  starting transfers between devices  19.7 us (20%)
  waiting for transfers between devices  13.5 us (14%)
  Pallas kernels  8.28 us (8%)
  local copies, waits for them, and re-layouts  2.61 us (3%)
    all_to_all x1, blocking collectives, local(): parts = lax.all_to_all(parts, VIEW, 0, 0, tiled=True)  21.9 us
    all_to_all x1, starting transfers between devices, local(): got = lax.all_to_all(sent, BINS, 0, 0, tiled=True)  19.7 us
    all_to_all x1, blocking collectives, local(): late = lax.all_to_all(sent, BINS, 0, 0, tiled=True)  17.2 us
    all_to_all x1, waiting for transfers between devices, local(): got = lax.all_to_all(sent, BINS, 0, 0, tiled=True)  13.5 us
    all_to_all x1, blocking collectives, local(): column = lax.all_to_all(mine, 'zl', 0, 0, tiled=True)  10.4 us
    all_gather x1, blocking collectives, local(): parts = lax.all_gather(column, 'core').reshape(CHUNKS * PART, K)  4.22 us
    pallas_call x1, Pallas kernels, local(): call(tracks_kernel, heads + [VMEM] * 7, [((NVIEW, STEPS, K), f32), ((PEER...  3.82 us
    unnamed x20, local copies, waits for them, and re-layouts  2.61 us
  transfers between devices with their start and end apart: 1, of which 1 were waited for; matrix products, arithmetic and copies ran while one was open for 0% of the time, Pallas kernels for 0%

profile of v1, /device:TPU:1, one launch (start us, length us, event | category | flops | bytes accessed | tf_op | source)
XLA Modules:
  0.0 97.9 jit_solution(1844415065883706459)
XLA Ops:
  0.0 0.0 copy-start.5
  0.0 0.0 copy-start.7
  0.0 0.0 copy-start.8
  0.0 0.7 copy-done.5
  0.7 0.0 copy-done.7
  0.7 0.0 copy-done.8
  0.7 0.0 copy-start
  0.7 0.9 copy-done
  1.6 0.0 copy-start.2
  1.6 0.9 copy-done.2
  2.6 0.0 copy-start.9
  2.6 0.0 copy-start.4
  2.6 0.0 copy-start.6
  2.6 0.0 copy-start.3
  2.6 1.9 %shard_map.82 = (f32[3,8,128]{2,1,0:T(8,128)S(1)}, f32[64,3,128]{2,1,0:T(4,128)}) custom-call(s32[1]{0:T(128)} %bitcast.here, s32[3]{0:T(128)S(1)} %copy-done.7, f32[1,128]{1,0:T(1,128)S(1)} %bitcast.8, f32[8,128]{1,0:T(8,128)S(1)} %bitcast.5, bf16[1024,128]{1,0:T(8,128)(2,1)S(1)} %copy-done.2, bf16[1024,128]{1,0:T(8,128)(2,1)S(1)} %copy-done), custom_call_target="tpu_custom_call" | custom-call | tf_op jit(solution)/shard_map/pallas_call | solution.py:178
  4.5 0.0 copy-start.1
  4.5 19.7 %all-to-all-start = ((f32[64,3,128]{2,1,0:T(4,128)}), f32[64,3,128]{2,1,0:T(4,128)S(1)}, u32[]{:S(2)}, u32[]{:S(2)}) async-start(f32[64,3,128]{2,1,0:T(4,128)} %get-tuple-element.12), calls=%async_computation | async-start | bytes 262144 | tf_op jit(solution)/shard_map/all_to_all | solution.py:181
  24.2 0.0 copy-done.9
  24.3 0.0 copy-done.4
  24.3 0.0 copy-done.6
  24.3 0.2 shard_map.83
  24.5 13.5 %all-to-all-done.got = f32[64,3,128]{2,1,0:T(4,128)S(1)} async-done(((f32[64,3,128]{2,1,0:T(4,128)}), f32[64,3,128]{2,1,0:T(4,128)S(1)}, u32[]{:S(2)}, u32[]{:S(2)}) %all-to-all-start) | async-done | bytes 98336 | tf_op jit(solution)/shard_map/all_to_all | solution.py:181
  38.0 0.0 copy-done.3
  38.0 0.0 copy-done.1
  38.0 3.8 %shard_map.84 = (f32[8,128,128]{2,1,0:T(8,128)S(1)}, f32[64,1,128]{2,1,0:T(1,128)S(1)}) custom-call(s32[1]{0:T(128)} %bitcast.here, s32[3]{0:T(128)S(1)} %copy-done.7, f32[1,128]{1,0:T(1,128)S(1)} %bitcast.9, f32[8,128]{1,0:T(8,128)S(1)} %bitcast.6, bf16[1024,128]{1,0:T(8,128)(2,1)S(1)} %copy-done.3, bf16[1024,128]{1,0:T(8,128)(2,1)S(1)} %copy-done.1, ...), custom_call_target="tpu_custom_call" | custom-call | tf_op jit(solution)/shard_map/pallas_call | solution.py:185
  41.8 17.2 %all_to_all.20.late = f32[64,1,128]{2,1,0:T(1,128)S(1)} all-to-all(f32[64,1,128]{2,1,0:T(1,128)S(1)} %get-tuple-element.15), channel_id=1, replica_groups=mesh['y'=8,'zh'=2,'x'=4,'zl'=4,'core'=2] {'y','zh','x'}, dimensions={0} | all-to-all | bytes 65536 | tf_op jit(solution)/shard_map/all_to_all | solution.py:191
  59.0 21.9 %all_to_all.21.parts = f32[8,128,128]{2,1,0:T(8,128)S(1)} all-to-all(f32[8,128,128]{2,1,0:T(8,128)S(1)} %get-tuple-element.16), channel_id=1, replica_groups=mesh['y'=8,'zh'=2,'x'=4,'zl'=4,'core'=2] {'zl','core'}, dimensions={0} | all-to-all | bytes 1048576 | tf_op jit(solution)/shard_map/all_to_all | solution.py:192
  81.0 0.2 shard_map.85
  81.2 10.4 %all_to_all.22 = f32[4,136,128]{2,1,0:T(8,128)S(1)} all-to-all(f32[4,136,128]{2,1,0:T(8,128)S(1)} %shard_map.85), channel_id=1, replica_groups=mesh['y'=8,'zh'=2,'x'=4,'zl'=4,'core'=2] {'zl'}, dimensions={0} | all-to-all | bytes 557056 | tf_op jit(solution)/shard_map/all_to_all | solution.py:194
  91.6 4.2 %all-gather = f32[8,136,128]{2,1,0:T(8,128)S(1)} all-gather(f32[4,136,128]{2,1,0:T(8,128)S(1)} %all_to_all.22), channel_id=2, replica_groups=mesh['y'=8,'zh'=2,'x'=4,'zl'=4,'core'=2] {'core'}, dimensions={0}, use_global_device_ids=true | all-gather | bytes 835584 | tf_op jit(solution)/shard_map/all_gather | solution.py:195
  95.8 2.1 %shard_map.86 = f32[1024,128]{1,0:T(8,128)} custom-call(s32[1]{0:T(128)} %bitcast.here, s32[3]{0:T(128)S(1)} %copy-done.7, f32[1,128]{1,0:T(1,128)S(1)} %bitcast.10, f32[8,128]{1,0:T(8,128)S(1)} %bitcast.7, bf16[1024,128]{1,0:T(8,128)(2,1)S(1)} %copy-done.1, f32[3,8,128]{2,1,0:T(8,128)S(1)} %get-tuple-element.11.chunk, f32[1088,128]{1,0:T(8,128)S(1)} %bitcast.4), custom_call_target="tpu_custom_call" | custom-call | tf_op jit(solution)/shard_map/pallas_call | solution.py:196
  (1 shorter events, 0.0 us)
Async XLA Ops:
  0.0 0.7 copy-start.5
  0.0 0.7 copy-start.7
  0.0 0.7 copy-start.8
  0.7 1.0 copy-start
  1.6 0.9 copy-start.2
  2.6 21.6 %copy-start.9 = (s32[640]{0:T(1024)S(1)}, s32[640]{0:T(1024)}, u32[]{:S(2)}) copy-start(s32[640]{0:T(1024)} %param.11) | copy-start | bytes 7684
  2.6 21.7 %copy-start.4 = (bf16[640,128]{1,0:T(8,128)(2,1)S(1)}, bf16[640,128]{1,0:T(8,128)(2,1)}, u32[]{:S(2)}) copy-start(bf16[640,128]{1,0:T(8,128)(2,1)} %coupling.3) | copy-start | bytes 491524
  2.6 21.7 %copy-start.6 = (f32[8,1024]{1,0:T(8,128)S(1)}, f32[8,1024]{1,0:T(8,128)}, u32[]{:S(2)}) copy-start(f32[8,1024]{1,0:T(8,128)} %shift.1) | copy-start | bytes 98308
  2.6 35.4 %copy-start.3 = (bf16[1024,128]{1,0:T(8,128)(2,1)S(1)}, bf16[1024,128]{1,0:T(8,128)(2,1)}, u32[]{:S(2)}) copy-start(bf16[1024,128]{1,0:T(8,128)(2,1)} %x.3) | copy-start | bytes 786436
  4.5 33.5 %copy-start.1 = (bf16[1024,128]{1,0:T(8,128)(2,1)S(1)}, bf16[1024,128]{1,0:T(8,128)(2,1)}, u32[]{:S(2)}) copy-start(bf16[1024,128]{1,0:T(8,128)(2,1)} %d.5) | copy-start | bytes 786436
  4.5 33.5 %all-to-all-start = ((f32[64,3,128]{2,1,0:T(4,128)}), f32[64,3,128]{2,1,0:T(4,128)S(1)}, u32[]{:S(2)}, u32[]{:S(2)}) async-start(f32[64,3,128]{2,1,0:T(4,128)} %get-tuple-element.12), calls=%async_computation | async-start | bytes 262144 | tf_op jit(solution)/shard_map/all_to_all | solution.py:181

commit v2 on v1

v2 whole, which is shorter than its diff:
```python
import jax
import jax.numpy as jnp
from jax import lax
from jax.experimental import pallas as pl
from jax.experimental.pallas import tpu as pltpu
from jax.sharding import Mesh, PartitionSpec as P

ROWS, HALF, K, CHUNKS, STEPS = 1024, 512, 128, 8, 128
PEERS, NVIEW, TRACKS = 64, 8, 640
BLOCK = 256
FINE = 64
TINY = 16
PART = STEPS + 8
BINS, VIEW = ("y", "zh", "x"), ("zl", "core")
VMEM, SMEM, HBM = pltpu.VMEM, pltpu.SMEM, pltpu.HBM
F32, BF16 = jnp.float32, jnp.bfloat16


def spec(space):
    return pl.BlockSpec(memory_space=space)


def call(body, ins, outs, scratch=()):
    return pl.pallas_call(
        body,
        in_specs=[spec(s) for s in ins],
        out_specs=[spec(VMEM) for _ in outs],
        out_shape=[jax.ShapeDtypeStruct(shape, dtype) for shape, dtype in outs],
        scratch_shapes=list(scratch),
        compiler_params=pltpu.CompilerParams(vmem_limit_bytes=48 * 1024 * 1024),
    )


def gains(span):
    forget = 1.0 / span
    return 1.0 - forget, jnp.sqrt(forget * (2.0 - forget))


def masked(carry, first, begin_ref):
    n = carry.shape[1]
    at = (
        first
        + lax.broadcasted_iota(jnp.int32, carry.shape, 0) * n
        + lax.broadcasted_iota(jnp.int32, carry.shape, 1)
    )
    begins = (at == begin_ref[0]) | (at == begin_ref[1]) | (at == begin_ref[2])
    return jnp.where(begins, 0.0, carry)


def column(carry, i):
    return jnp.broadcast_to(carry[:, i : i + 1], (CHUNKS, K))


def rows(ref, i, stride):
    return ref[pl.ds(i, CHUNKS, stride=stride), :]


def ends_kernel(
    here, begin_hbm, span_hbm, carry_hbm, x_hbm, d_hbm, chunk, sent,
    begin, span, carry_ref, x, d, xs, ds, sems,
):
    pairs = [(x_hbm, x), (d_hbm, d), (carry_hbm, carry_ref), (span_hbm, span), (begin_hbm, begin)]
    copies = [pltpu.make_async_copy(a, b, sems.at[i]) for i, (a, b) in enumerate(pairs)]
    for copy in copies:
        copy.start()
    for copy in copies[::-1]:
        copy.wait()
    keep, gain = gains(span[...])
    carry = masked(carry_ref[...], here[0] * ROWS, begin)
    xs[...] = gain * x[...].astype(F32)
    ds[...] = gain * d[...].astype(F32)
    half = STEPS // 2
    ends = []
    for first in (0, half):
        z, v = rows(xs, first, STEPS), rows(ds, first, STEPS)
        m = column(carry, first) * keep
        for i in range(first + 1, first + half):
            decay = column(carry, i) * keep
            z = decay * z + rows(xs, i, STEPS)
            v = decay * v + rows(ds, i, STEPS)
            m = decay * m
        ends.append((m, z, v))
    (m0, z0, v0), (m1, z1, v1) = ends
    m, z, v = m0 * m1, m1 * z0 + z1, m1 * v0 + v1
    chunk[0] = m
    chunk[1] = z
    chunk[2] = v
    mt, zt, vt = m[0:1], z[0:1], v[0:1]
    for j in range(1, CHUNKS):
        mj = m[j : j + 1]
        mt, zt, vt = mj * mt, mj * zt + z[j : j + 1], mj * vt + v[j : j + 1]
    sent[...] = jnp.broadcast_to(jnp.concatenate([mt, zt, vt], axis=0)[None], sent.shape)


def widen_kernel(chunk, coupling, assay, out):
    del chunk
    out[0:TRACKS, :] = coupling[...].astype(F32)
    lanes = [assay[:, i * K : (i + 1) * K] for i in range(TRACKS // K)]
    rest = jnp.zeros((8 - len(lanes), K), jnp.int32)
    out[TRACKS : TRACKS + 8, :] = jnp.concatenate(lanes + [rest], axis=0).astype(F32)


def prepare_kernel(
    here, begin, span, carry_wide, carry_fine, x, d, chunk, shift,
    latent, moved, product, shift_t, suffix, own_decay, xs, ds, decays,
):
    core, owned = here[2], here[2] * 4 + here[1]
    keep, gain = gains(span[...])
    start = pl.multiple_of(core * HALF, HALF)
    carry = masked(
        carry_fine[pl.ds(pl.multiple_of(core * CHUNKS, CHUNKS), CHUNKS), :],
        here[0] * ROWS + core * HALF,
        begin,
    )
    xs[...] = gain * x[pl.ds(start, HALF), :].astype(F32)
    ds[...] = gain * d[pl.ds(start, HALF), :].astype(F32)
    z, v = rows(xs, 0, FINE), rows(ds, 0, FINE)
    m = column(carry, 0) * keep
    for i in range(1, FINE):
        decay = column(carry, i) * keep
        z = decay * z + rows(xs, i, FINE)
        v = decay * v + rows(ds, i, FINE)
        m = decay * m
    q, ez, ev = jnp.ones((1, K), F32), jnp.zeros((1, K), F32), jnp.zeros((1, K), F32)
    for j in range(CHUNKS // 2):
        mj = chunk[0, j : j + 1, :]
        q, ez, ev = mj * q, mj * ez + chunk[1, j : j + 1, :], mj * ev + chunk[2, j : j + 1, :]
    second = core == 1
    qs, zs, vs = [jnp.where(second, q, 1.0)], [jnp.where(second, ez, 0.0)], [jnp.where(second, ev, 0.0)]
    for j in range(CHUNKS - 1):
        mj = m[j : j + 1]
        qs.append(mj * qs[-1])
        zs.append(mj * zs[-1] + z[j : j + 1])
        vs.append(mj * vs[-1] + v[j : j + 1])
    q, z, v = (jnp.concatenate(a, axis=0) for a in (qs, zs, vs))
    for i in range(FINE):
        decay = column(carry, i) * keep
        q = decay * q
        z = decay * z + rows(xs, i, FINE)
        v = decay * v + rows(ds, i, FINE)
        at = pl.ds(i, CHUNKS, stride=FINE)
        product[at, :] = q
        latent[at, :] = z
        moved[at, :] = v
    carry = masked(carry_wide[...], here[0] * ROWS, begin)
    f = jnp.ones((CHUNKS, K), F32)
    for i in reversed(range(STEPS)):
        decay = column(carry, i) * keep
        at = pl.ds(i, CHUNKS, stride=STEPS)
        suffix[at, :] = f
        decays[at, :] = decay
        f = decay * f
    own_decay[...] = decays[pl.ds(pl.multiple_of(owned * STEPS, STEPS), STEPS), :]
    s = shift[:, pl.ds(start, HALF)]
    hi = s.astype(BF16).astype(F32)
    mid = (s - hi).astype(BF16).astype(F32)
    low = s - hi - mid
    blank = jnp.zeros((K - 3 * NVIEW, HALF), F32)
    shift_t[...] = jnp.concatenate([hi, mid, low, blank], axis=0).T.astype(BF16)


def couple_kernel(mine, other, coupling_t, coupling):
    for side, ref in enumerate((mine, other)):
        at = pl.ds(side * TRACKS, TRACKS)
        w = ref[0:TRACKS, :]
        coupling[at, :] = w.astype(BF16)
        coupling_t[0:K, at] = w.T.astype(BF16)
        assay = ref[TRACKS : TRACKS + 8, :]
        assay = jnp.concatenate([assay[i : i + 1] for i in range(TRACKS // K)], axis=1)
        view = lax.broadcasted_iota(jnp.int32, (NVIEW, TRACKS), 0).astype(F32)
        member = (assay == view).astype(F32)
        blank = jnp.zeros((K - 3 * NVIEW, TRACKS), F32)
        coupling_t[K : 2 * K, at] = jnp.concatenate([member] * 3 + [blank], axis=0).astype(BF16)


def tracks_kernel(
    here, got, latent_ref, moved_ref, product_ref, shift_t, coupling_t, coupling,
    keep, send1, send2, send3, sent, pulled,
):
    ez = jnp.zeros((1, K), F32)
    ev = jnp.zeros((1, K), F32)
    for e in range(PEERS - 1):
        m, z, v = got[e, 0:1, :], got[e, 1:2, :], got[e, 2:3, :]
        earlier = e < here[0]
        ez = jnp.where(earlier, m * ez + z, ez)
        ev = jnp.where(earlier, m * ev + v, ev)
    total = jnp.zeros((1, K), F32)
    for b in range(HALF // BLOCK):
        at = pl.ds(b * BLOCK, BLOCK)
        product = product_ref[at, :]
        latent = (latent_ref[at, :] + product * ez).astype(BF16)
        moved = (moved_ref[at, :] + product * ev).astype(BF16)
        log_rate = jnp.dot(
            jnp.concatenate([latent, shift_t[at, :]], axis=1),
            coupling_t[...],
            preferred_element_type=F32,
        )
        along = jnp.dot(moved, coupling_t[0:K, :], preferred_element_type=F32)
        weighted = (jnp.exp(log_rate) * along).astype(BF16)
        p = jnp.dot(weighted, coupling[...], preferred_element_type=F32)
        pulled[at, :] = p
        total = total + jnp.sum(product * p, axis=0, keepdims=True)
    sent[...] = jnp.broadcast_to(total[None], sent.shape)
    for k, out in enumerate((keep, send1, send2, send3)):
        part = lax.rem(here[1] + k, 4)
        out[...] = pulled[pl.ds(pl.multiple_of(part * STEPS, STEPS), STEPS), :]


def weights_kernel(here, got, weights):
    w = jnp.ones((1, K), F32)
    for e in range(PEERS):
        later = e > here[0]
        weights[e] = jnp.where(later, w, 0.0)
        w = jnp.where(later, w * got[e, 0:1, :], w)


def sum_kernel(weights, late, own_decay, keep, got1, got2, got3, out, p, a):
    p[...] = (keep[...] + got1[...]) + (got2[...] + got3[...])
    r = jnp.zeros((CHUNKS, K), F32)
    m = jnp.ones((CHUNKS, K), F32)
    for i in reversed(range(TINY)):
        decay = rows(own_decay, i, TINY)
        r = decay * (rows(p, i, TINY) + r)
        m = decay * m
    entries = [jnp.zeros((1, K), F32)]
    for j in reversed(range(CHUNKS)):
        entries.append(m[j : j + 1] * entries[-1] + r[j : j + 1])
    total = entries.pop()
    r = jnp.concatenate(entries[::-1], axis=0)
    for i in reversed(range(TINY)):
        adjoint = rows(p, i, TINY) + r
        a[pl.ds(i, CHUNKS, stride=TINY), :] = adjoint
        r = rows(own_decay, i, TINY) * adjoint
    entry = jnp.sum(weights[...] * late[...], axis=0)
    tail = jnp.concatenate([total, entry, jnp.zeros((PART - STEPS - 2, K), F32)], axis=0)
    for j in range(4):
        out[j, 0:STEPS, :] = a[...]
        out[j, STEPS:PART, :] = tail


def finish_kernel(span, d, chunk, suffix, parts, out):
    _, gain = gains(span[...])
    entry = parts[0, STEPS + 1 : STEPS + 2, :]
    for j in range(1, CHUNKS):
        entry = entry + parts[j, STEPS + 1 : STEPS + 2, :]
    for j in reversed(range(CHUNKS)):
        at = pl.ds(j * STEPS, STEPS)
        adjoint = parts[j, 0:STEPS, :] + suffix[at, :] * entry
        out[at, :] = gain * adjoint + d[at, :].astype(F32)
        entry = chunk[0, j : j + 1, :] * entry + parts[j, STEPS : STEPS + 1, :]


def local(x, d, coupling, assay, shift, span, carry, begin):
    here = jnp.stack([lax.axis_index(BINS), lax.axis_index("zl"), lax.axis_index("core")])
    span = span.reshape(1, K)
    carry_wide = carry.reshape(CHUNKS, STEPS)
    wide = ((ROWS, K), F32)
    half = ((HALF, K), F32)
    tile = ((STEPS, K), F32)
    chunk, sent = call(
        ends_kernel,
        [SMEM] + [HBM] * 5,
        [((3, CHUNKS, K), F32), ((PEERS, 3, K), F32)],
        [
            SMEM((3,), jnp.int32),
            VMEM((1, K), F32),
            VMEM((CHUNKS, STEPS), F32),
            VMEM((ROWS, K), BF16),
            VMEM((ROWS, K), BF16),
            VMEM(*wide),
            VMEM(*wide),
            pltpu.SemaphoreType.DMA((5,)),
        ],
    )(here, begin, span, carry_wide, x, d)
    got = lax.all_to_all(sent, BINS, 0, 0, tiled=True)

    (mine,) = call(widen_kernel, [VMEM] * 3, [((TRACKS + 8, K), F32)])(
        chunk, coupling, assay.reshape(1, TRACKS)
    )
    other = lax.ppermute(mine, "core", [(0, 1), (1, 0)])
    latent, moved, product, shift_t, suffix, own_decay = call(
        prepare_kernel,
        [SMEM] * 2 + [VMEM] * 7,
        [half, half, half, ((HALF, K), BF16), wide, tile],
        [VMEM(*half), VMEM(*half), VMEM(*wide)],
    )(here, begin, span, carry_wide, carry.reshape(2 * CHUNKS, FINE), x, d, chunk, shift)
    coupling_t, both = call(
        couple_kernel, [VMEM] * 2, [((2 * K, 2 * TRACKS), BF16), ((2 * TRACKS, K), BF16)]
    )(mine, other)

    keep, send1, send2, send3, sent = call(
        tracks_kernel,
        [SMEM] + [VMEM] * 7,
        [tile] * 4 + [((PEERS, 1, K), F32)],
        [VMEM(*half)],
    )(here, got, latent, moved, product, shift_t, coupling_t, both)
    late = lax.all_to_all(sent, BINS, 0, 0, tiled=True)
    received = [
        lax.ppermute(s, "zl", [(i, (i + k) % 4) for i in range(4)])
        for k, s in ((1, send1), (2, send2), (3, send3))
    ]
    (weights,) = call(weights_kernel, [SMEM, VMEM], [((PEERS, 1, K), F32)])(here, got)
    (mine,) = call(
        sum_kernel, [VMEM] * 7, [((4, PART, K), F32)], [VMEM(*tile)] * 2
    )(weights, late, own_decay, keep, *received)
    quarter = lax.all_to_all(mine, "zl", 0, 0, tiled=True)
    parts = lax.all_gather(quarter, "core").reshape(CHUNKS, PART, K)
    (out,) = call(finish_kernel, [VMEM] * 5, [wide])(span, d, chunk, suffix, parts)
    return out


def solution(mesh):
    fine = Mesh(mesh.devices.reshape(8, 2, 4, 4, 2), ("y", "zh", "x", "zl", "core"))
    in_specs = (
        P(BINS, None),
        P(BINS, None),
        P(VIEW, None),
        P(VIEW),
        P(None, BINS),
        P(),
        P(BINS),
        P(),
    )
    return jax.shard_map(
        local, mesh=fine, in_specs=in_specs, out_specs=P(BINS, None), check_vma=False
    )
```

time: 98.3 us -> 90 us (0.916)
  blocking collectives: 53.8 us -> 15 us
  starting transfers between devices: 19.7 us -> 37.9 us
  waiting for transfers between devices: 13.5 us -> 22.7 us
  local copies, waits for them, and re-layouts: 2.61 us -> 3.97 us
  Pallas kernels: 8.28 us -> 9.62 us
    all_to_all x3 -> x1, blocking collectives: 49.6 us -> 9.03 us  [local(): quarter = lax.all_to_all(mine, 'zl', 0, 0, tiled=True)]
    ppermute x0 -> x4, starting transfers between devices: none -> 19.1 us  [the longest x3 10.2 us: local(): lax.ppermute(s, 'zl', [(i, (i + k) % 4) for i in range(4)])]
    all_to_all x0 -> x1, waiting for transfers between devices: none -> 12.5 us  [local(): late = lax.all_to_all(sent, BINS, 0, 0, tiled=True)]
    all_to_all x1, starting transfers between devices: 19.7 us -> 13.4 us  [local(): got = lax.all_to_all(sent, BINS, 0, 0, tiled=True)]
    all_to_all x0 -> x1, starting transfers between devices: none -> 5.47 us  [local(): late = lax.all_to_all(sent, BINS, 0, 0, tiled=True)]
    all_to_all x1, waiting for transfers between devices: 13.5 us -> 10.3 us  [local(): got = lax.all_to_all(sent, BINS, 0, 0, tiled=True)]
    all_gather x1, blocking collectives: 4.22 us -> 5.98 us  [local(): parts = lax.all_gather(quarter, 'core').reshape(CHUNKS, PART, K)]
    pallas_call x5 -> x8, Pallas kernels: 8.28 us -> 9.62 us  [the longest x1 2.63 us: local(): call(tracks_kernel, [SMEM] + [VMEM] * 7, [tile] * 4 + [((PEERS, 1, K), F3...]
  transfers between devices with their start and end apart: 1 -> 6, of which waited for: 1 -> 2; matrix products, arithmetic and copies ran while one was open for 0% -> 0% of each run, Pallas kernels for 0% -> 4%
where the time goes in v2:
time: 90 us; the launch traced here: 89.5 us
  starting transfers between devices  37.9 us (42%)
  waiting for transfers between devices  22.7 us (25%)
  blocking collectives  15 us (17%)
  Pallas kernels  9.62 us (11%)
  local copies, waits for them, and re-layouts  3.97 us (4%)
    all_to_all x1, starting transfers between devices, local(): got = lax.all_to_all(sent, BINS, 0, 0, tiled=True)  13.4 us
    all_to_all x1, waiting for transfers between devices, local(): late = lax.all_to_all(sent, BINS, 0, 0, tiled=True)  12.5 us
    all_to_all x1, waiting for transfers between devices, local(): got = lax.all_to_all(sent, BINS, 0, 0, tiled=True)  10.3 us
    ppermute x3, starting transfers between devices, local(): lax.ppermute(s, 'zl', [(i, (i + k) % 4) for i in range(4)])  10.2 us
    all_to_all x1, blocking collectives, local(): quarter = lax.all_to_all(mine, 'zl', 0, 0, tiled=True)  9.03 us
    ppermute x1, starting transfers between devices, local(): other = lax.ppermute(mine, 'core', [(0, 1), (1, 0)])  8.92 us
    all_gather x1, blocking collectives, local(): parts = lax.all_gather(quarter, 'core').reshape(CHUNKS, PART, K)  5.98 us
    all_to_all x1, starting transfers between devices, local(): late = lax.all_to_all(sent, BINS, 0, 0, tiled=True)  5.47 us
  transfers between devices with their start and end apart: 6, of which 2 were waited for; matrix products, arithmetic and copies ran while one was open for 0% of the time, Pallas kernels for 4%

profile of v2, /device:TPU:1, one launch (start us, length us, event | category | flops | bytes accessed | tf_op | source)
XLA Modules:
  0.0 89.5 jit_solution(10402413002464080747)
XLA Ops:
  0.0 0.0 copy-start.11
  0.0 0.7 copy-done.11
  0.7 0.0 copy-start.7
  0.7 0.1 pad_add_fusion.here
  0.8 0.0 copy-start.9
  0.8 0.0 copy-start.10
  0.8 0.6 copy-done.7
  1.4 0.0 copy-done.9
  1.4 0.0 copy-done.10
  1.4 0.0 copy-start
  1.4 0.9 %copy-done = bf16[1024,128]{1,0:T(8,128)(2,1)S(1)} copy-done((bf16[1024,128]{1,0:T(8,128)(2,1)S(1)}, bf16[1024,128]{1,0:T(8,128)(2,1)}, u32[]{:S(2)}) %copy-start) | copy-done | bytes 262168
  2.4 0.0 copy-start.2
  2.4 0.9 %copy-done.2 = bf16[1024,128]{1,0:T(8,128)(2,1)S(1)} copy-done((bf16[1024,128]{1,0:T(8,128)(2,1)S(1)}, bf16[1024,128]{1,0:T(8,128)(2,1)}, u32[]{:S(2)}) %copy-start.2) | copy-done | bytes 262168
  3.3 0.0 copy-start.4
  3.3 2.6 %shard_map.82 = (f32[3,8,128]{2,1,0:T(8,128)S(1)}, f32[64,3,128]{2,1,0:T(4,128)}) custom-call(s32[3]{0:T(128)S(1)} %pad_add_fusion.here, s32[3]{0:T(128)S(1)} %copy-done.10, f32[1,128]{1,0:T(1,128)S(1)} %bitcast.7, f32[8,128]{1,0:T(8,128)S(1)} %bitcast.5, bf16[1024,128]{1,0:T(8,128)(2,1)S(1)} %copy-done.2, bf16[1024,128]{1,0:T(8,128)(2,1)S(1)} %copy-done), custom_call_target="tpu_custom_call" | custom-call | tf_op jit(solution)/shard_map/pallas_call | solution.py:260
  5.9 0.0 copy-done.4
  5.9 0.0 copy-start.3
  5.9 0.0 copy-start.8
  6.0 0.0 copy-start.1
  6.0 8.9 %collective-permute-start = (f32[648,128]{1,0:T(8,128)S(1)}, f32[648,128]{1,0:T(8,128)S(1)}, u32[]{:S(2)}, u32[]{:S(2)}) collective-permute-start(f32[648,128]{1,0:T(8,128)S(1)} %shard_map.85.mine), channel_id=1, source_target_pairs={{0,1},{1,0},{2,3},{3,2},{4,5},{5,4},{6,7},{7,6},{8,9},{9,8},{10,11... | collective-permute-start | bytes 995336 | tf_op jit(solution)/shard_map/ppermute | solution.py:280
  14.9 13.4 %all-to-all-start = ((f32[64,3,128]{2,1,0:T(4,128)}), f32[64,3,128]{2,1,0:T(4,128)S(1)}, u32[]{:S(2)}, u32[]{:S(2)}) async-start(f32[64,3,128]{2,1,0:T(4,128)} %get-tuple-element.22), calls=%async_computation | async-start | bytes 262144 | tf_op jit(solution)/shard_map/all_to_all | solution.py:275
  28.3 0.1 reshape.17.carry_fine
  28.4 0.0 copy-done.3
  28.4 0.0 copy-done.8
  28.4 0.0 copy-done.1
  28.4 2.5 %shard_map.83 = (f32[512,128]{1,0:T(8,128)S(1)}, f32[512,128]{1,0:T(8,128)S(1)}, f32[512,128]{1,0:T(8,128)S(1)}, bf16[512,128]{1,0:T(8,128)(2,1)S(1)}, f32[1024,128]{1,0:T(8,128)S(1)}, /*index=5*/f32[128,128]{1,0:T(8,128)S(1)}) custom-call(s32[3]{0:T(128)S(1)} %pad_add_fusion.here, s32[3]{0:T(128)S(1)} %copy-done.10, f32[1,128]{1,0:T(1,128)S(1)} %bitcast.8, ...), custom_call_target="tpu_custom_call" | custom-call | tf_op jit(solution)/shard_map/pallas_call | solution.py:281
  30.9 0.0 copy-start.5
  30.9 0.6 copy-done.5
  31.5 0.0 collective-permute-done.other
  31.5 0.2 shard_map.86
  31.7 10.3 %all-to-all-done.got = f32[64,3,128]{2,1,0:T(4,128)S(1)} async-done(((f32[64,3,128]{2,1,0:T(4,128)}), f32[64,3,128]{2,1,0:T(4,128)S(1)}, u32[]{:S(2)}, u32[]{:S(2)}) %all-to-all-start) | async-done | bytes 98336 | tf_op jit(solution)/shard_map/all_to_all | solution.py:275
  42.0 2.6 %shard_map.87 = (f32[128,128]{1,0:T(8,128)S(1)}, f32[128,128]{1,0:T(8,128)S(1)}, f32[128,128]{1,0:T(8,128)S(1)}, f32[128,128]{1,0:T(8,128)S(1)}, f32[64,1,128]{2,1,0:T(1,128)}) custom-call(s32[3]{0:T(128)S(1)} %pad_add_fusion.here, f32[64,3,128]{2,1,0:T(4,128)S(1)} %all-to-all-done.got, f32[512,128]{1,0:T(8,128)S(1)} %get-tuple-element.23.latent_ref, ...), custom_call_target="tpu_custom_call" | custom-call | tf_op jit(solution)/shard_map/pallas_call | solution.py:291
  44.6 3.1 %collective-permute-start.1 = (f32[128,128]{1,0:T(8,128)S(1)}, f32[128,128]{1,0:T(8,128)S(1)}, u32[]{:S(2)}, u32[]{:S(2)}) collective-permute-start(f32[128,128]{1,0:T(8,128)S(1)} %get-tuple-element.32), channel_id=1, source_target_pairs={{0,2},{2,4},{4,6},{6,0},{1,3},{3,5},{5,7},{7,1},{8,10},{10,12},{12... | collective-permute-start | bytes 196616 | tf_op jit(solution)/shard_map/ppermute | solution.py:299
  47.7 4.0 %collective-permute-start.2 = (f32[128,128]{1,0:T(8,128)S(1)}, f32[128,128]{1,0:T(8,128)S(1)}, u32[]{:S(2)}, u32[]{:S(2)}) collective-permute-start(f32[128,128]{1,0:T(8,128)S(1)} %get-tuple-element.33), channel_id=1, source_target_pairs={{0,4},{2,6},{4,0},{6,2},{1,5},{3,7},{5,1},{7,3},{8,12},{10,14},{12... | collective-permute-start | bytes 196616 | tf_op jit(solution)/shard_map/ppermute | solution.py:299
  51.7 3.1 %collective-permute-start.3 = (f32[128,128]{1,0:T(8,128)S(1)}, f32[128,128]{1,0:T(8,128)S(1)}, u32[]{:S(2)}, u32[]{:S(2)}) collective-permute-start(f32[128,128]{1,0:T(8,128)S(1)} %get-tuple-element.34), channel_id=1, source_target_pairs={{0,6},{2,0},{4,2},{6,4},{1,7},{3,1},{5,3},{7,5},{8,14},{10,8},{12,... | collective-permute-start | bytes 196616 | tf_op jit(solution)/shard_map/ppermute | solution.py:299
  54.8 5.5 %all-to-all-start.1 = ((f32[64,1,128]{2,1,0:T(1,128)}), f32[64,1,128]{2,1,0:T(1,128)S(1)}, u32[]{:S(2)}, u32[]{:S(2)}) async-start(f32[64,1,128]{2,1,0:T(1,128)} %get-tuple-element.29), calls=%async_computation.1 | async-start | bytes 65536 | tf_op jit(solution)/shard_map/all_to_all | solution.py:297
  60.3 0.0 copy-start.6
  60.3 0.6 shard_map.84.weights
  61.0 12.5 %all-to-all-done.1.late = f32[64,1,128]{2,1,0:T(1,128)S(1)} async-done(((f32[64,1,128]{2,1,0:T(1,128)}), f32[64,1,128]{2,1,0:T(1,128)S(1)}, u32[]{:S(2)}, u32[]{:S(2)}) %all-to-all-start.1) | async-done | bytes 32800 | tf_op jit(solution)/shard_map/all_to_all | solution.py:297
  73.4 0.0 collective-permute-done.1.got1
  73.4 0.0 collective-permute-done.2.got2
  73.4 0.0 collective-permute-done.3.got3
  73.4 0.0 copy-done.6
  73.4 0.1 shard_map.88
  73.6 9.0 %all_to_all.15 = f32[4,136,128]{2,1,0:T(8,128)S(1)} all-to-all(f32[4,136,128]{2,1,0:T(8,128)S(1)} %shard_map.88), channel_id=1, replica_groups=mesh['y'=8,'zh'=2,'x'=4,'zl'=4,'core'=2] {'zl'}, dimensions={0} | all-to-all | bytes 557056 | tf_op jit(solution)/shard_map/all_to_all | solution.py:306
  82.6 6.0 %all-gather.parts = f32[8,136,128]{2,1,0:T(8,128)S(1)} all-gather(f32[4,136,128]{2,1,0:T(8,128)S(1)} %all_to_all.15), channel_id=2, replica_groups=mesh['y'=8,'zh'=2,'x'=4,'zl'=4,'core'=2] {'core'}, dimensions={0}, use_global_device_ids=true | all-gather | bytes 835584 | tf_op jit(solution)/shard_map/all_gather | solution.py:307
  88.6 0.9 %shard_map.89 = f32[1024,128]{1,0:T(8,128)} custom-call(f32[1,128]{1,0:T(1,128)S(1)} %bitcast.9, bf16[1024,128]{1,0:T(8,128)(2,1)S(1)} %copy-done.1, f32[3,8,128]{2,1,0:T(8,128)S(1)} %get-tuple-element.20.chunk, f32[1024,128]{1,0:T(8,128)S(1)} %get-tuple-element.21.suffix, f32[8,136,128]{2,1,0:T(8,128)S(1)} %all-gather.parts), custom_call_target="tpu_custom_call" | custom-call | tf_op jit(solution)/shard_map/pallas_call | solution.py:308
  (2 shorter events, 0.0 us)
Async XLA Ops:
  0.0 0.7 copy-start.11
  0.7 0.7 copy-start.7
  0.8 0.7 copy-start.9
  0.8 0.7 copy-start.10
  1.4 0.9 %copy-start = (bf16[1024,128]{1,0:T(8,128)(2,1)S(1)}, bf16[1024,128]{1,0:T(8,128)(2,1)}, u32[]{:S(2)}) copy-start(bf16[1024,128]{1,0:T(8,128)(2,1)} %d.3) | copy-start | bytes 786436
  2.4 0.9 %copy-start.2 = (bf16[1024,128]{1,0:T(8,128)(2,1)S(1)}, bf16[1024,128]{1,0:T(8,128)(2,1)}, u32[]{:S(2)}) copy-start(bf16[1024,128]{1,0:T(8,128)(2,1)} %x.1) | copy-start | bytes 786436
  3.3 2.6 %copy-start.4 = (bf16[640,128]{1,0:T(8,128)(2,1)S(1)}, bf16[640,128]{1,0:T(8,128)(2,1)}, u32[]{:S(2)}) copy-start(bf16[640,128]{1,0:T(8,128)(2,1)} %coupling.1) | copy-start | bytes 491524
  5.9 22.4 %copy-start.3 = (bf16[1024,128]{1,0:T(8,128)(2,1)S(1)}, bf16[1024,128]{1,0:T(8,128)(2,1)}, u32[]{:S(2)}) copy-start(bf16[1024,128]{1,0:T(8,128)(2,1)} %x.1) | copy-start | bytes 786436
  5.9 22.4 %copy-start.8 = (f32[8,1024]{1,0:T(8,128)S(1)}, f32[8,1024]{1,0:T(8,128)}, u32[]{:S(2)}) copy-start(f32[8,1024]{1,0:T(8,128)} %shift.1) | copy-start | bytes 98308
  6.0 22.4 %copy-start.1 = (bf16[1024,128]{1,0:T(8,128)(2,1)S(1)}, bf16[1024,128]{1,0:T(8,128)(2,1)}, u32[]{:S(2)}) copy-start(bf16[1024,128]{1,0:T(8,128)(2,1)} %d.3) | copy-start | bytes 786436
  6.0 25.5 %collective-permute-start = (f32[648,128]{1,0:T(8,128)S(1)}, f32[648,128]{1,0:T(8,128)S(1)}, u32[]{:S(2)}, u32[]{:S(2)}) collective-permute-start(f32[648,128]{1,0:T(8,128)S(1)} %shard_map.85.mine), channel_id=1, source_target_pairs={{0,1},{1,0},{2,3},{3,2},{4,5},{5,4},{6,7},{7,6},{8,9},{9,8},{10,11... | collective-permute-start | bytes 995336 | tf_op jit(solution)/shard_map/ppermute | solution.py:280
  14.9 27.0 %all-to-all-start = ((f32[64,3,128]{2,1,0:T(4,128)}), f32[64,3,128]{2,1,0:T(4,128)S(1)}, u32[]{:S(2)}, u32[]{:S(2)}) async-start(f32[64,3,128]{2,1,0:T(4,128)} %get-tuple-element.22), calls=%async_computation | async-start | bytes 262144 | tf_op jit(solution)/shard_map/all_to_all | solution.py:275
  30.9 0.6 copy-start.5
  44.6 28.8 %collective-permute-start.1 = (f32[128,128]{1,0:T(8,128)S(1)}, f32[128,128]{1,0:T(8,128)S(1)}, u32[]{:S(2)}, u32[]{:S(2)}) collective-permute-start(f32[128,128]{1,0:T(8,128)S(1)} %get-tuple-element.32), channel_id=1, source_target_pairs={{0,2},{2,4},{4,6},{6,0},{1,3},{3,5},{5,7},{7,1},{8,10},{10,12},{12... | collective-permute-start | bytes 196616 | tf_op jit(solution)/shard_map/ppermute | solution.py:299
  47.7 25.7 %collective-permute-start.2 = (f32[128,128]{1,0:T(8,128)S(1)}, f32[128,128]{1,0:T(8,128)S(1)}, u32[]{:S(2)}, u32[]{:S(2)}) collective-permute-start(f32[128,128]{1,0:T(8,128)S(1)} %get-tuple-element.33), channel_id=1, source_target_pairs={{0,4},{2,6},{4,0},{6,2},{1,5},{3,7},{5,1},{7,3},{8,12},{10,14},{12... | collective-permute-start | bytes 196616 | tf_op jit(solution)/shard_map/ppermute | solution.py:299
  51.7 21.7 %collective-permute-start.3 = (f32[128,128]{1,0:T(8,128)S(1)}, f32[128,128]{1,0:T(8,128)S(1)}, u32[]{:S(2)}, u32[]{:S(2)}) collective-permute-start(f32[128,128]{1,0:T(8,128)S(1)} %get-tuple-element.34), channel_id=1, source_target_pairs={{0,6},{2,0},{4,2},{6,4},{1,7},{3,1},{5,3},{7,5},{8,14},{10,8},{12,... | collective-permute-start | bytes 196616 | tf_op jit(solution)/shard_map/ppermute | solution.py:299
  54.8 18.6 %all-to-all-start.1 = ((f32[64,1,128]{2,1,0:T(1,128)}), f32[64,1,128]{2,1,0:T(1,128)S(1)}, u32[]{:S(2)}, u32[]{:S(2)}) async-start(f32[64,1,128]{2,1,0:T(1,128)} %get-tuple-element.29), calls=%async_computation.1 | async-start | bytes 65536 | tf_op jit(solution)/shard_map/all_to_all | solution.py:297
  60.3 13.1 %copy-start.6 = (f32[128,128]{1,0:T(8,128)S(1)}, f32[128,128]{1,0:T(8,128)}, u32[]{:S(2)}) copy-start(f32[128,128]{1,0:T(8,128)} %copy-done.5) | copy-start | bytes 196612

commit v3 on v2

v3 whole, which is shorter than its diff:
```python
import jax
import jax.numpy as jnp
from jax import lax
from jax.experimental import pallas as pl
from jax.experimental.pallas import tpu as pltpu
from jax.sharding import Mesh, PartitionSpec as P

ROWS, QUARTER, K, CHUNKS, STEPS = 1024, 256, 128, 8, 128
PEERS, NVIEW, TRACKS = 64, 8, 640
SHARD = TRACKS + 8
FINE = 32
TINY = 16
PART = STEPS + 8
BINS, VIEW = ("y", "zh", "x"), ("zl", "core")
VMEM, SMEM, HBM = pltpu.VMEM, pltpu.SMEM, pltpu.HBM
F32, BF16 = jnp.float32, jnp.bfloat16


def spec(space):
    return pl.BlockSpec(memory_space=space)


def call(body, ins, outs, scratch=(), vmem=16):
    return pl.pallas_call(
        body,
        in_specs=[spec(s) for s in ins],
        out_specs=[spec(VMEM) for _ in outs],
        out_shape=[jax.ShapeDtypeStruct(shape, dtype) for shape, dtype in outs],
        scratch_shapes=list(scratch),
        compiler_params=pltpu.CompilerParams(vmem_limit_bytes=vmem * 1024 * 1024),
    )


def gains(span):
    forget = 1.0 / span
    return 1.0 - forget, jnp.sqrt(forget * (2.0 - forget))


def masked(carry, first, begin_ref):
    m = carry.shape[1]
    at = (
        first
        + lax.broadcasted_iota(jnp.int32, carry.shape, 0) * m
        + lax.broadcasted_iota(jnp.int32, carry.shape, 1)
    )
    begins = (at == begin_ref[0]) | (at == begin_ref[1]) | (at == begin_ref[2])
    return jnp.where(begins, 0.0, carry)


def column(carry, i):
    return jnp.broadcast_to(carry[:, i : i + 1], (CHUNKS, K))


def rows(ref, i, stride):
    return ref[pl.ds(i, CHUNKS, stride=stride), :]


def ends_kernel(
    here, begin_hbm, span_hbm, carry_hbm, assay_hbm, coupling_hbm, x_hbm, d_hbm, chunk, sent, shard,
    begin, span, carry_ref, assay, coupling, x, d, xs, ds, sems,
):
    pairs = [
        (x_hbm, x),
        (d_hbm, d),
        (coupling_hbm, coupling),
        (assay_hbm, assay),
        (carry_hbm, carry_ref),
        (span_hbm, span),
        (begin_hbm, begin),
    ]
    copies = [pltpu.make_async_copy(a, b, sems.at[i]) for i, (a, b) in enumerate(pairs)]
    for copy in copies:
        copy.start()
    for copy in copies[::-1]:
        copy.wait()
    rest = jnp.zeros((SHARD - TRACKS - TRACKS // K, K), jnp.int32)
    shard[0:TRACKS, :] = coupling[...].astype(F32)
    shard[TRACKS:SHARD, :] = jnp.concatenate([assay[...], rest], axis=0).astype(F32)
    keep, gain = gains(span[...])
    carry = masked(carry_ref[...], here[0] * ROWS, begin)
    xs[...] = gain * x[...].astype(F32)
    ds[...] = gain * d[...].astype(F32)
    half = STEPS // 2
    ends = []
    for first in (0, half):
        z, v = rows(xs, first, STEPS), rows(ds, first, STEPS)
        m = column(carry, first) * keep
        for i in range(first + 1, first + half):
            decay = column(carry, i) * keep
            z = decay * z + rows(xs, i, STEPS)
            v = decay * v + rows(ds, i, STEPS)
            m = decay * m
        ends.append((m, z, v))
    (m0, z0, v0), (m1, z1, v1) = ends
    m, z, v = m0 * m1, m1 * z0 + z1, m1 * v0 + v1
    chunk[0] = m
    chunk[1] = z
    chunk[2] = v
    mt, zt, vt = m[0:1], z[0:1], v[0:1]
    for j in range(1, CHUNKS):
        mj = m[j : j + 1]
        mt, zt, vt = mj * mt, mj * zt + z[j : j + 1], mj * vt + v[j : j + 1]
    sent[...] = jnp.broadcast_to(jnp.concatenate([mt, zt, vt], axis=0)[None], sent.shape)


def prepare_kernel(
    here, zl, core, begin, span, carry_ref, x, d, chunk, shift,
    latent, moved, product, shift_t, xs, ds,
):
    at = core[0] * 4 + lax.rem(zl[0], 2) * 2
    start = pl.multiple_of(at * STEPS, QUARTER)
    keep, gain = gains(span[...])
    pair = masked(carry_ref[pl.ds(at, 2), :], here[0] * ROWS + start, begin)
    carry = jnp.concatenate(
        [pair[j : j + 1, i : i + FINE] for j in range(2) for i in range(0, STEPS, FINE)], axis=0
    )
    xs[...] = gain * x[pl.ds(start, QUARTER), :].astype(F32)
    ds[...] = gain * d[pl.ds(start, QUARTER), :].astype(F32)
    z, v = rows(xs, 0, FINE), rows(ds, 0, FINE)
    m = column(carry, 0) * keep
    for i in range(1, FINE):
        decay = column(carry, i) * keep
        z = decay * z + rows(xs, i, FINE)
        v = decay * v + rows(ds, i, FINE)
        m = decay * m
    q, ez, ev = jnp.ones((1, K), F32), jnp.zeros((1, K), F32), jnp.zeros((1, K), F32)
    for j in range(CHUNKS - 2):
        before = j < at
        mj, zj, vj = (chunk[i, j : j + 1, :] for i in range(3))
        q = jnp.where(before, mj * q, q)
        ez = jnp.where(before, mj * ez + zj, ez)
        ev = jnp.where(before, mj * ev + vj, ev)
    qs, zs, vs = [q], [ez], [ev]
    for j in range(CHUNKS - 1):
        mj = m[j : j + 1]
        qs.append(mj * qs[-1])
        zs.append(mj * zs[-1] + z[j : j + 1])
        vs.append(mj * vs[-1] + v[j : j + 1])
    q, z, v = (jnp.concatenate(a, axis=0) for a in (qs, zs, vs))
    for i in range(FINE):
        decay = column(carry, i) * keep
        q = decay * q
        z = decay * z + rows(xs, i, FINE)
        v = decay * v + rows(ds, i, FINE)
        to = pl.ds(i, CHUNKS, stride=FINE)
        product[to, :] = q
        latent[to, :] = z
        moved[to, :] = v
    s = shift[:, pl.ds(start, QUARTER)]
    hi = s.astype(BF16).astype(F32)
    mid = (s - hi).astype(BF16).astype(F32)
    low = s - hi - mid
    blank = jnp.zeros((K - 3 * NVIEW, QUARTER), F32)
    shift_t[...] = jnp.concatenate([hi, mid, low, blank], axis=0).T.astype(BF16)


def couple_kernel(mine, other, both):
    for side in range(4):
        ref = (mine, other)[side // 2].at[side % 2]
        at = pl.ds(side * TRACKS, TRACKS)
        w = ref[0:TRACKS, :]
        both[0:K, at] = w.T.astype(BF16)
        both[2 * K : 3 * K, at] = jnp.concatenate(
            [w[i : i + K] for i in range(0, TRACKS, K)], axis=1
        ).astype(BF16)
        assay = ref[TRACKS:SHARD, :]
        assay = jnp.concatenate([assay[i : i + 1] for i in range(TRACKS // K)], axis=1)
        view = lax.broadcasted_iota(jnp.int32, (NVIEW, TRACKS), 0).astype(F32)
        member = (assay == view).astype(F32)
        blank = jnp.zeros((K - 3 * NVIEW, TRACKS), F32)
        both[K : 2 * K, at] = jnp.concatenate([member] * 3 + [blank], axis=0).astype(BF16)


def tracks_kernel(
    here, zl, got, latent_ref, moved_ref, product_ref, shift_t, both,
    keep, send, sent, pulled,
):
    ez = jnp.zeros((1, K), F32)
    ev = jnp.zeros((1, K), F32)
    for e in range(PEERS - 1):
        m, z, v = got[e, 0:1, :], got[e, 1:2, :], got[e, 2:3, :]
        earlier = e < here[0]
        ez = jnp.where(earlier, m * ez + z, ez)
        ev = jnp.where(earlier, m * ev + v, ev)
    product = product_ref[...]
    latent = (latent_ref[...] + product * ez).astype(BF16)
    latent = jnp.concatenate([latent, shift_t[...]], axis=1)
    moved = (moved_ref[...] + product * ev).astype(BF16)
    p = jnp.zeros((QUARTER, K), F32)
    for side in range(4):
        at = pl.ds(side * TRACKS, TRACKS)
        log_rate = jnp.dot(latent, both[0 : 2 * K, at], preferred_element_type=F32)
        along = jnp.dot(moved, both[0:K, at], preferred_element_type=F32)
        weighted = (jnp.exp(log_rate) * along).astype(BF16)
        blocks = both[2 * K : 3 * K, at]
        coupling = jnp.concatenate([blocks[:, i : i + K] for i in range(0, TRACKS, K)], axis=0)
        p = p + jnp.dot(weighted, coupling, preferred_element_type=F32)
    pulled[...] = p
    total = jnp.sum(product * p, axis=0, keepdims=True)
    sent[...] = jnp.broadcast_to(total[None], sent.shape)
    own = lax.div(zl[0], 2)
    keep[...] = pulled[pl.ds(pl.multiple_of(own * STEPS, STEPS), STEPS), :]
    send[...] = pulled[pl.ds(pl.multiple_of((1 - own) * STEPS, STEPS), STEPS), :]


def later_kernel(here, zl, core, begin, span, carry_ref, got, weights, suffix, own_decay, decays):
    w = jnp.ones((1, K), F32)
    for e in range(PEERS):
        later = e > here[0]
        weights[e] = jnp.where(later, w, 0.0)
        w = jnp.where(later, w * got[e, 0:1, :], w)
    keep, _ = gains(span[...])
    carry = masked(carry_ref[...], here[0] * ROWS, begin)
    f = jnp.ones((CHUNKS, K), F32)
    for i in reversed(range(STEPS)):
        decay = column(carry, i) * keep
        to = pl.ds(i, CHUNKS, stride=STEPS)
        suffix[to, :] = f
        decays[to, :] = decay
        f = decay * f
    owned = core[0] * 4 + lax.rem(zl[0], 2) * 2 + lax.div(zl[0], 2)
    owned = pl.multiple_of(owned * STEPS, STEPS)
    own_decay[...] = decays[pl.ds(owned, STEPS), :]


def sum_kernel(weights, late, own_decay, keep, got, out, p, a):
    p[...] = keep[...] + got[...]
    r = jnp.zeros((CHUNKS, K), F32)
    m = jnp.ones((CHUNKS, K), F32)
    for i in reversed(range(TINY)):
        decay = rows(own_decay, i, TINY)
        r = decay * (rows(p, i, TINY) + r)
        m = decay * m
    entries = [jnp.zeros((1, K), F32)]
    for j in reversed(range(CHUNKS)):
        entries.append(m[j : j + 1] * entries[-1] + r[j : j + 1])
    total = entries.pop()
    r = jnp.concatenate(entries[::-1], axis=0)
    for i in reversed(range(TINY)):
        adjoint = rows(p, i, TINY) + r
        a[pl.ds(i, CHUNKS, stride=TINY), :] = adjoint
        r = rows(own_decay, i, TINY) * adjoint
    entry = jnp.sum(weights[...] * late[...], axis=0)
    tail = jnp.concatenate([total, entry, jnp.zeros((PART - STEPS - 2, K), F32)], axis=0)
    for j in range(4):
        out[j, 0:STEPS, :] = a[...]
        out[j, STEPS:PART, :] = tail


def finish_kernel(span, d, chunk, suffix, parts, out):
    _, gain = gains(span[...])
    entry = parts[0, STEPS + 1 : STEPS + 2, :]
    for j in range(1, CHUNKS):
        entry = entry + parts[j, STEPS + 1 : STEPS + 2, :]
    for j in reversed(range(CHUNKS)):
        at = pl.ds(j * STEPS, STEPS)
        part = j // 4 * 4 + j % 2 * 2 + j // 2 % 2
        adjoint = parts[part, 0:STEPS, :] + suffix[at, :] * entry
        out[at, :] = gain * adjoint + d[at, :].astype(F32)
        entry = chunk[0, j : j + 1, :] * entry + parts[part, STEPS : STEPS + 1, :]


def local(x, d, coupling, assay, shift, span, carry, begin):
    here = lax.axis_index(BINS)[None]
    zl, core = lax.axis_index("zl")[None], lax.axis_index("core")[None]
    span = span.reshape(1, K)
    carry = carry.reshape(CHUNKS, STEPS)
    wide, quarter, tile = ((ROWS, K), F32), ((QUARTER, K), F32), ((STEPS, K), F32)
    chunk, sent, shard = call(
        ends_kernel,
        [SMEM] + [HBM] * 7,
        [((3, CHUNKS, K), F32), ((PEERS, 3, K), F32), ((SHARD, K), F32)],
        [
            SMEM((3,), jnp.int32),
            VMEM((1, K), F32),
            VMEM((CHUNKS, STEPS), F32),
            VMEM((TRACKS // K, K), jnp.int32),
            VMEM((TRACKS, K), BF16),
            VMEM((ROWS, K), BF16),
            VMEM((ROWS, K), BF16),
            VMEM(*wide),
            VMEM(*wide),
            pltpu.SemaphoreType.DMA((7,)),
        ],
        vmem=60,
    )(here, begin, span, carry, assay.reshape(TRACKS // K, K), coupling, x, d)
    got = lax.all_to_all(sent, BINS, 0, 0, tiled=True)

    mine = lax.all_gather(shard, "core")
    other = lax.ppermute(mine, "zl", [(i, i ^ 1) for i in range(4)])
    (both,) = call(couple_kernel, [VMEM] * 2, [((3 * K, 4 * TRACKS), BF16)])(mine, other)
    latent, moved, product, shift_t = call(
        prepare_kernel,
        [SMEM] * 4 + [VMEM] * 6,
        [quarter, quarter, quarter, ((QUARTER, K), BF16)],
        [VMEM(*quarter), VMEM(*quarter)],
    )(here, zl, core, begin, span, carry, x, d, chunk, shift)

    keep, send, sent = call(
        tracks_kernel,
        [SMEM] * 2 + [VMEM] * 6,
        [tile] * 2 + [((PEERS, 1, K), F32)],
        [VMEM(*quarter)],
    )(here, zl, got, latent, moved, product, shift_t, both)
    late = lax.all_to_all(sent, BINS, 0, 0, tiled=True)
    received = lax.ppermute(send, "zl", [(i, i ^ 2) for i in range(4)])
    weights, suffix, own_decay = call(
        later_kernel,
        [SMEM] * 4 + [VMEM] * 3,
        [((PEERS, 1, K), F32), wide, tile],
        [VMEM(*wide)],
    )(here, zl, core, begin, span, carry, got)
    (mine,) = call(sum_kernel, [VMEM] * 5, [((4, PART, K), F32)], [VMEM(*tile)] * 2)(
        weights, late, own_decay, keep, received
    )
    column_parts = lax.all_to_all(mine, "zl", 0, 0, tiled=True)
    parts = lax.all_gather(column_parts, "core").reshape(CHUNKS, PART, K)
    (out,) = call(finish_kernel, [VMEM] * 5, [wide])(span, d, chunk, suffix, parts)
    return out


def solution(mesh):
    fine = Mesh(mesh.devices.reshape(8, 2, 4, 4, 2), ("y", "zh", "x", "zl", "core"))
    in_specs = (
        P(BINS, None),
        P(BINS, None),
        P(VIEW, None),
        P(VIEW),
        P(None, BINS),
        P(),
        P(BINS),
        P(),
    )
    return jax.shard_map(
        local, mesh=fine, in_specs=in_specs, out_specs=P(BINS, None), check_vma=False
    )
```

time: 90 us -> 83.6 us (0.929)
  starting transfers between devices: 37.9 us -> 25.7 us
  blocking collectives: 15 us -> 24.7 us
  waiting for transfers between devices: 22.7 us -> 21.1 us
  local copies, waits for them, and re-layouts: 3.97 us -> 2.66 us
    ppermute x4 -> x2, starting transfers between devices: 19.1 us -> 5.9 us  [the longest x1 3.99 us: local(): received = lax.ppermute(send, 'zl', [(i, i ^ 2) for i in range(4)])]
    all_gather x1 -> x2, blocking collectives: 5.98 us -> 15.8 us  [the longest x1 8.98 us: local(): mine = lax.all_gather(shard, 'core')]
    unnamed x24 -> x20, local copies, waits for them, and re-layouts: 3.9 us -> 2.66 us
    all_to_all x1, starting transfers between devices: 13.4 us -> 14.6 us  [local(): got = lax.all_to_all(sent, BINS, 0, 0, tiled=True)]
    pallas_call x7 -> x6, Pallas kernels: 8.71 us -> 8.02 us  [the longest x1 2.7 us: local(): call(ends_kernel, [SMEM] + [HBM] * 7, [((3, CHUNKS, K), F32), ((PEERS, 3,...]
  transfers between devices with their start and end apart: 6 -> 4, of which waited for: 2 -> 2; matrix products, arithmetic and copies ran while one was open for 0% -> 0% of each run, Pallas kernels for 4% -> 4%
where the time goes in v3:
time: 83.6 us; the launch traced here: 83.2 us
  starting transfers between devices  25.7 us (31%)
  blocking collectives  24.7 us (30%)
  waiting for transfers between devices  21.1 us (25%)
  Pallas kernels  8.92 us (11%)
  local copies, waits for them, and re-layouts  2.66 us (3%)
    all_to_all x1, starting transfers between devices, local(): got = lax.all_to_all(sent, BINS, 0, 0, tiled=True)  14.6 us
    all_to_all x1, waiting for transfers between devices, local(): late = lax.all_to_all(sent, BINS, 0, 0, tiled=True)  11.7 us
    all_to_all x1, waiting for transfers between devices, local(): got = lax.all_to_all(sent, BINS, 0, 0, tiled=True)  9.41 us
    all_gather x1, blocking collectives, local(): mine = lax.all_gather(shard, 'core')  8.98 us
    all_to_all x1, blocking collectives, local(): column_parts = lax.all_to_all(mine, 'zl', 0, 0, tiled=True)  8.93 us
    all_gather x1, blocking collectives, local(): parts = lax.all_gather(column_parts, 'core').reshape(CHUNKS, PART, K)  6.77 us
    all_to_all x1, starting transfers between devices, local(): late = lax.all_to_all(sent, BINS, 0, 0, tiled=True)  5.19 us
    ppermute x1, starting transfers between devices, local(): received = lax.ppermute(send, 'zl', [(i, i ^ 2) for i in range(4)])  3.99 us
  transfers between devices with their start and end apart: 4, of which 2 were waited for; matrix products, arithmetic and copies ran while one was open for 0% of the time, Pallas kernels for 4%

profile of v3, /device:TPU:1, one launch (start us, length us, event | category | flops | bytes accessed | tf_op | source)
XLA Modules:
  0.0 83.2 jit_solution(7277622077826252641)
XLA Ops:
  0.0 0.0 copy-start.8
  0.0 0.0 copy-start.6
  0.0 0.0 copy-start.9
  0.0 0.0 copy-start.1
  0.0 0.0 copy-start
  0.0 0.0 copy-start.7
  0.0 2.7 %shard_map.82 = (f32[3,8,128]{2,1,0:T(8,128)}, f32[64,3,128]{2,1,0:T(4,128)}, f32[648,128]{1,0:T(8,128)}) custom-call(s32[1]{0:T(128)} %bitcast.1.here, s32[3]{0:T(128)} %begin.3, f32[1,128]{1,0:T(1,128)} %bitcast.12, f32[8,128]{1,0:T(8,128)} %bitcast.9, s32[5,128]{1,0:T(8,128)} %bitcast.16, bf16[640,128]{1,0:T(8,128)(2,1)} %coupling_hbm.1, ...), custom_call_target="tpu_custom_call" | custom-call | tf_op jit(solution)/shard_map/pallas_call | solution.py:269
  2.8 9.0 %all-gather = f32[1296,128]{1,0:T(8,128)S(1)} all-gather(f32[648,128]{1,0:T(8,128)} %get-tuple-element.26), channel_id=2, replica_groups=mesh['y'=8,'zh'=2,'x'=4,'zl'=4,'core'=2] {'core'}, dimensions={0}, use_global_device_ids=true | all-gather | bytes 995328 | tf_op jit(solution)/shard_map/all_gather | solution.py:289
  11.7 1.9 %collective-permute-start = (f32[2,648,128]{2,1,0:T(8,128)S(1)}, f32[2,648,128]{2,1,0:T(8,128)S(1)}, u32[]{:S(2)}, u32[]{:S(2)}) collective-permute-start(f32[2,648,128]{2,1,0:T(8,128)S(1)} %bitcast.7), channel_id=1, source_target_pairs={{0,2},{2,0},{4,6},{6,4},{1,3},{3,1},{5,7},{7,5},{8,10},{10,8},{12,... | collective-permute-start | bytes 1990664 | tf_op jit(solution)/shard_map/ppermute | solution.py:290
  13.7 14.6 %all-to-all-start = ((f32[64,3,128]{2,1,0:T(4,128)}), f32[64,3,128]{2,1,0:T(4,128)S(1)}, u32[]{:S(2)}, u32[]{:S(2)}) async-start(f32[64,3,128]{2,1,0:T(4,128)} %get-tuple-element.19), calls=%async_computation | async-start | bytes 262144 | tf_op jit(solution)/shard_map/all_to_all | solution.py:287
  28.2 0.0 copy-done.8
  28.3 0.0 copy-done.6
  28.3 0.0 copy-done.9
  28.3 0.0 copy-done.1
  28.3 0.0 copy-done
  28.3 0.0 copy-done.7
  28.3 0.0 copy-start.4
  28.3 0.7 copy-done.4
  29.0 1.2 %shard_map.84 = (f32[256,128]{1,0:T(8,128)S(1)}, f32[256,128]{1,0:T(8,128)S(1)}, f32[256,128]{1,0:T(8,128)S(1)}, bf16[256,128]{1,0:T(8,128)(2,1)S(1)}) custom-call(s32[1]{0:T(128)} %bitcast.1.here, s32[1]{0:T(128)} %bitcast.4.zl, s32[1]{0:T(128)} %bitcast.5.core, s32[3]{0:T(128)S(1)} %copy-done.9, f32[1,128]{1,0:T(1,128)S(1)} %bitcast.13, ...), custom_call_target="tpu_custom_call" | custom-call | tf_op jit(solution)/shard_map/pallas_call | solution.py:292
  30.3 0.0 collective-permute-done.other
  30.3 0.0 copy-start.2
  30.3 0.8 %copy-done.2 = f32[2,648,128]{2,1,0:T(8,128)} copy-done((f32[2,648,128]{2,1,0:T(8,128)}, f32[2,648,128]{2,1,0:T(8,128)S(1)}, u32[]{:S(2)}) %copy-start.2) | copy-done | bytes 663576
  31.1 0.0 copy-start.3
  31.1 1.1 %copy-done.3 = f32[2,648,128]{2,1,0:T(8,128)S(1)} copy-done((f32[2,648,128]{2,1,0:T(8,128)S(1)}, f32[2,648,128]{2,1,0:T(8,128)}, u32[]{:S(2)}) %copy-start.3) | copy-done | bytes 663576
  32.2 0.3 shard_map.85.both
  32.5 9.4 %all-to-all-done.got = f32[64,3,128]{2,1,0:T(4,128)S(1)} async-done(((f32[64,3,128]{2,1,0:T(4,128)}), f32[64,3,128]{2,1,0:T(4,128)S(1)}, u32[]{:S(2)}, u32[]{:S(2)}) %all-to-all-start) | async-done | bytes 98336 | tf_op jit(solution)/shard_map/all_to_all | solution.py:287
  41.9 0.0 copy-start.5
  41.9 2.2 %shard_map.86 = (f32[128,128]{1,0:T(8,128)S(1)}, f32[128,128]{1,0:T(8,128)S(1)}, f32[64,1,128]{2,1,0:T(1,128)}) custom-call(s32[1]{0:T(128)} %bitcast.1.here, s32[1]{0:T(128)} %bitcast.4.zl, f32[64,3,128]{2,1,0:T(4,128)S(1)} %all-to-all-done.got, f32[256,128]{1,0:T(8,128)S(1)} %get-tuple-element.22.latent_ref, f32[256,128]{1,0:T(8,128)S(1)} %get-tuple-element.23.moved_ref, ...), custom_call_target="tpu_custom_call" | custom-call | tf_op jit(solution)/shard_map/pallas_call | solution.py:299
  44.1 4.0 %collective-permute-start.1 = (f32[128,128]{1,0:T(8,128)S(1)}, f32[128,128]{1,0:T(8,128)S(1)}, u32[]{:S(2)}, u32[]{:S(2)}) collective-permute-start(f32[128,128]{1,0:T(8,128)S(1)} %get-tuple-element.30), channel_id=1, source_target_pairs={{0,4},{2,6},{4,0},{6,2},{1,5},{3,7},{5,1},{7,3},{8,12},{10,14},{12... | collective-permute-start | bytes 196616 | tf_op jit(solution)/shard_map/ppermute | solution.py:306
  48.1 5.2 %all-to-all-start.1 = ((f32[64,1,128]{2,1,0:T(1,128)}), f32[64,1,128]{2,1,0:T(1,128)S(1)}, u32[]{:S(2)}, u32[]{:S(2)}) async-start(f32[64,1,128]{2,1,0:T(1,128)} %get-tuple-element.27), calls=%async_computation.1 | async-start | bytes 65536 | tf_op jit(solution)/shard_map/all_to_all | solution.py:305
  53.3 1.4 %shard_map.83 = (f32[64,1,128]{2,1,0:T(1,128)S(1)}, f32[1024,128]{1,0:T(8,128)S(1)}, f32[128,128]{1,0:T(8,128)S(1)}) custom-call(s32[1]{0:T(128)} %bitcast.1.here, s32[1]{0:T(128)} %bitcast.4.zl, s32[1]{0:T(128)} %bitcast.5.core, s32[3]{0:T(128)S(1)} %copy-done.9, f32[1,128]{1,0:T(1,128)S(1)} %bitcast.14, f32[8,128]{1,0:T(8,128)S(1)} %bitcast.11, ...), custom_call_target="tpu_custom_call" | custom-call | tf_op jit(solution)/shard_map/pallas_call | solution.py:307
  54.8 11.7 %all-to-all-done.1.late = f32[64,1,128]{2,1,0:T(1,128)S(1)} async-done(((f32[64,1,128]{2,1,0:T(1,128)}), f32[64,1,128]{2,1,0:T(1,128)S(1)}, u32[]{:S(2)}, u32[]{:S(2)}) %all-to-all-start.1) | async-done | bytes 32800 | tf_op jit(solution)/shard_map/all_to_all | solution.py:305
  66.4 0.0 collective-permute-done.1.got
  66.4 0.1 shard_map.87
  66.6 8.9 %all_to_all.15 = f32[4,136,128]{2,1,0:T(8,128)S(1)} all-to-all(f32[4,136,128]{2,1,0:T(8,128)S(1)} %shard_map.87), channel_id=1, replica_groups=mesh['y'=8,'zh'=2,'x'=4,'zl'=4,'core'=2] {'zl'}, dimensions={0} | all-to-all | bytes 557056 | tf_op jit(solution)/shard_map/all_to_all | solution.py:316
  75.5 6.8 %all-gather.1.parts = f32[8,136,128]{2,1,0:T(8,128)S(1)} all-gather(f32[4,136,128]{2,1,0:T(8,128)S(1)} %all_to_all.15), channel_id=3, replica_groups=mesh['y'=8,'zh'=2,'x'=4,'zl'=4,'core'=2] {'core'}, dimensions={0}, use_global_device_ids=true | all-gather | bytes 835584 | tf_op jit(solution)/shard_map/all_gather | solution.py:317
  82.3 0.0 copy-done.5
  82.3 0.9 %shard_map.88 = f32[1024,128]{1,0:T(8,128)} custom-call(f32[1,128]{1,0:T(1,128)S(1)} %bitcast.15, bf16[1024,128]{1,0:T(8,128)(2,1)S(1)} %copy-done, f32[3,8,128]{2,1,0:T(8,128)S(1)} %copy-done.5, f32[1024,128]{1,0:T(8,128)S(1)} %get-tuple-element.20.suffix, f32[8,136,128]{2,1,0:T(8,128)S(1)} %all-gather.1.parts), custom_call_target="tpu_custom_call" | custom-call | tf_op jit(solution)/shard_map/pallas_call | solution.py:318
Async XLA Ops:
  0.0 28.2 %copy-start.8 = (f32[128]{0:T(128)S(1)}, f32[128]{0:T(128)}, u32[]{:S(2)}) copy-start(f32[128]{0:T(128)} %param.13) | copy-start | bytes 1540
  0.0 28.3 %copy-start.6 = (f32[1024]{0:T(1024)S(1)}, f32[1024]{0:T(1024)}, u32[]{:S(2)}) copy-start(f32[1024]{0:T(1024)} %param.14) | copy-start | bytes 12292
  0.0 28.3 %copy-start.9 = (s32[3]{0:T(128)S(1)}, s32[3]{0:T(128)}, u32[]{:S(2)}) copy-start(s32[3]{0:T(128)} %begin.3) | copy-start | bytes 40
  0.0 28.3 %copy-start.1 = (bf16[1024,128]{1,0:T(8,128)(2,1)S(1)}, bf16[1024,128]{1,0:T(8,128)(2,1)}, u32[]{:S(2)}) copy-start(bf16[1024,128]{1,0:T(8,128)(2,1)} %x.1) | copy-start | bytes 786436
  0.0 28.3 %copy-start = (bf16[1024,128]{1,0:T(8,128)(2,1)S(1)}, bf16[1024,128]{1,0:T(8,128)(2,1)}, u32[]{:S(2)}) copy-start(bf16[1024,128]{1,0:T(8,128)(2,1)} %d.3) | copy-start | bytes 786436
  0.0 28.3 %copy-start.7 = (f32[8,1024]{1,0:T(8,128)S(1)}, f32[8,1024]{1,0:T(8,128)}, u32[]{:S(2)}) copy-start(f32[8,1024]{1,0:T(8,128)} %shift.1) | copy-start | bytes 98308
  11.7 18.5 %collective-permute-start = (f32[2,648,128]{2,1,0:T(8,128)S(1)}, f32[2,648,128]{2,1,0:T(8,128)S(1)}, u32[]{:S(2)}, u32[]{:S(2)}) collective-permute-start(f32[2,648,128]{2,1,0:T(8,128)S(1)} %bitcast.7), channel_id=1, source_target_pairs={{0,2},{2,0},{4,6},{6,4},{1,3},{3,1},{5,7},{7,5},{8,10},{10,8},{12,... | collective-permute-start | bytes 1990664 | tf_op jit(solution)/shard_map/ppermute | solution.py:290
  13.7 28.2 %all-to-all-start = ((f32[64,3,128]{2,1,0:T(4,128)}), f32[64,3,128]{2,1,0:T(4,128)S(1)}, u32[]{:S(2)}, u32[]{:S(2)}) async-start(f32[64,3,128]{2,1,0:T(4,128)} %get-tuple-element.19), calls=%async_computation | async-start | bytes 262144 | tf_op jit(solution)/shard_map/all_to_all | solution.py:287
  28.3 0.7 copy-start.4
  30.3 0.9 %copy-start.2 = (f32[2,648,128]{2,1,0:T(8,128)}, f32[2,648,128]{2,1,0:T(8,128)S(1)}, u32[]{:S(2)}) copy-start(f32[2,648,128]{2,1,0:T(8,128)S(1)} %collective-permute-done.other) | copy-start | bytes 1990660
  31.1 1.1 %copy-start.3 = (f32[2,648,128]{2,1,0:T(8,128)S(1)}, f32[2,648,128]{2,1,0:T(8,128)}, u32[]{:S(2)}) copy-start(f32[2,648,128]{2,1,0:T(8,128)} %copy-done.2) | copy-start | bytes 1990660
  41.9 40.4 %copy-start.5 = (f32[3,8,128]{2,1,0:T(8,128)S(1)}, f32[3,8,128]{2,1,0:T(8,128)}, u32[]{:S(2)}) copy-start(f32[3,8,128]{2,1,0:T(8,128)} %get-tuple-element.18.chunk) | copy-start | bytes 36868
  44.1 22.3 %collective-permute-start.1 = (f32[128,128]{1,0:T(8,128)S(1)}, f32[128,128]{1,0:T(8,128)S(1)}, u32[]{:S(2)}, u32[]{:S(2)}) collective-permute-start(f32[128,128]{1,0:T(8,128)S(1)} %get-tuple-element.30), channel_id=1, source_target_pairs={{0,4},{2,6},{4,0},{6,2},{1,5},{3,7},{5,1},{7,3},{8,12},{10,14},{12... | collective-permute-start | bytes 196616 | tf_op jit(solution)/shard_map/ppermute | solution.py:306
  48.1 18.3 %all-to-all-start.1 = ((f32[64,1,128]{2,1,0:T(1,128)}), f32[64,1,128]{2,1,0:T(1,128)S(1)}, u32[]{:S(2)}, u32[]{:S(2)}) async-start(f32[64,1,128]{2,1,0:T(1,128)} %get-tuple-element.27), calls=%async_computation.1 | async-start | bytes 65536 | tf_op jit(solution)/shard_map/all_to_all | solution.py:305

commit v4 on v3

--- a/solution.py
+++ b/solution.py
@@ -104,8 +104,8 @@
 
 
 def prepare_kernel(
-    here, zl, core, begin, span, carry_ref, x, d, chunk, shift,
-    latent, moved, product, shift_t, xs, ds,
+    here, zl, core, begin, span, carry_ref, x, d, chunk, shift, mine,
+    latent, moved, product, shift_t, both, xs, ds,
 ):
     at = core[0] * 4 + lax.rem(zl[0], 2) * 2
     start = pl.multiple_of(at * STEPS, QUARTER)
@@ -152,11 +152,12 @@
     low = s - hi - mid
     blank = jnp.zeros((K - 3 * NVIEW, QUARTER), F32)
     shift_t[...] = jnp.concatenate([hi, mid, low, blank], axis=0).T.astype(BF16)
-
-
-def couple_kernel(mine, other, both):
-    for side in range(4):
-        ref = (mine, other)[side // 2].at[side % 2]
+    couple(mine, both)
+
+
+def couple(shards, both):
+    for side in range(2):
+        ref = shards.at[side]
         at = pl.ds(side * TRACKS, TRACKS)
         w = ref[0:TRACKS, :]
         both[0:K, at] = w.T.astype(BF16)
@@ -172,9 +173,10 @@
 
 
 def tracks_kernel(
-    here, zl, got, latent_ref, moved_ref, product_ref, shift_t, both,
-    keep, send, sent, pulled,
+    here, zl, got, latent_ref, moved_ref, product_ref, shift_t, mine, other,
+    keep, send, sent, pulled, theirs,
 ):
+    couple(other, theirs)
     ez = jnp.zeros((1, K), F32)
     ev = jnp.zeros((1, K), F32)
     for e in range(PEERS - 1):
@@ -188,7 +190,7 @@
     moved = (moved_ref[...] + product * ev).astype(BF16)
     p = jnp.zeros((QUARTER, K), F32)
     for side in range(4):
-        at = pl.ds(side * TRACKS, TRACKS)
+        both, at = (mine, theirs)[side // 2], pl.ds(side % 2 * TRACKS, TRACKS)
         log_rate = jnp.dot(latent, both[0 : 2 * K, at], preferred_element_type=F32)
         along = jnp.dot(moved, both[0:K, at], preferred_element_type=F32)
         weighted = (jnp.exp(log_rate) * along).astype(BF16)
@@ -266,6 +268,7 @@
     span = span.reshape(1, K)
     carry = carry.reshape(CHUNKS, STEPS)
     wide, quarter, tile = ((ROWS, K), F32), ((QUARTER, K), F32), ((STEPS, K), F32)
+    packed = ((3 * K, 2 * TRACKS), BF16)
     chunk, sent, shard = call(
         ends_kernel,
         [SMEM] + [HBM] * 7,
@@ -288,20 +291,19 @@
 
     mine = lax.all_gather(shard, "core")
     other = lax.ppermute(mine, "zl", [(i, i ^ 1) for i in range(4)])
-    (both,) = call(couple_kernel, [VMEM] * 2, [((3 * K, 4 * TRACKS), BF16)])(mine, other)
-    latent, moved, product, shift_t = call(
+    latent, moved, product, shift_t, both = call(
         prepare_kernel,
-        [SMEM] * 4 + [VMEM] * 6,
-        [quarter, quarter, quarter, ((QUARTER, K), BF16)],
+        [SMEM] * 4 + [VMEM] * 7,
+        [quarter, quarter, quarter, ((QUARTER, K), BF16), packed],
         [VMEM(*quarter), VMEM(*quarter)],
-    )(here, zl, core, begin, span, carry, x, d, chunk, shift)
+    )(here, zl, core, begin, span, carry, x, d, chunk, shift, mine)
 
     keep, send, sent = call(
         tracks_kernel,
-        [SMEM] * 2 + [VMEM] * 6,
+        [SMEM] * 2 + [VMEM] * 7,
         [tile] * 2 + [((PEERS, 1, K), F32)],
-        [VMEM(*quarter)],
-    )(here, zl, got, latent, moved, product, shift_t, both)
+        [VMEM(*quarter), VMEM(*packed)],
+    )(here, zl, got, latent, moved, product, shift_t, both, other)
     late = lax.all_to_all(sent, BINS, 0, 0, tiled=True)
     received = lax.ppermute(send, "zl", [(i, i ^ 2) for i in range(4)])
     weights, suffix, own_decay = call(

time: 83.6 us -> 83 us (level)
  waiting for transfers between devices: 21.1 us -> 23.3 us
  local copies, waits for them, and re-layouts: 2.66 us -> 0.67 us
    all_to_all x1, waiting for transfers between devices: 9.41 us -> 11.6 us  [local(): got = lax.all_to_all(sent, BINS, 0, 0, tiled=True)]
    unnamed x20 -> x14, local copies, waits for them, and re-layouts: 2.66 us -> 0.67 us
    pallas_call x3 -> x2, Pallas kernels: 3.73 us -> 3.64 us  [the longest x1 2.27 us: local(): call(tracks_kernel, [SMEM] * 2 + [VMEM] * 7, [tile] * 2 + [((PEERS, 1, K)...]
  transfers between devices with their start and end apart: 4 -> 4, of which waited for: 2 -> 2; matrix products, arithmetic and copies ran while one was open for 0% -> 0% of each run, Pallas kernels for 4% -> 3%
where the time goes in v4:
time: 83 us; the launch traced here: 82.6 us
  starting transfers between devices  25.2 us (30%)
  blocking collectives  24.5 us (30%)
  waiting for transfers between devices  23.3 us (28%)
  Pallas kernels  8.77 us (11%)
    all_to_all x1, starting transfers between devices, local(): got = lax.all_to_all(sent, BINS, 0, 0, tiled=True)  14.6 us
    all_to_all x1, waiting for transfers between devices, local(): late = lax.all_to_all(sent, BINS, 0, 0, tiled=True)  11.7 us
    all_to_all x1, waiting for transfers between devices, local(): got = lax.all_to_all(sent, BINS, 0, 0, tiled=True)  11.6 us
    all_gather x1, blocking collectives, local(): mine = lax.all_gather(shard, 'core')  9.13 us
    all_to_all x1, blocking collectives, local(): column_parts = lax.all_to_all(mine, 'zl', 0, 0, tiled=True)  8.93 us
    all_gather x1, blocking collectives, local(): parts = lax.all_gather(column_parts, 'core').reshape(CHUNKS, PART, K)  6.49 us
    all_to_all x1, starting transfers between devices, local(): late = lax.all_to_all(sent, BINS, 0, 0, tiled=True)  4.6 us
    ppermute x1, starting transfers between devices, local(): received = lax.ppermute(send, 'zl', [(i, i ^ 2) for i in range(4)])  4 us
  transfers between devices with their start and end apart: 4, of which 2 were waited for; matrix products, arithmetic and copies ran while one was open for 0% of the time, Pallas kernels for 3%

profile of v4, /device:TPU:1, one launch (start us, length us, event | category | flops | bytes accessed | tf_op | source)
XLA Modules:
  0.0 82.6 jit_solution(7775474701204514216)
XLA Ops:
  0.0 2.6 %shard_map.82 = (f32[3,8,128]{2,1,0:T(8,128)}, f32[64,3,128]{2,1,0:T(4,128)}, f32[648,128]{1,0:T(8,128)}) custom-call(s32[1]{0:T(128)} %bitcast.1.here, s32[3]{0:T(128)} %begin.3, f32[1,128]{1,0:T(1,128)} %bitcast.12, f32[8,128]{1,0:T(8,128)} %bitcast.9, s32[5,128]{1,0:T(8,128)} %bitcast.16, bf16[640,128]{1,0:T(8,128)(2,1)} %coupling_hbm.1, ...), custom_call_target="tpu_custom_call" | custom-call | tf_op jit(solution)/shard_map/pallas_call | solution.py:272
  2.7 0.0 copy-start.1
  2.7 0.0 copy-start.4
  2.7 9.1 %all-gather = f32[1296,128]{1,0:T(8,128)S(1)} all-gather(f32[648,128]{1,0:T(8,128)} %get-tuple-element.23), channel_id=2, replica_groups=mesh['y'=8,'zh'=2,'x'=4,'zl'=4,'core'=2] {'core'}, dimensions={0}, use_global_device_ids=true | all-gather | bytes 995328 | tf_op jit(solution)/shard_map/all_gather | solution.py:292
  11.8 0.0 copy-start
  11.8 2.0 %collective-permute-start = (f32[2,648,128]{2,1,0:T(8,128)S(1)}, f32[2,648,128]{2,1,0:T(8,128)S(1)}, u32[]{:S(2)}, u32[]{:S(2)}) collective-permute-start(f32[2,648,128]{2,1,0:T(8,128)S(1)} %bitcast.7), channel_id=1, source_target_pairs={{0,2},{2,0},{4,6},{6,4},{1,3},{3,1},{5,7},{7,5},{8,10},{10,8},{12,... | collective-permute-start | bytes 1990664 | tf_op jit(solution)/shard_map/ppermute | solution.py:293
  13.9 0.0 copy-start.3
  13.9 14.6 %all-to-all-start = ((f32[64,3,128]{2,1,0:T(4,128)}), f32[64,3,128]{2,1,0:T(4,128)S(1)}, u32[]{:S(2)}, u32[]{:S(2)}) async-start(f32[64,3,128]{2,1,0:T(4,128)} %get-tuple-element.20), calls=%async_computation | async-start | bytes 262144 | tf_op jit(solution)/shard_map/all_to_all | solution.py:290
  28.4 0.0 copy-start.2
  28.4 0.0 copy-start.5
  28.5 0.0 copy-start.6
  28.5 0.0 copy-done.1
  28.5 0.0 copy-done.4
  28.5 0.0 copy-done
  28.5 0.0 copy-done.3
  28.5 0.6 copy-done.2
  29.1 0.0 copy-done.5
  29.1 0.0 copy-done.6
  29.1 1.4 %shard_map.84 = (f32[256,128]{1,0:T(8,128)S(1)}, f32[256,128]{1,0:T(8,128)S(1)}, f32[256,128]{1,0:T(8,128)S(1)}, bf16[256,128]{1,0:T(8,128)(2,1)S(1)}, bf16[384,1280]{1,0:T(8,128)(2,1)S(1)}) custom-call(s32[1]{0:T(128)} %bitcast.1.here, s32[1]{0:T(128)} %bitcast.4.zl, s32[1]{0:T(128)} %bitcast.5.core, s32[3]{0:T(128)S(1)} %copy-done.6, ...), custom_call_target="tpu_custom_call" | custom-call | tf_op jit(solution)/shard_map/pallas_call | solution.py:294
  30.5 11.6 %all-to-all-done.got = f32[64,3,128]{2,1,0:T(4,128)S(1)} async-done(((f32[64,3,128]{2,1,0:T(4,128)}), f32[64,3,128]{2,1,0:T(4,128)S(1)}, u32[]{:S(2)}, u32[]{:S(2)}) %all-to-all-start) | async-done | bytes 98336 | tf_op jit(solution)/shard_map/all_to_all | solution.py:290
  42.1 0.0 collective-permute-done.other
  42.1 2.3 %shard_map.85 = (f32[128,128]{1,0:T(8,128)S(1)}, f32[128,128]{1,0:T(8,128)S(1)}, f32[64,1,128]{2,1,0:T(1,128)}) custom-call(s32[1]{0:T(128)} %bitcast.1.here, s32[1]{0:T(128)} %bitcast.4.zl, f32[64,3,128]{2,1,0:T(4,128)S(1)} %all-to-all-done.got, f32[256,128]{1,0:T(8,128)S(1)} %get-tuple-element.24.latent_ref, f32[256,128]{1,0:T(8,128)S(1)} %get-tuple-element.25.moved_ref, ...), custom_call_target="tpu_custom_call" | custom-call | tf_op jit(solution)/shard_map/pallas_call | solution.py:301
  44.4 4.0 %collective-permute-start.1 = (f32[128,128]{1,0:T(8,128)S(1)}, f32[128,128]{1,0:T(8,128)S(1)}, u32[]{:S(2)}, u32[]{:S(2)}) collective-permute-start(f32[128,128]{1,0:T(8,128)S(1)} %get-tuple-element.32), channel_id=1, source_target_pairs={{0,4},{2,6},{4,0},{6,2},{1,5},{3,7},{5,1},{7,3},{8,12},{10,14},{12... | collective-permute-start | bytes 196616 | tf_op jit(solution)/shard_map/ppermute | solution.py:308
  48.4 4.6 %all-to-all-start.1 = ((f32[64,1,128]{2,1,0:T(1,128)}), f32[64,1,128]{2,1,0:T(1,128)S(1)}, u32[]{:S(2)}, u32[]{:S(2)}) async-start(f32[64,1,128]{2,1,0:T(1,128)} %get-tuple-element.29), calls=%async_computation.1 | async-start | bytes 65536 | tf_op jit(solution)/shard_map/all_to_all | solution.py:307
  53.0 1.4 %shard_map.83 = (f32[64,1,128]{2,1,0:T(1,128)S(1)}, f32[1024,128]{1,0:T(8,128)S(1)}, f32[128,128]{1,0:T(8,128)S(1)}) custom-call(s32[1]{0:T(128)} %bitcast.1.here, s32[1]{0:T(128)} %bitcast.4.zl, s32[1]{0:T(128)} %bitcast.5.core, s32[3]{0:T(128)S(1)} %copy-done.6, f32[1,128]{1,0:T(1,128)S(1)} %bitcast.14, f32[8,128]{1,0:T(8,128)S(1)} %bitcast.11, ...), custom_call_target="tpu_custom_call" | custom-call | tf_op jit(solution)/shard_map/pallas_call | solution.py:309
  54.4 11.7 %all-to-all-done.1.late = f32[64,1,128]{2,1,0:T(1,128)S(1)} async-done(((f32[64,1,128]{2,1,0:T(1,128)}), f32[64,1,128]{2,1,0:T(1,128)S(1)}, u32[]{:S(2)}, u32[]{:S(2)}) %all-to-all-start.1) | async-done | bytes 32800 | tf_op jit(solution)/shard_map/all_to_all | solution.py:307
  66.1 0.0 collective-permute-done.1.got
  66.1 0.1 shard_map.86
  66.3 8.9 %all_to_all.15 = f32[4,136,128]{2,1,0:T(8,128)S(1)} all-to-all(f32[4,136,128]{2,1,0:T(8,128)S(1)} %shard_map.86), channel_id=1, replica_groups=mesh['y'=8,'zh'=2,'x'=4,'zl'=4,'core'=2] {'zl'}, dimensions={0} | all-to-all | bytes 557056 | tf_op jit(solution)/shard_map/all_to_all | solution.py:318
  75.2 6.5 %all-gather.1.parts = f32[8,136,128]{2,1,0:T(8,128)S(1)} all-gather(f32[4,136,128]{2,1,0:T(8,128)S(1)} %all_to_all.15), channel_id=3, replica_groups=mesh['y'=8,'zh'=2,'x'=4,'zl'=4,'core'=2] {'core'}, dimensions={0}, use_global_device_ids=true | all-gather | bytes 835584 | tf_op jit(solution)/shard_map/all_gather | solution.py:319
  81.7 0.9 %shard_map.87 = f32[1024,128]{1,0:T(8,128)} custom-call(f32[1,128]{1,0:T(1,128)S(1)} %bitcast.15, bf16[1024,128]{1,0:T(8,128)(2,1)S(1)} %copy-done, f32[3,8,128]{2,1,0:T(8,128)S(1)} %copy-done.2, f32[1024,128]{1,0:T(8,128)S(1)} %get-tuple-element.21.suffix, f32[8,136,128]{2,1,0:T(8,128)S(1)} %all-gather.1.parts), custom_call_target="tpu_custom_call" | custom-call | tf_op jit(solution)/shard_map/pallas_call | solution.py:320
Async XLA Ops:
  2.7 25.8 %copy-start.1 = (bf16[1024,128]{1,0:T(8,128)(2,1)S(1)}, bf16[1024,128]{1,0:T(8,128)(2,1)}, u32[]{:S(2)}) copy-start(bf16[1024,128]{1,0:T(8,128)(2,1)} %x.1) | copy-start | bytes 786436
  2.7 25.8 %copy-start.4 = (f32[8,1024]{1,0:T(8,128)S(1)}, f32[8,1024]{1,0:T(8,128)}, u32[]{:S(2)}) copy-start(f32[8,1024]{1,0:T(8,128)} %shift.1) | copy-start | bytes 98308
  11.8 16.7 %copy-start = (bf16[1024,128]{1,0:T(8,128)(2,1)S(1)}, bf16[1024,128]{1,0:T(8,128)(2,1)}, u32[]{:S(2)}) copy-start(bf16[1024,128]{1,0:T(8,128)(2,1)} %d.3) | copy-start | bytes 786436
  11.8 30.3 %collective-permute-start = (f32[2,648,128]{2,1,0:T(8,128)S(1)}, f32[2,648,128]{2,1,0:T(8,128)S(1)}, u32[]{:S(2)}, u32[]{:S(2)}) collective-permute-start(f32[2,648,128]{2,1,0:T(8,128)S(1)} %bitcast.7), channel_id=1, source_target_pairs={{0,2},{2,0},{4,6},{6,4},{1,3},{3,1},{5,7},{7,5},{8,10},{10,8},{12,... | collective-permute-start | bytes 1990664 | tf_op jit(solution)/shard_map/ppermute | solution.py:293
  13.9 14.6 %copy-start.3 = (f32[1024]{0:T(1024)S(1)}, f32[1024]{0:T(1024)}, u32[]{:S(2)}) copy-start(f32[1024]{0:T(1024)} %param.14) | copy-start | bytes 12292
  13.9 28.2 %all-to-all-start = ((f32[64,3,128]{2,1,0:T(4,128)}), f32[64,3,128]{2,1,0:T(4,128)S(1)}, u32[]{:S(2)}, u32[]{:S(2)}) async-start(f32[64,3,128]{2,1,0:T(4,128)} %get-tuple-element.20), calls=%async_computation | async-start | bytes 262144 | tf_op jit(solution)/shard_map/all_to_all | solution.py:290
  28.4 0.7 copy-start.2
  28.4 0.7 copy-start.5
  28.5 0.7 copy-start.6
  44.4 21.7 %collective-permute-start.1 = (f32[128,128]{1,0:T(8,128)S(1)}, f32[128,128]{1,0:T(8,128)S(1)}, u32[]{:S(2)}, u32[]{:S(2)}) collective-permute-start(f32[128,128]{1,0:T(8,128)S(1)} %get-tuple-element.32), channel_id=1, source_target_pairs={{0,4},{2,6},{4,0},{6,2},{1,5},{3,7},{5,1},{7,3},{8,12},{10,14},{12... | collective-permute-start | bytes 196616 | tf_op jit(solution)/shard_map/ppermute | solution.py:308
  48.4 17.7 %all-to-all-start.1 = ((f32[64,1,128]{2,1,0:T(1,128)}), f32[64,1,128]{2,1,0:T(1,128)S(1)}, u32[]{:S(2)}, u32[]{:S(2)}) async-start(f32[64,1,128]{2,1,0:T(1,128)} %get-tuple-element.29), calls=%async_computation.1 | async-start | bytes 65536 | tf_op jit(solution)/shard_map/all_to_all | solution.py:307

commit v5 on v4

--- a/solution.py
+++ b/solution.py
@@ -9,9 +9,9 @@
 PEERS, NVIEW, TRACKS = 64, 8, 640
 SHARD = TRACKS + 8
 FINE = 32
-TINY = 16
-PART = STEPS + 8
-BINS, VIEW = ("y", "zh", "x"), ("zl", "core")
+PAD = STEPS + 8
+PART = QUARTER + 8
+BINS, VIEW = ("y", "zh", "x"), ("zb", "za", "core")
 VMEM, SMEM, HBM = pltpu.VMEM, pltpu.SMEM, pltpu.HBM
 F32, BF16 = jnp.float32, jnp.bfloat16
 
@@ -20,11 +20,11 @@
     return pl.BlockSpec(memory_space=space)
 
 
-def call(body, ins, outs, scratch=(), vmem=16):
+def call(body, ins, outs, scratch=(), vmem=16, spaces=None):
     return pl.pallas_call(
         body,
         in_specs=[spec(s) for s in ins],
-        out_specs=[spec(VMEM) for _ in outs],
+        out_specs=[spec(s) for s in spaces or [VMEM] * len(outs)],
         out_shape=[jax.ShapeDtypeStruct(shape, dtype) for shape, dtype in outs],
         scratch_shapes=list(scratch),
         compiler_params=pltpu.CompilerParams(vmem_limit_bytes=vmem * 1024 * 1024),
@@ -56,39 +56,46 @@
 
 
 def ends_kernel(
-    here, begin_hbm, span_hbm, carry_hbm, assay_hbm, coupling_hbm, x_hbm, d_hbm, chunk, sent, shard,
-    begin, span, carry_ref, assay, coupling, x, d, xs, ds, sems,
+    here, begin_hbm, span_hbm, carry_hbm, assay_hbm, coupling_hbm, x_hbm, d_hbm,
+    chunk, sent, shard_hbm,
+    begin, span, carry_ref, assay, coupling, x, d, shard, xs, ds, sems,
 ):
     pairs = [
-        (x_hbm, x),
-        (d_hbm, d),
         (coupling_hbm, coupling),
         (assay_hbm, assay),
         (carry_hbm, carry_ref),
         (span_hbm, span),
         (begin_hbm, begin),
+        (x_hbm, x),
+        (d_hbm, d),
     ]
     copies = [pltpu.make_async_copy(a, b, sems.at[i]) for i, (a, b) in enumerate(pairs)]
     for copy in copies:
         copy.start()
-    for copy in copies[::-1]:
-        copy.wait()
+    copies[0].wait()
+    copies[1].wait()
     rest = jnp.zeros((SHARD - TRACKS - TRACKS // K, K), jnp.int32)
     shard[0:TRACKS, :] = coupling[...].astype(F32)
     shard[TRACKS:SHARD, :] = jnp.concatenate([assay[...], rest], axis=0).astype(F32)
+    leave = pltpu.make_async_copy(shard, shard_hbm, sems.at[len(pairs)])
+    leave.start()
+    for copy in copies[2:]:
+        copy.wait()
     keep, gain = gains(span[...])
     carry = masked(carry_ref[...], here[0] * ROWS, begin)
-    xs[...] = gain * x[...].astype(F32)
-    ds[...] = gain * d[...].astype(F32)
+    for j in range(CHUNKS):
+        at, to = pl.ds(j * STEPS, STEPS), pl.ds(j * PAD, STEPS)
+        xs[to, :] = gain * x[at, :].astype(F32)
+        ds[to, :] = gain * d[at, :].astype(F32)
     half = STEPS // 2
     ends = []
     for first in (0, half):
-        z, v = rows(xs, first, STEPS), rows(ds, first, STEPS)
+        z, v = rows(xs, first, PAD), rows(ds, first, PAD)
         m = column(carry, first) * keep
         for i in range(first + 1, first + half):
             decay = column(carry, i) * keep
-            z = decay * z + rows(xs, i, STEPS)
-            v = decay * v + rows(ds, i, STEPS)
+            z = decay * z + rows(xs, i, PAD)
+            v = decay * v + rows(ds, i, PAD)
             m = decay * m
         ends.append((m, z, v))
     (m0, z0, v0), (m1, z1, v1) = ends
@@ -101,13 +108,14 @@
         mj = m[j : j + 1]
         mt, zt, vt = mj * mt, mj * zt + z[j : j + 1], mj * vt + v[j : j + 1]
     sent[...] = jnp.broadcast_to(jnp.concatenate([mt, zt, vt], axis=0)[None], sent.shape)
+    leave.wait()
 
 
 def prepare_kernel(
-    here, zl, core, begin, span, carry_ref, x, d, chunk, shift, mine,
+    here, za, core, begin, span, carry_ref, x, d, chunk, shift, mine,
     latent, moved, product, shift_t, both, xs, ds,
 ):
-    at = core[0] * 4 + lax.rem(zl[0], 2) * 2
+    at = core[0] * 4 + za[0] * 2
     start = pl.multiple_of(at * STEPS, QUARTER)
     keep, gain = gains(span[...])
     pair = masked(carry_ref[pl.ds(at, 2), :], here[0] * ROWS + start, begin)
@@ -173,8 +181,8 @@
 
 
 def tracks_kernel(
-    here, zl, got, latent_ref, moved_ref, product_ref, shift_t, mine, other,
-    keep, send, sent, pulled, theirs,
+    here, got, latent_ref, moved_ref, product_ref, shift_t, mine, other,
+    pulled, sent, theirs,
 ):
     couple(other, theirs)
     ez = jnp.zeros((1, K), F32)
@@ -200,12 +208,9 @@
     pulled[...] = p
     total = jnp.sum(product * p, axis=0, keepdims=True)
     sent[...] = jnp.broadcast_to(total[None], sent.shape)
-    own = lax.div(zl[0], 2)
-    keep[...] = pulled[pl.ds(pl.multiple_of(own * STEPS, STEPS), STEPS), :]
-    send[...] = pulled[pl.ds(pl.multiple_of((1 - own) * STEPS, STEPS), STEPS), :]
-
-
-def later_kernel(here, zl, core, begin, span, carry_ref, got, weights, suffix, own_decay, decays):
+
+
+def later_kernel(here, za, core, begin, span, carry_ref, got, weights, suffix, own_decay, decays):
     w = jnp.ones((1, K), F32)
     for e in range(PEERS):
         later = e > here[0]
@@ -220,55 +225,62 @@
         suffix[to, :] = f
         decays[to, :] = decay
         f = decay * f
-    owned = core[0] * 4 + lax.rem(zl[0], 2) * 2 + lax.div(zl[0], 2)
-    owned = pl.multiple_of(owned * STEPS, STEPS)
-    own_decay[...] = decays[pl.ds(owned, STEPS), :]
-
-
-def sum_kernel(weights, late, own_decay, keep, got, out, p, a):
-    p[...] = keep[...] + got[...]
+    start = pl.multiple_of((core[0] * 4 + za[0] * 2) * STEPS, QUARTER)
+    own_decay[...] = decays[pl.ds(start, QUARTER), :]
+
+
+def sum_kernel(weights, late, own_decay, mine, other, out, p):
+    p[...] = mine[...] + other[...]
     r = jnp.zeros((CHUNKS, K), F32)
     m = jnp.ones((CHUNKS, K), F32)
-    for i in reversed(range(TINY)):
-        decay = rows(own_decay, i, TINY)
-        r = decay * (rows(p, i, TINY) + r)
+    for i in reversed(range(FINE)):
+        decay = rows(own_decay, i, FINE)
+        r = decay * (rows(p, i, FINE) + r)
         m = decay * m
     entries = [jnp.zeros((1, K), F32)]
     for j in reversed(range(CHUNKS)):
         entries.append(m[j : j + 1] * entries[-1] + r[j : j + 1])
     total = entries.pop()
     r = jnp.concatenate(entries[::-1], axis=0)
-    for i in reversed(range(TINY)):
-        adjoint = rows(p, i, TINY) + r
-        a[pl.ds(i, CHUNKS, stride=TINY), :] = adjoint
-        r = rows(own_decay, i, TINY) * adjoint
-    entry = jnp.sum(weights[...] * late[...], axis=0)
-    tail = jnp.concatenate([total, entry, jnp.zeros((PART - STEPS - 2, K), F32)], axis=0)
-    for j in range(4):
-        out[j, 0:STEPS, :] = a[...]
-        out[j, STEPS:PART, :] = tail
-
-
-def finish_kernel(span, d, chunk, suffix, parts, out):
+    for i in reversed(range(FINE)):
+        adjoint = rows(p, i, FINE) + r
+        out[pl.ds(i, CHUNKS, stride=FINE), :] = adjoint
+        r = rows(own_decay, i, FINE) * adjoint
+    late = late[...]
+    entry = jnp.sum(weights[...] * (late[:, 0:1, :] + late[:, 1:2, :]), axis=0)
+    out[QUARTER:PART, :] = jnp.concatenate(
+        [total, entry, jnp.zeros((PART - QUARTER - 2, K), F32)], axis=0
+    )
+
+
+def finish_kernel(za, span, d, chunk, suffix, mine, other, out):
     _, gain = gains(span[...])
-    entry = parts[0, STEPS + 1 : STEPS + 2, :]
-    for j in range(1, CHUNKS):
-        entry = entry + parts[j, STEPS + 1 : STEPS + 2, :]
-    for j in reversed(range(CHUNKS)):
-        at = pl.ds(j * STEPS, STEPS)
-        part = j // 4 * 4 + j % 2 * 2 + j // 2 % 2
-        adjoint = parts[part, 0:STEPS, :] + suffix[at, :] * entry
-        out[at, :] = gain * adjoint + d[at, :].astype(F32)
-        entry = chunk[0, j : j + 1, :] * entry + parts[part, STEPS : STEPS + 1, :]
+    tail = (mine[0, QUARTER:PART, :] + mine[1, QUARTER:PART, :]) + (
+        other[0, QUARTER:PART, :] + other[1, QUARTER:PART, :]
+    )
+    entry = tail[1:2]
+    for quarter in reversed(range(4)):
+        own = za[0] == quarter % 2
+
+        def part(at):
+            return jnp.where(own, mine[quarter // 2, at, :], other[quarter // 2, at, :])
+
+        for j in (1, 0):
+            at = pl.ds((quarter * 2 + j) * STEPS, STEPS)
+            entering = entry if j else chunk[0, quarter * 2 + 1 : quarter * 2 + 2, :] * entry
+            adjoint = part(pl.ds(j * STEPS, STEPS)) + suffix[at, :] * entering
+            out[at, :] = gain * adjoint + d[at, :].astype(F32)
+        entry = chunk[0, quarter * 2 : quarter * 2 + 1, :] * entering + part(pl.ds(QUARTER, 8))[0:1]
 
 
 def local(x, d, coupling, assay, shift, span, carry, begin):
     here = lax.axis_index(BINS)[None]
-    zl, core = lax.axis_index("zl")[None], lax.axis_index("core")[None]
+    za, core = lax.axis_index("za")[None], lax.axis_index("core")[None]
     span = span.reshape(1, K)
     carry = carry.reshape(CHUNKS, STEPS)
-    wide, quarter, tile = ((ROWS, K), F32), ((QUARTER, K), F32), ((STEPS, K), F32)
+    wide, quarter = ((ROWS, K), F32), ((QUARTER, K), F32)
     packed = ((3 * K, 2 * TRACKS), BF16)
+    pad = VMEM((CHUNKS * PAD, K), F32)
     chunk, sent, shard = call(
         ends_kernel,
         [SMEM] + [HBM] * 7,
@@ -281,48 +293,54 @@
             VMEM((TRACKS, K), BF16),
             VMEM((ROWS, K), BF16),
             VMEM((ROWS, K), BF16),
-            VMEM(*wide),
-            VMEM(*wide),
-            pltpu.SemaphoreType.DMA((7,)),
+            VMEM((SHARD, K), F32),
+            pad,
+            pad,
+            pltpu.SemaphoreType.DMA((8,)),
         ],
         vmem=60,
+        spaces=[VMEM, VMEM, HBM],
     )(here, begin, span, carry, assay.reshape(TRACKS // K, K), coupling, x, d)
     got = lax.all_to_all(sent, BINS, 0, 0, tiled=True)
 
+    swap = [(0, 1), (1, 0)]
     mine = lax.all_gather(shard, "core")
-    other = lax.ppermute(mine, "zl", [(i, i ^ 1) for i in range(4)])
+    other = lax.ppermute(mine, "za", swap)
     latent, moved, product, shift_t, both = call(
         prepare_kernel,
         [SMEM] * 4 + [VMEM] * 7,
         [quarter, quarter, quarter, ((QUARTER, K), BF16), packed],
         [VMEM(*quarter), VMEM(*quarter)],
-    )(here, zl, core, begin, span, carry, x, d, chunk, shift, mine)
-
-    keep, send, sent = call(
+    )(here, za, core, begin, span, carry, x, d, chunk, shift, mine)
+
+    pulled, sent = call(
         tracks_kernel,
-        [SMEM] * 2 + [VMEM] * 7,
-        [tile] * 2 + [((PEERS, 1, K), F32)],
-        [VMEM(*quarter), VMEM(*packed)],
-    )(here, zl, got, latent, moved, product, shift_t, both, other)
-    late = lax.all_to_all(sent, BINS, 0, 0, tiled=True)
-    received = lax.ppermute(send, "zl", [(i, i ^ 2) for i in range(4)])
+        [SMEM] + [VMEM] * 7,
+        [quarter, ((2 * PEERS, 1, K), F32)],
+        [VMEM(*packed)],
+    )(here, got, latent, moved, product, shift_t, both, other)
+    late = lax.all_to_all(sent, BINS + ("zb",), 0, 0, tiled=True)
+    received = lax.ppermute(pulled, "zb", swap)
     weights, suffix, own_decay = call(
         later_kernel,
         [SMEM] * 4 + [VMEM] * 3,
-        [((PEERS, 1, K), F32), wide, tile],
+        [((PEERS, 1, K), F32), wide, quarter],
         [VMEM(*wide)],
-    )(here, zl, core, begin, span, carry, got)
-    (mine,) = call(sum_kernel, [VMEM] * 5, [((4, PART, K), F32)], [VMEM(*tile)] * 2)(
-        weights, late, own_decay, keep, received
-    )
-    column_parts = lax.all_to_all(mine, "zl", 0, 0, tiled=True)
-    parts = lax.all_gather(column_parts, "core").reshape(CHUNKS, PART, K)
-    (out,) = call(finish_kernel, [VMEM] * 5, [wide])(span, d, chunk, suffix, parts)
+    )(here, za, core, begin, span, carry, got)
+    (part,) = call(sum_kernel, [VMEM] * 5, [((PART, K), F32)], [VMEM(*quarter)])(
+        weights, late.reshape(PEERS, 2, K), own_decay, pulled, received
+    )
+    other = lax.ppermute(part, "za", swap)
+    mine = lax.all_gather(part, "core")
+    other = lax.all_gather(other, "core")
+    (out,) = call(finish_kernel, [SMEM] + [VMEM] * 6, [wide])(
+        za, span, d, chunk, suffix, mine, other
+    )
     return out
 
 
 def solution(mesh):
-    fine = Mesh(mesh.devices.reshape(8, 2, 4, 4, 2), ("y", "zh", "x", "zl", "core"))
+    fine = Mesh(mesh.devices.reshape(8, 2, 4, 2, 2, 2), ("y", "zh", "x", "zb", "za", "core"))
     in_specs = (
         P(BINS, None),
         P(BINS, None),

time: 83 us -> 81.1 us (0.977)
  blocking collectives: 24.5 us -> 19 us
  starting transfers between devices: 25.2 us -> 28.9 us
    all_to_all x1 -> x0, blocking collectives: 8.93 us -> none  [local(): column_parts = lax.all_to_all(mine, 'zl', 0, 0, tiled=True)]
    all_gather x1 -> x2, blocking collectives: 6.49 us -> 9.88 us  [the longest x1 5.46 us: local(): mine = lax.all_gather(part, 'core')]
    ppermute x2 -> x3, starting transfers between devices: 6.04 us -> 8.2 us  [the longest x1 4 us: local(): received = lax.ppermute(pulled, 'zb', swap)]
    all_to_all x1, starting transfers between devices: 4.6 us -> 6.16 us  [local(): late = lax.all_to_all(sent, BINS + ('zb',), 0, 0, tiled=True)]
  transfers between devices with their start and end apart: 4 -> 5, of which waited for: 2 -> 2; matrix products, arithmetic and copies ran while one was open for 0% -> 0% of each run, Pallas kernels for 3% -> 3%
where the time goes in v5:
time: 81.1 us; the launch traced here: 80.7 us
  starting transfers between devices  28.9 us (36%)
  waiting for transfers between devices  23.1 us (28%)
  blocking collectives  19 us (23%)
  Pallas kernels  8.9 us (11%)
    all_to_all x1, starting transfers between devices, local(): got = lax.all_to_all(sent, BINS, 0, 0, tiled=True)  14.6 us
    all_to_all x1, waiting for transfers between devices, local(): got = lax.all_to_all(sent, BINS, 0, 0, tiled=True)  11.6 us
    all_to_all x1, waiting for transfers between devices, local(): late = lax.all_to_all(sent, BINS + ('zb',), 0, 0, tiled=True)  11.5 us
    all_gather x1, blocking collectives, local(): mine = lax.all_gather(shard, 'core')  9.13 us
    all_to_all x1, starting transfers between devices, local(): late = lax.all_to_all(sent, BINS + ('zb',), 0, 0, tiled=True)  6.16 us
    all_gather x1, blocking collectives, local(): mine = lax.all_gather(part, 'core')  5.46 us
    all_gather x1, blocking collectives, local(): other = lax.all_gather(other, 'core')  4.42 us
    ppermute x1, starting transfers between devices, local(): received = lax.ppermute(pulled, 'zb', swap)  4 us
  transfers between devices with their start and end apart: 5, of which 2 were waited for; matrix products, arithmetic and copies ran while one was open for 0% of the time, Pallas kernels for 3%

profile of v5, /device:TPU:1, one launch (start us, length us, event | category | flops | bytes accessed | tf_op | source)
XLA Modules:
  0.0 80.7 jit_solution(16504465647198441242)
XLA Ops:
  0.0 2.4 %shard_map.82 = (f32[3,8,128]{2,1,0:T(8,128)}, f32[64,3,128]{2,1,0:T(4,128)}, f32[648,128]{1,0:T(8,128)}) custom-call(s32[1]{0:T(128)} %bitcast.2.here, s32[3]{0:T(128)} %begin.3, f32[1,128]{1,0:T(1,128)} %bitcast.18, f32[8,128]{1,0:T(8,128)} %bitcast.15, s32[5,128]{1,0:T(8,128)} %bitcast.22, bf16[640,128]{1,0:T(8,128)(2,1)} %coupling_hbm.1, ...), custom_call_target="tpu_custom_call" | custom-call | tf_op jit(solution)/shard_map/pallas_call | solution.py:284
  2.4 0.0 copy-start.1
  2.4 0.0 copy-start.4
  2.4 9.1 %all-gather = f32[1296,128]{1,0:T(8,128)S(1)} all-gather(f32[648,128]{1,0:T(8,128)} %get-tuple-element.22), channel_id=2, replica_groups=mesh['y'=8,'zh'=2,'x'=4,'zb'=2,'za'=2,'core'=2] {'core'}, dimensions={0}, use_global_device_ids=true | all-gather | bytes 995328 | tf_op jit(solution)/shard_map/all_gather | solution.py:307
  11.6 0.0 copy-start
  11.6 2.0 %collective-permute-start = (f32[2,648,128]{2,1,0:T(8,128)S(1)}, f32[2,648,128]{2,1,0:T(8,128)S(1)}, u32[]{:S(2)}, u32[]{:S(2)}) collective-permute-start(f32[2,648,128]{2,1,0:T(8,128)S(1)} %bitcast.10), channel_id=1, source_target_pairs={{0,2},{2,0},{1,3},{3,1},{4,6},{6,4},{5,7},{7,5},{8,10},{10,8},{9,1... | collective-permute-start | bytes 1990664 | tf_op jit(solution)/shard_map/ppermute | solution.py:308
  13.6 0.0 copy-start.3
  13.6 14.6 %all-to-all-start = ((f32[64,3,128]{2,1,0:T(4,128)}), f32[64,3,128]{2,1,0:T(4,128)S(1)}, u32[]{:S(2)}, u32[]{:S(2)}) async-start(f32[64,3,128]{2,1,0:T(4,128)} %get-tuple-element.19), calls=%async_computation | async-start | bytes 262144 | tf_op jit(solution)/shard_map/all_to_all | solution.py:304
  28.2 0.0 copy-start.2
  28.2 0.0 copy-start.5
  28.2 0.0 copy-start.6
  28.2 0.0 copy-done.1
  28.2 0.0 copy-done.4
  28.3 0.0 copy-done
  28.3 0.0 copy-done.3
  28.3 0.6 copy-done.2
  28.9 0.0 copy-done.5
  28.9 0.0 copy-done.6
  28.9 1.4 %shard_map.84 = (f32[256,128]{1,0:T(8,128)S(1)}, f32[256,128]{1,0:T(8,128)S(1)}, f32[256,128]{1,0:T(8,128)S(1)}, bf16[256,128]{1,0:T(8,128)(2,1)S(1)}, bf16[384,1280]{1,0:T(8,128)(2,1)S(1)}) custom-call(s32[1]{0:T(128)} %bitcast.2.here, s32[1]{0:T(128)} %bitcast.za, s32[1]{0:T(128)} %bitcast.5.core, s32[3]{0:T(128)S(1)} %copy-done.6, f32[1,128]{1,0:T(1,128)S(1)} %bitcast.19, ...), custom_call_target="tpu_custom_call" | custom-call | tf_op jit(solution)/shard_map/pallas_call | solution.py:309
  30.3 11.6 %all-to-all-done.got = f32[64,3,128]{2,1,0:T(4,128)S(1)} async-done(((f32[64,3,128]{2,1,0:T(4,128)}), f32[64,3,128]{2,1,0:T(4,128)S(1)}, u32[]{:S(2)}, u32[]{:S(2)}) %all-to-all-start) | async-done | bytes 98336 | tf_op jit(solution)/shard_map/all_to_all | solution.py:304
  41.9 0.0 collective-permute-done.other
  41.9 2.3 %shard_map.85 = (f32[256,128]{1,0:T(8,128)S(1)}, f32[128,1,128]{2,1,0:T(1,128)}) custom-call(s32[1]{0:T(128)} %bitcast.2.here, f32[64,3,128]{2,1,0:T(4,128)S(1)} %all-to-all-done.got, f32[256,128]{1,0:T(8,128)S(1)} %get-tuple-element.23.latent_ref, f32[256,128]{1,0:T(8,128)S(1)} %get-tuple-element.24.moved_ref, ...), custom_call_target="tpu_custom_call" | custom-call | tf_op jit(solution)/shard_map/pallas_call | solution.py:316
  44.2 4.0 %collective-permute-start.1 = (f32[256,128]{1,0:T(8,128)S(1)}, f32[256,128]{1,0:T(8,128)S(1)}, u32[]{:S(2)}, u32[]{:S(2)}) collective-permute-start(f32[256,128]{1,0:T(8,128)S(1)} %get-tuple-element.30.mine), channel_id=1, source_target_pairs={{0,4},{4,0},{1,5},{5,1},{2,6},{6,2},{3,7},{7,3},{8,12},{12,8},{9,1... | collective-permute-start | bytes 393224 | tf_op jit(solution)/shard_map/ppermute | solution.py:323
  48.2 6.2 %all-to-all-start.1 = ((f32[128,1,128]{2,1,0:T(1,128)}), f32[128,1,128]{2,1,0:T(1,128)S(1)}, u32[]{:S(2)}, u32[]{:S(2)}) async-start(f32[128,1,128]{2,1,0:T(1,128)} %get-tuple-element.28), calls=%async_computation.1 | async-start | bytes 131072 | tf_op jit(solution)/shard_map/all_to_all | solution.py:322
  54.3 1.5 %shard_map.83 = (f32[64,1,128]{2,1,0:T(1,128)S(1)}, f32[1024,128]{1,0:T(8,128)S(1)}, f32[256,128]{1,0:T(8,128)S(1)}) custom-call(s32[1]{0:T(128)} %bitcast.2.here, s32[1]{0:T(128)} %bitcast.za, s32[1]{0:T(128)} %bitcast.5.core, s32[3]{0:T(128)S(1)} %copy-done.6, f32[1,128]{1,0:T(1,128)S(1)} %bitcast.20, f32[8,128]{1,0:T(8,128)S(1)} %bitcast.17, ...), custom_call_target="tpu_custom_call" | custom-call | tf_op jit(solution)/shard_map/pallas_call | solution.py:324
  55.8 11.5 %all-to-all-done.1 = f32[128,1,128]{2,1,0:T(1,128)S(1)} async-done(((f32[128,1,128]{2,1,0:T(1,128)}), f32[128,1,128]{2,1,0:T(1,128)S(1)}, u32[]{:S(2)}, u32[]{:S(2)}) %all-to-all-start.1) | async-done | bytes 65568 | tf_op jit(solution)/shard_map/all_to_all | solution.py:322
  67.3 0.0 collective-permute-done.1.other
  67.3 0.4 shard_map.86
  67.7 2.2 %collective-permute-start.2 = (f32[264,128]{1,0:T(8,128)S(1)}, f32[264,128]{1,0:T(8,128)S(1)}, u32[]{:S(2)}, u32[]{:S(2)}) collective-permute-start(f32[264,128]{1,0:T(8,128)S(1)} %shard_map.86), channel_id=1, source_target_pairs={{0,2},{2,0},{1,3},{3,1},{4,6},{6,4},{5,7},{7,5},{8,10},{10,8},{9,1... | collective-permute-start | bytes 405512 | tf_op jit(solution)/shard_map/ppermute | solution.py:333
  69.9 5.5 %all-gather.1 = f32[528,128]{1,0:T(8,128)S(1)} all-gather(f32[264,128]{1,0:T(8,128)S(1)} %shard_map.86), channel_id=3, replica_groups=mesh['y'=8,'zh'=2,'x'=4,'zb'=2,'za'=2,'core'=2] {'core'}, dimensions={0}, use_global_device_ids=true | all-gather | bytes 405504 | tf_op jit(solution)/shard_map/all_gather | solution.py:334
  75.3 0.0 collective-permute-done.2
  75.3 4.4 %all-gather.2 = f32[528,128]{1,0:T(8,128)S(1)} all-gather(f32[264,128]{1,0:T(8,128)S(1)} %collective-permute-done.2), channel_id=4, replica_groups=mesh['y'=8,'zh'=2,'x'=4,'zb'=2,'za'=2,'core'=2] {'core'}, dimensions={0}, use_global_device_ids=true | all-gather | bytes 405504 | tf_op jit(solution)/shard_map/all_gather | solution.py:335
  79.8 0.9 %shard_map.87 = f32[1024,128]{1,0:T(8,128)} custom-call(s32[1]{0:T(128)} %bitcast.za, f32[1,128]{1,0:T(1,128)S(1)} %bitcast.21, bf16[1024,128]{1,0:T(8,128)(2,1)S(1)} %copy-done, f32[3,8,128]{2,1,0:T(8,128)S(1)} %copy-done.2, f32[1024,128]{1,0:T(8,128)S(1)} %get-tuple-element.20.suffix, f32[2,264,128]{2,1,0:T(8,128)S(1)} %bitcast.12, f32[2,264,128]{2,1,0:T(8,128)S(1)} %bitcast.13), custom_call_target="tpu_custom_call" | custom-call | tf_op jit(solution)/shard_map/pallas_call | solution.py:336
Async XLA Ops:
  2.4 25.8 %copy-start.1 = (bf16[1024,128]{1,0:T(8,128)(2,1)S(1)}, bf16[1024,128]{1,0:T(8,128)(2,1)}, u32[]{:S(2)}) copy-start(bf16[1024,128]{1,0:T(8,128)(2,1)} %x.1) | copy-start | bytes 786436
  2.4 25.8 %copy-start.4 = (f32[8,1024]{1,0:T(8,128)S(1)}, f32[8,1024]{1,0:T(8,128)}, u32[]{:S(2)}) copy-start(f32[8,1024]{1,0:T(8,128)} %shift.1) | copy-start | bytes 98308
  11.6 16.7 %copy-start = (bf16[1024,128]{1,0:T(8,128)(2,1)S(1)}, bf16[1024,128]{1,0:T(8,128)(2,1)}, u32[]{:S(2)}) copy-start(bf16[1024,128]{1,0:T(8,128)(2,1)} %d.3) | copy-start | bytes 786436
  11.6 30.3 %collective-permute-start = (f32[2,648,128]{2,1,0:T(8,128)S(1)}, f32[2,648,128]{2,1,0:T(8,128)S(1)}, u32[]{:S(2)}, u32[]{:S(2)}) collective-permute-start(f32[2,648,128]{2,1,0:T(8,128)S(1)} %bitcast.10), channel_id=1, source_target_pairs={{0,2},{2,0},{1,3},{3,1},{4,6},{6,4},{5,7},{7,5},{8,10},{10,8},{9,1... | collective-permute-start | bytes 1990664 | tf_op jit(solution)/shard_map/ppermute | solution.py:308
  13.6 14.6 %copy-start.3 = (f32[1024]{0:T(1024)S(1)}, f32[1024]{0:T(1024)}, u32[]{:S(2)}) copy-start(f32[1024]{0:T(1024)} %param.14) | copy-start | bytes 12292
  13.6 28.2 %all-to-all-start = ((f32[64,3,128]{2,1,0:T(4,128)}), f32[64,3,128]{2,1,0:T(4,128)S(1)}, u32[]{:S(2)}, u32[]{:S(2)}) async-start(f32[64,3,128]{2,1,0:T(4,128)} %get-tuple-element.19), calls=%async_computation | async-start | bytes 262144 | tf_op jit(solution)/shard_map/all_to_all | solution.py:304
  28.2 0.7 copy-start.2
  28.2 0.7 copy-start.5
  28.2 0.7 copy-start.6
  44.2 23.1 %collective-permute-start.1 = (f32[256,128]{1,0:T(8,128)S(1)}, f32[256,128]{1,0:T(8,128)S(1)}, u32[]{:S(2)}, u32[]{:S(2)}) collective-permute-start(f32[256,128]{1,0:T(8,128)S(1)} %get-tuple-element.30.mine), channel_id=1, source_target_pairs={{0,4},{4,0},{1,5},{5,1},{2,6},{6,2},{3,7},{7,3},{8,12},{12,8},{9,1... | collective-permute-start | bytes 393224 | tf_op jit(solution)/shard_map/ppermute | solution.py:323
  48.2 19.1 %all-to-all-start.1 = ((f32[128,1,128]{2,1,0:T(1,128)}), f32[128,1,128]{2,1,0:T(1,128)S(1)}, u32[]{:S(2)}, u32[]{:S(2)}) async-start(f32[128,1,128]{2,1,0:T(1,128)} %get-tuple-element.28), calls=%async_computation.1 | async-start | bytes 131072 | tf_op jit(solution)/shard_map/all_to_all | solution.py:322
  67.7 7.6 %collective-permute-start.2 = (f32[264,128]{1,0:T(8,128)S(1)}, f32[264,128]{1,0:T(8,128)S(1)}, u32[]{:S(2)}, u32[]{:S(2)}) collective-permute-start(f32[264,128]{1,0:T(8,128)S(1)} %shard_map.86), channel_id=1, source_target_pairs={{0,2},{2,0},{1,3},{3,1},{4,6},{6,4},{5,7},{7,5},{8,10},{10,8},{9,1... | collective-permute-start | bytes 405512 | tf_op jit(solution)/shard_map/ppermute | solution.py:333

commit v6 on v5

--- a/solution.py
+++ b/solution.py
@@ -11,7 +11,9 @@
 FINE = 32
 PAD = STEPS + 8
 PART = QUARTER + 8
-BINS, VIEW = ("y", "zh", "x"), ("zb", "za", "core")
+BINS, VIEW = "bins", ("zb", "za", "core")
+FIRST = 38
+ORDER = [(FIRST + i) % PEERS for i in range(PEERS)]
 VMEM, SMEM, HBM = pltpu.VMEM, pltpu.SMEM, pltpu.HBM
 F32, BF16 = jnp.float32, jnp.bfloat16
 
@@ -188,7 +190,8 @@
     ez = jnp.zeros((1, K), F32)
     ev = jnp.zeros((1, K), F32)
     for e in range(PEERS - 1):
-        m, z, v = got[e, 0:1, :], got[e, 1:2, :], got[e, 2:3, :]
+        at = (e - FIRST) % PEERS
+        m, z, v = got[at, 0:1, :], got[at, 1:2, :], got[at, 2:3, :]
         earlier = e < here[0]
         ez = jnp.where(earlier, m * ez + z, ez)
         ev = jnp.where(earlier, m * ev + v, ev)
@@ -215,7 +218,7 @@
     for e in range(PEERS):
         later = e > here[0]
         weights[e] = jnp.where(later, w, 0.0)
-        w = jnp.where(later, w * got[e, 0:1, :], w)
+        w = jnp.where(later, w * got[(e - FIRST) % PEERS, 0:1, :], w)
     keep, _ = gains(span[...])
     carry = masked(carry_ref[...], here[0] * ROWS, begin)
     f = jnp.ones((CHUNKS, K), F32)
@@ -301,7 +304,7 @@
         vmem=60,
         spaces=[VMEM, VMEM, HBM],
     )(here, begin, span, carry, assay.reshape(TRACKS // K, K), coupling, x, d)
-    got = lax.all_to_all(sent, BINS, 0, 0, tiled=True)
+    got = lax.all_to_all(sent, BINS, 0, 0, axis_index_groups=[ORDER], tiled=True)
 
     swap = [(0, 1), (1, 0)]
     mine = lax.all_gather(shard, "core")
@@ -319,7 +322,7 @@
         [quarter, ((2 * PEERS, 1, K), F32)],
         [VMEM(*packed)],
     )(here, got, latent, moved, product, shift_t, both, other)
-    late = lax.all_to_all(sent, BINS + ("zb",), 0, 0, tiled=True)
+    late = lax.all_to_all(sent, (BINS, "zb"), 0, 0, tiled=True)
     received = lax.ppermute(pulled, "zb", swap)
     weights, suffix, own_decay = call(
         later_kernel,
@@ -340,7 +343,7 @@
 
 
 def solution(mesh):
-    fine = Mesh(mesh.devices.reshape(8, 2, 4, 2, 2, 2), ("y", "zh", "x", "zb", "za", "core"))
+    fine = Mesh(mesh.devices.reshape(PEERS, 2, 2, 2), (BINS, *VIEW))
     in_specs = (
         P(BINS, None),
         P(BINS, None),

time: 81.1 us -> 80.8 us (level)
  waiting for transfers between devices: 23.1 us -> 15.7 us
  starting transfers between devices: 28.9 us -> 36 us
    all_to_all x2, waiting for transfers between devices: 23 us -> 15.7 us  [the longest x1 11.5 us: local(): late = lax.all_to_all(sent, (BINS, 'zb'), 0, 0, tiled=True)]
    all_to_all x2, starting transfers between devices: 20.7 us -> 26.5 us  [the longest x1 16.5 us: local(): lax.all_to_all(sent, BINS, 0, 0, axis_index_groups=[ORDER], tiled=True)]
    ppermute x1, starting transfers between devices: 4 us -> 5.12 us  [local(): received = lax.ppermute(pulled, 'zb', swap)]
  transfers between devices with their start and end apart: 5 -> 5, of which waited for: 2 -> 2; matrix products, arithmetic and copies ran while one was open for 0% -> 0% of each run, Pallas kernels for 3% -> 4%
where the time goes in v6:
time: 80.8 us; the launch traced here: 80.4 us
  starting transfers between devices  36 us (45%)
  blocking collectives  19 us (24%)
  waiting for transfers between devices  15.7 us (19%)
  Pallas kernels  8.89 us (11%)
    all_to_all x1, starting transfers between devices, local(): lax.all_to_all(sent, BINS, 0, 0, axis_index_groups=[ORDER], tiled=True)  16.5 us
    all_to_all x1, waiting for transfers between devices, local(): late = lax.all_to_all(sent, (BINS, 'zb'), 0, 0, tiled=True)  11.5 us
    all_to_all x1, starting transfers between devices, local(): late = lax.all_to_all(sent, (BINS, 'zb'), 0, 0, tiled=True)  10 us
    all_gather x1, blocking collectives, local(): mine = lax.all_gather(shard, 'core')  9.13 us
    all_gather x1, blocking collectives, local(): mine = lax.all_gather(part, 'core')  5.46 us
    ppermute x1, starting transfers between devices, local(): received = lax.ppermute(pulled, 'zb', swap)  5.12 us
    all_gather x1, blocking collectives, local(): other = lax.all_gather(other, 'core')  4.42 us
    all_to_all x1, waiting for transfers between devices, local(): lax.all_to_all(sent, BINS, 0, 0, axis_index_groups=[ORDER], tiled=True)  4.21 us
  transfers between devices with their start and end apart: 5, of which 2 were waited for; matrix products, arithmetic and copies ran while one was open for 0% of the time, Pallas kernels for 4%

profile of v6, /device:TPU:1, one launch (start us, length us, event | category | flops | bytes accessed | tf_op | source)
XLA Modules:
  0.0 80.4 jit_solution(11528396180959941349)
XLA Ops:
  0.0 2.4 %shard_map.82 = (f32[3,8,128]{2,1,0:T(8,128)}, f32[64,3,128]{2,1,0:T(4,128)}, f32[648,128]{1,0:T(8,128)}) custom-call(s32[1]{0:T(128)} %bitcast.2.here, s32[3]{0:T(128)} %begin.3, f32[1,128]{1,0:T(1,128)} %bitcast.18, f32[8,128]{1,0:T(8,128)} %bitcast.15, s32[5,128]{1,0:T(8,128)} %bitcast.22, bf16[640,128]{1,0:T(8,128)(2,1)} %coupling_hbm.1, ...), custom_call_target="tpu_custom_call" | custom-call | tf_op jit(solution)/shard_map/pallas_call | solution.py:287
  2.4 0.0 copy-start.1
  2.4 0.0 copy-start.4
  2.4 9.1 %all-gather = f32[1296,128]{1,0:T(8,128)S(1)} all-gather(f32[648,128]{1,0:T(8,128)} %get-tuple-element.22), channel_id=2, replica_groups=mesh['bins'=64,'zb'=2,'za'=2,'core'=2] {'core'}, dimensions={0}, use_global_device_ids=true | all-gather | bytes 995328 | tf_op jit(solution)/shard_map/all_gather | solution.py:310
  11.6 0.0 copy-start
  11.6 2.0 %collective-permute-start = (f32[2,648,128]{2,1,0:T(8,128)S(1)}, f32[2,648,128]{2,1,0:T(8,128)S(1)}, u32[]{:S(2)}, u32[]{:S(2)}) collective-permute-start(f32[2,648,128]{2,1,0:T(8,128)S(1)} %bitcast.10), channel_id=1, source_target_pairs={{0,2},{2,0},{1,3},{3,1},{4,6},{6,4},{5,7},{7,5},{8,10},{10,8},{9,1... | collective-permute-start | bytes 1990664 | tf_op jit(solution)/shard_map/ppermute | solution.py:311
  13.6 0.0 copy-start.3
  13.6 16.5 %all-to-all-start = ((f32[64,3,128]{2,1,0:T(4,128)}), f32[64,3,128]{2,1,0:T(4,128)S(1)}, u32[]{:S(2)}, u32[]{:S(2)}) async-start(f32[64,3,128]{2,1,0:T(4,128)} %get-tuple-element.19), calls=%async_computation | async-start | bytes 262144 | tf_op jit(solution)/shard_map/all_to_all | solution.py:307
  30.1 0.0 copy-start.2
  30.1 0.0 copy-start.5
  30.2 0.0 copy-start.6
  30.2 0.0 copy-done.1
  30.2 0.0 copy-done.4
  30.2 0.0 copy-done
  30.2 0.0 copy-done.3
  30.2 0.6 copy-done.2
  30.8 0.0 copy-done.5
  30.8 0.0 copy-done.6
  30.8 1.4 %shard_map.84 = (f32[256,128]{1,0:T(8,128)S(1)}, f32[256,128]{1,0:T(8,128)S(1)}, f32[256,128]{1,0:T(8,128)S(1)}, bf16[256,128]{1,0:T(8,128)(2,1)S(1)}, bf16[384,1280]{1,0:T(8,128)(2,1)S(1)}) custom-call(s32[1]{0:T(128)} %bitcast.2.here, s32[1]{0:T(128)} %bitcast.za, s32[1]{0:T(128)} %bitcast.5.core, s32[3]{0:T(128)S(1)} %copy-done.6, f32[1,128]{1,0:T(1,128)S(1)} %bitcast.19, ...), custom_call_target="tpu_custom_call" | custom-call | tf_op jit(solution)/shard_map/pallas_call | solution.py:312
  32.2 4.2 %all-to-all-done.got = f32[64,3,128]{2,1,0:T(4,128)S(1)} async-done(((f32[64,3,128]{2,1,0:T(4,128)}), f32[64,3,128]{2,1,0:T(4,128)S(1)}, u32[]{:S(2)}, u32[]{:S(2)}) %all-to-all-start) | async-done | bytes 98336 | tf_op jit(solution)/shard_map/all_to_all | solution.py:307
  36.4 0.0 collective-permute-done.other
  36.4 2.3 %shard_map.85 = (f32[256,128]{1,0:T(8,128)S(1)}, f32[128,1,128]{2,1,0:T(1,128)}) custom-call(s32[1]{0:T(128)} %bitcast.2.here, f32[64,3,128]{2,1,0:T(4,128)S(1)} %all-to-all-done.got, f32[256,128]{1,0:T(8,128)S(1)} %get-tuple-element.23.latent_ref, f32[256,128]{1,0:T(8,128)S(1)} %get-tuple-element.24.moved_ref, ...), custom_call_target="tpu_custom_call" | custom-call | tf_op jit(solution)/shard_map/pallas_call | solution.py:319
  38.7 5.1 %collective-permute-start.1 = (f32[256,128]{1,0:T(8,128)S(1)}, f32[256,128]{1,0:T(8,128)S(1)}, u32[]{:S(2)}, u32[]{:S(2)}) collective-permute-start(f32[256,128]{1,0:T(8,128)S(1)} %get-tuple-element.30.mine), channel_id=1, source_target_pairs={{0,4},{4,0},{1,5},{5,1},{2,6},{6,2},{3,7},{7,3},{8,12},{12,8},{9,1... | collective-permute-start | bytes 393224 | tf_op jit(solution)/shard_map/ppermute | solution.py:326
  43.8 10.0 %all-to-all-start.1 = ((f32[128,1,128]{2,1,0:T(1,128)}), f32[128,1,128]{2,1,0:T(1,128)S(1)}, u32[]{:S(2)}, u32[]{:S(2)}) async-start(f32[128,1,128]{2,1,0:T(1,128)} %get-tuple-element.28), calls=%async_computation.1 | async-start | bytes 131072 | tf_op jit(solution)/shard_map/all_to_all | solution.py:325
  53.9 1.5 %shard_map.83 = (f32[64,1,128]{2,1,0:T(1,128)S(1)}, f32[1024,128]{1,0:T(8,128)S(1)}, f32[256,128]{1,0:T(8,128)S(1)}) custom-call(s32[1]{0:T(128)} %bitcast.2.here, s32[1]{0:T(128)} %bitcast.za, s32[1]{0:T(128)} %bitcast.5.core, s32[3]{0:T(128)S(1)} %copy-done.6, f32[1,128]{1,0:T(1,128)S(1)} %bitcast.20, f32[8,128]{1,0:T(8,128)S(1)} %bitcast.17, ...), custom_call_target="tpu_custom_call" | custom-call | tf_op jit(solution)/shard_map/pallas_call | solution.py:327
  55.3 11.5 %all-to-all-done.1 = f32[128,1,128]{2,1,0:T(1,128)S(1)} async-done(((f32[128,1,128]{2,1,0:T(1,128)}), f32[128,1,128]{2,1,0:T(1,128)S(1)}, u32[]{:S(2)}, u32[]{:S(2)}) %all-to-all-start.1) | async-done | bytes 65568 | tf_op jit(solution)/shard_map/all_to_all | solution.py:325
  66.8 0.0 collective-permute-done.1.other
  66.8 0.4 shard_map.86
  67.2 2.3 %collective-permute-start.2 = (f32[264,128]{1,0:T(8,128)S(1)}, f32[264,128]{1,0:T(8,128)S(1)}, u32[]{:S(2)}, u32[]{:S(2)}) collective-permute-start(f32[264,128]{1,0:T(8,128)S(1)} %shard_map.86), channel_id=1, source_target_pairs={{0,2},{2,0},{1,3},{3,1},{4,6},{6,4},{5,7},{7,5},{8,10},{10,8},{9,1... | collective-permute-start | bytes 405512 | tf_op jit(solution)/shard_map/ppermute | solution.py:336
  69.5 5.5 %all-gather.1 = f32[528,128]{1,0:T(8,128)S(1)} all-gather(f32[264,128]{1,0:T(8,128)S(1)} %shard_map.86), channel_id=3, replica_groups=mesh['bins'=64,'zb'=2,'za'=2,'core'=2] {'core'}, dimensions={0}, use_global_device_ids=true | all-gather | bytes 405504 | tf_op jit(solution)/shard_map/all_gather | solution.py:337
  75.0 0.0 collective-permute-done.2
  75.0 4.4 %all-gather.2 = f32[528,128]{1,0:T(8,128)S(1)} all-gather(f32[264,128]{1,0:T(8,128)S(1)} %collective-permute-done.2), channel_id=4, replica_groups=mesh['bins'=64,'zb'=2,'za'=2,'core'=2] {'core'}, dimensions={0}, use_global_device_ids=true | all-gather | bytes 405504 | tf_op jit(solution)/shard_map/all_gather | solution.py:338
  79.4 0.9 %shard_map.87 = f32[1024,128]{1,0:T(8,128)} custom-call(s32[1]{0:T(128)} %bitcast.za, f32[1,128]{1,0:T(1,128)S(1)} %bitcast.21, bf16[1024,128]{1,0:T(8,128)(2,1)S(1)} %copy-done, f32[3,8,128]{2,1,0:T(8,128)S(1)} %copy-done.2, f32[1024,128]{1,0:T(8,128)S(1)} %get-tuple-element.20.suffix, f32[2,264,128]{2,1,0:T(8,128)S(1)} %bitcast.12, f32[2,264,128]{2,1,0:T(8,128)S(1)} %bitcast.13), custom_call_target="tpu_custom_call" | custom-call | tf_op jit(solution)/shard_map/pallas_call | solution.py:339
Async XLA Ops:
  2.4 27.8 %copy-start.1 = (bf16[1024,128]{1,0:T(8,128)(2,1)S(1)}, bf16[1024,128]{1,0:T(8,128)(2,1)}, u32[]{:S(2)}) copy-start(bf16[1024,128]{1,0:T(8,128)(2,1)} %x.1) | copy-start | bytes 786436
  2.4 27.8 %copy-start.4 = (f32[8,1024]{1,0:T(8,128)S(1)}, f32[8,1024]{1,0:T(8,128)}, u32[]{:S(2)}) copy-start(f32[8,1024]{1,0:T(8,128)} %shift.1) | copy-start | bytes 98308
  11.6 18.6 %copy-start = (bf16[1024,128]{1,0:T(8,128)(2,1)S(1)}, bf16[1024,128]{1,0:T(8,128)(2,1)}, u32[]{:S(2)}) copy-start(bf16[1024,128]{1,0:T(8,128)(2,1)} %d.3) | copy-start | bytes 786436
  11.6 24.8 %collective-permute-start = (f32[2,648,128]{2,1,0:T(8,128)S(1)}, f32[2,648,128]{2,1,0:T(8,128)S(1)}, u32[]{:S(2)}, u32[]{:S(2)}) collective-permute-start(f32[2,648,128]{2,1,0:T(8,128)S(1)} %bitcast.10), channel_id=1, source_target_pairs={{0,2},{2,0},{1,3},{3,1},{4,6},{6,4},{5,7},{7,5},{8,10},{10,8},{9,1... | collective-permute-start | bytes 1990664 | tf_op jit(solution)/shard_map/ppermute | solution.py:311
  13.6 16.6 %copy-start.3 = (f32[1024]{0:T(1024)S(1)}, f32[1024]{0:T(1024)}, u32[]{:S(2)}) copy-start(f32[1024]{0:T(1024)} %param.14) | copy-start | bytes 12292
  13.6 22.8 %all-to-all-start = ((f32[64,3,128]{2,1,0:T(4,128)}), f32[64,3,128]{2,1,0:T(4,128)S(1)}, u32[]{:S(2)}, u32[]{:S(2)}) async-start(f32[64,3,128]{2,1,0:T(4,128)} %get-tuple-element.19), calls=%async_computation | async-start | bytes 262144 | tf_op jit(solution)/shard_map/all_to_all | solution.py:307
  30.1 0.7 copy-start.2
  30.1 0.7 copy-start.5
  30.2 0.7 copy-start.6
  38.7 28.1 %collective-permute-start.1 = (f32[256,128]{1,0:T(8,128)S(1)}, f32[256,128]{1,0:T(8,128)S(1)}, u32[]{:S(2)}, u32[]{:S(2)}) collective-permute-start(f32[256,128]{1,0:T(8,128)S(1)} %get-tuple-element.30.mine), channel_id=1, source_target_pairs={{0,4},{4,0},{1,5},{5,1},{2,6},{6,2},{3,7},{7,3},{8,12},{12,8},{9,1... | collective-permute-start | bytes 393224 | tf_op jit(solution)/shard_map/ppermute | solution.py:326
  43.8 23.0 %all-to-all-start.1 = ((f32[128,1,128]{2,1,0:T(1,128)}), f32[128,1,128]{2,1,0:T(1,128)S(1)}, u32[]{:S(2)}, u32[]{:S(2)}) async-start(f32[128,1,128]{2,1,0:T(1,128)} %get-tuple-element.28), calls=%async_computation.1 | async-start | bytes 131072 | tf_op jit(solution)/shard_map/all_to_all | solution.py:325
  67.2 7.8 %collective-permute-start.2 = (f32[264,128]{1,0:T(8,128)S(1)}, f32[264,128]{1,0:T(8,128)S(1)}, u32[]{:S(2)}, u32[]{:S(2)}) collective-permute-start(f32[264,128]{1,0:T(8,128)S(1)} %shard_map.86), channel_id=1, source_target_pairs={{0,2},{2,0},{1,3},{3,1},{4,6},{6,4},{5,7},{7,5},{8,10},{10,8},{9,1... | collective-permute-start | bytes 405512 | tf_op jit(solution)/shard_map/ppermute | solution.py:336

commit v7 on v6

--- a/solution.py
+++ b/solution.py
@@ -58,8 +58,8 @@
 
 
 def ends_kernel(
-    here, begin_hbm, span_hbm, carry_hbm, assay_hbm, coupling_hbm, x_hbm, d_hbm,
-    chunk, sent, shard_hbm,
+    here, za, core, begin_hbm, span_hbm, carry_hbm, assay_hbm, coupling_hbm, x_hbm, d_hbm,
+    chunk, sent, shard_hbm, scaled_hbm,
     begin, span, carry_ref, assay, coupling, x, d, shard, xs, ds, sems,
 ):
     pairs = [
@@ -79,8 +79,8 @@
     rest = jnp.zeros((SHARD - TRACKS - TRACKS // K, K), jnp.int32)
     shard[0:TRACKS, :] = coupling[...].astype(F32)
     shard[TRACKS:SHARD, :] = jnp.concatenate([assay[...], rest], axis=0).astype(F32)
-    leave = pltpu.make_async_copy(shard, shard_hbm, sems.at[len(pairs)])
-    leave.start()
+    leaves = [pltpu.make_async_copy(shard, shard_hbm, sems.at[len(pairs)])]
+    leaves[0].start()
     for copy in copies[2:]:
         copy.wait()
     keep, gain = gains(span[...])
@@ -89,6 +89,16 @@
         at, to = pl.ds(j * STEPS, STEPS), pl.ds(j * PAD, STEPS)
         xs[to, :] = gain * x[at, :].astype(F32)
         ds[to, :] = gain * d[at, :].astype(F32)
+    for j in range(2):
+        at = pl.multiple_of((core[0] * 4 + za[0] * 2 + j) * PAD, 8)
+        for k, ref in enumerate((xs, ds)):
+            to = scaled_hbm.at[k, pl.ds(j * STEPS, STEPS), :]
+            sem = sems.at[len(pairs) + len(leaves)]
+            leaves.append(pltpu.make_async_copy(ref.at[pl.ds(at, STEPS), :], to, sem))
+            leaves[-1].start()
+    chunk[3] = carry
+    chunk[4] = jnp.broadcast_to(keep, (CHUNKS, K))
+    chunk[5] = jnp.broadcast_to(gain, (CHUNKS, K))
     half = STEPS // 2
     ends = []
     for first in (0, half):
@@ -110,22 +120,21 @@
         mj = m[j : j + 1]
         mt, zt, vt = mj * mt, mj * zt + z[j : j + 1], mj * vt + v[j : j + 1]
     sent[...] = jnp.broadcast_to(jnp.concatenate([mt, zt, vt], axis=0)[None], sent.shape)
-    leave.wait()
+    for copy in leaves:
+        copy.wait()
 
 
 def prepare_kernel(
-    here, za, core, begin, span, carry_ref, x, d, chunk, shift, mine,
-    latent, moved, product, shift_t, both, xs, ds,
+    za, core, chunk, scaled, shift, shard, latent, moved, product, shift_t, mine
 ):
+    mine[...] = shard[...]
     at = core[0] * 4 + za[0] * 2
     start = pl.multiple_of(at * STEPS, QUARTER)
-    keep, gain = gains(span[...])
-    pair = masked(carry_ref[pl.ds(at, 2), :], here[0] * ROWS + start, begin)
+    pair, keep = chunk[3, pl.ds(at, 2), :], chunk[4, 0:1, :]
     carry = jnp.concatenate(
         [pair[j : j + 1, i : i + FINE] for j in range(2) for i in range(0, STEPS, FINE)], axis=0
     )
-    xs[...] = gain * x[pl.ds(start, QUARTER), :].astype(F32)
-    ds[...] = gain * d[pl.ds(start, QUARTER), :].astype(F32)
+    xs, ds = scaled.at[0], scaled.at[1]
     z, v = rows(xs, 0, FINE), rows(ds, 0, FINE)
     m = column(carry, 0) * keep
     for i in range(1, FINE):
@@ -162,12 +171,11 @@
     low = s - hi - mid
     blank = jnp.zeros((K - 3 * NVIEW, QUARTER), F32)
     shift_t[...] = jnp.concatenate([hi, mid, low, blank], axis=0).T.astype(BF16)
-    couple(mine, both)
-
-
-def couple(shards, both):
-    for side in range(2):
-        ref = shards.at[side]
+
+
+def couple_kernel(mine, other, both):
+    for side in range(4):
+        ref = (mine, other)[side // 2].at[side % 2]
         at = pl.ds(side * TRACKS, TRACKS)
         w = ref[0:TRACKS, :]
         both[0:K, at] = w.T.astype(BF16)
@@ -183,10 +191,9 @@
 
 
 def tracks_kernel(
-    here, got, latent_ref, moved_ref, product_ref, shift_t, mine, other,
-    pulled, sent, theirs,
+    here, got, latent_ref, moved_ref, product_ref, shift_t, both,
+    pulled, sent,
 ):
-    couple(other, theirs)
     ez = jnp.zeros((1, K), F32)
     ev = jnp.zeros((1, K), F32)
     for e in range(PEERS - 1):
@@ -201,7 +208,7 @@
     moved = (moved_ref[...] + product * ev).astype(BF16)
     p = jnp.zeros((QUARTER, K), F32)
     for side in range(4):
-        both, at = (mine, theirs)[side // 2], pl.ds(side % 2 * TRACKS, TRACKS)
+        at = pl.ds(side * TRACKS, TRACKS)
         log_rate = jnp.dot(latent, both[0 : 2 * K, at], preferred_element_type=F32)
         along = jnp.dot(moved, both[0:K, at], preferred_element_type=F32)
         weighted = (jnp.exp(log_rate) * along).astype(BF16)
@@ -213,14 +220,13 @@
     sent[...] = jnp.broadcast_to(total[None], sent.shape)
 
 
-def later_kernel(here, za, core, begin, span, carry_ref, got, weights, suffix, own_decay, decays):
+def later_kernel(here, za, core, chunk, got, weights, suffix, own_decay, decays):
     w = jnp.ones((1, K), F32)
     for e in range(PEERS):
         later = e > here[0]
         weights[e] = jnp.where(later, w, 0.0)
         w = jnp.where(later, w * got[(e - FIRST) % PEERS, 0:1, :], w)
-    keep, _ = gains(span[...])
-    carry = masked(carry_ref[...], here[0] * ROWS, begin)
+    carry, keep = chunk[3], chunk[4, 0:1, :]
     f = jnp.ones((CHUNKS, K), F32)
     for i in reversed(range(STEPS)):
         decay = column(carry, i) * keep
@@ -256,8 +262,8 @@
     )
 
 
-def finish_kernel(za, span, d, chunk, suffix, mine, other, out):
-    _, gain = gains(span[...])
+def finish_kernel(za, d, chunk, suffix, mine, other, out):
+    gain = chunk[5, 0:1, :]
     tail = (mine[0, QUARTER:PART, :] + mine[1, QUARTER:PART, :]) + (
         other[0, QUARTER:PART, :] + other[1, QUARTER:PART, :]
     )
@@ -282,12 +288,11 @@
     span = span.reshape(1, K)
     carry = carry.reshape(CHUNKS, STEPS)
     wide, quarter = ((ROWS, K), F32), ((QUARTER, K), F32)
-    packed = ((3 * K, 2 * TRACKS), BF16)
     pad = VMEM((CHUNKS * PAD, K), F32)
-    chunk, sent, shard = call(
+    chunk, sent, shard, scaled = call(
         ends_kernel,
-        [SMEM] + [HBM] * 7,
-        [((3, CHUNKS, K), F32), ((PEERS, 3, K), F32), ((SHARD, K), F32)],
+        [SMEM] * 3 + [HBM] * 7,
+        [((6, CHUNKS, K), F32), ((PEERS, 3, K), F32), ((SHARD, K), F32), ((2, QUARTER, K), F32)],
         [
             SMEM((3,), jnp.int32),
             VMEM((1, K), F32),
@@ -299,45 +304,45 @@
             VMEM((SHARD, K), F32),
             pad,
             pad,
-            pltpu.SemaphoreType.DMA((8,)),
+            pltpu.SemaphoreType.DMA((12,)),
         ],
         vmem=60,
-        spaces=[VMEM, VMEM, HBM],
-    )(here, begin, span, carry, assay.reshape(TRACKS // K, K), coupling, x, d)
+        spaces=[VMEM, VMEM, HBM, HBM],
+    )(here, za, core, begin, span, carry, assay.reshape(TRACKS // K, K), coupling, x, d)
     got = lax.all_to_all(sent, BINS, 0, 0, axis_index_groups=[ORDER], tiled=True)
 
     swap = [(0, 1), (1, 0)]
-    mine = lax.all_gather(shard, "core")
-    other = lax.ppermute(mine, "za", swap)
-    latent, moved, product, shift_t, both = call(
+    other = lax.ppermute(shard, "za", swap)
+    latent, moved, product, shift_t, mine = call(
         prepare_kernel,
-        [SMEM] * 4 + [VMEM] * 7,
-        [quarter, quarter, quarter, ((QUARTER, K), BF16), packed],
-        [VMEM(*quarter), VMEM(*quarter)],
-    )(here, za, core, begin, span, carry, x, d, chunk, shift, mine)
+        [SMEM] * 2 + [VMEM] * 4,
+        [quarter, quarter, quarter, ((QUARTER, K), BF16), ((SHARD, K), F32)],
+    )(za, core, chunk, scaled, shift, shard)
+    (both,) = call(couple_kernel, [VMEM] * 2, [((3 * K, 4 * TRACKS), BF16)])(
+        *(lax.all_gather(s, "core") for s in (mine, other))
+    )
 
     pulled, sent = call(
         tracks_kernel,
-        [SMEM] + [VMEM] * 7,
+        [SMEM] + [VMEM] * 6,
         [quarter, ((2 * PEERS, 1, K), F32)],
-        [VMEM(*packed)],
-    )(here, got, latent, moved, product, shift_t, both, other)
+    )(here, got, latent, moved, product, shift_t, both)
     late = lax.all_to_all(sent, (BINS, "zb"), 0, 0, tiled=True)
     received = lax.ppermute(pulled, "zb", swap)
     weights, suffix, own_decay = call(
         later_kernel,
-        [SMEM] * 4 + [VMEM] * 3,
+        [SMEM] * 3 + [VMEM] * 2,
         [((PEERS, 1, K), F32), wide, quarter],
         [VMEM(*wide)],
-    )(here, za, core, begin, span, carry, got)
+    )(here, za, core, chunk, got)
     (part,) = call(sum_kernel, [VMEM] * 5, [((PART, K), F32)], [VMEM(*quarter)])(
         weights, late.reshape(PEERS, 2, K), own_decay, pulled, received
     )
     other = lax.ppermute(part, "za", swap)
     mine = lax.all_gather(part, "core")
     other = lax.all_gather(other, "core")
-    (out,) = call(finish_kernel, [SMEM] + [VMEM] * 6, [wide])(
-        za, span, d, chunk, suffix, mine, other
+    (out,) = call(finish_kernel, [SMEM] + [VMEM] * 5, [wide])(
+        za, d, chunk, suffix, mine, other
     )
     return out
 

time: 80.8 us -> 78.3 us (0.969)
  waiting for transfers between devices: 15.7 us -> 12.1 us
  blocking collectives: 19 us -> 15.6 us
  local copies, waits for them, and re-layouts: 0.67 us -> 3.42 us
  starting transfers between devices: 36 us -> 38.3 us
    all_to_all x1, waiting for transfers between devices: 4.21 us -> 0.01 us  [local(): lax.all_to_all(sent, BINS, 0, 0, axis_index_groups=[ORDER], tiled=True)]
    all_gather x1 -> x2, blocking collectives: 9.13 us -> 5.41 us  [local(): lax.all_gather(s, 'core')]
    all_to_all x1, starting transfers between devices: 16.5 us -> 19.8 us  [local(): lax.all_to_all(sent, BINS, 0, 0, axis_index_groups=[ORDER], tiled=True)]
    ppermute x1, starting transfers between devices: 2.04 us -> 4.83 us  [local(): other = lax.ppermute(shard, 'za', swap)]
    unnamed x14 -> x12, local copies, waits for them, and re-layouts: 0.67 us -> 3.42 us
    all_to_all x1, starting transfers between devices: 10 us -> 7.52 us  [local(): late = lax.all_to_all(sent, (BINS, 'zb'), 0, 0, tiled=True)]
    ppermute x1, starting transfers between devices: 5.12 us -> 4 us  [local(): received = lax.ppermute(pulled, 'zb', swap)]
    pallas_call x5 -> x6, Pallas kernels: 8.45 us -> 7.81 us  [the longest x1 2.87 us: local(): call(ends_kernel, [SMEM] * 3 + [HBM] * 7, [((6, CHUNKS, K), F32), ((PEERS...]
  transfers between devices with their start and end apart: 5 -> 5, of which waited for: 2 -> 1; matrix products, arithmetic and copies ran while one was open for 0% -> 0% of each run, Pallas kernels for 4% -> 2%
where the time goes in v7:
time: 78.3 us; the launch traced here: 77.8 us
  starting transfers between devices  38.3 us (49%)
  blocking collectives  15.6 us (20%)
  waiting for transfers between devices  12.1 us (15%)
  Pallas kernels  8.24 us (11%)
  local copies, waits for them, and re-layouts  3.42 us (4%)
    all_to_all x1, starting transfers between devices, local(): lax.all_to_all(sent, BINS, 0, 0, axis_index_groups=[ORDER], tiled=True)  19.8 us
    all_to_all x1, waiting for transfers between devices, local(): late = lax.all_to_all(sent, (BINS, 'zb'), 0, 0, tiled=True)  12.1 us
    all_to_all x1, starting transfers between devices, local(): late = lax.all_to_all(sent, (BINS, 'zb'), 0, 0, tiled=True)  7.52 us
    all_gather x1, blocking collectives, local(): mine = lax.all_gather(part, 'core')  5.72 us
    all_gather x2, blocking collectives, local(): lax.all_gather(s, 'core')  5.41 us
    ppermute x1, starting transfers between devices, local(): other = lax.ppermute(shard, 'za', swap)  4.83 us
    all_gather x1, blocking collectives, local(): other = lax.all_gather(other, 'core')  4.42 us
    ppermute x1, starting transfers between devices, local(): received = lax.ppermute(pulled, 'zb', swap)  4 us
  transfers between devices with their start and end apart: 5, of which 1 were waited for; matrix products, arithmetic and copies ran while one was open for 0% of the time, Pallas kernels for 2%

profile of v7, /device:TPU:1, one launch (start us, length us, event | category | flops | bytes accessed | tf_op | source)
XLA Modules:
  0.0 77.8 jit_solution(1711351495885932679)
XLA Ops:
  0.0 2.9 %shard_map.82 = (f32[6,8,128]{2,1,0:T(8,128)}, f32[64,3,128]{2,1,0:T(4,128)}, f32[648,128]{1,0:T(8,128)}, f32[2,256,128]{2,1,0:T(8,128)}) custom-call(s32[1]{0:T(128)} %bitcast.1.here, s32[1]{0:T(128)} %bitcast.za, s32[1]{0:T(128)} %bitcast.2.core, s32[3]{0:T(128)} %begin_hbm.1, f32[1,128]{1,0:T(1,128)} %bitcast.18, f32[8,128]{1,0:T(8,128)} %bitcast.16, ...), custom_call_target="tpu_custom_call" | custom-call | tf_op jit(solution)/shard_map/pallas_call | solution.py:292
  2.9 4.8 %collective-permute-start = (f32[648,128]{1,0:T(8,128)}, f32[648,128]{1,0:T(8,128)S(1)}, u32[]{:S(2)}, u32[]{:S(2)}) collective-permute-start(f32[648,128]{1,0:T(8,128)} %get-tuple-element.24.shard), channel_id=1, source_target_pairs={{0,2},{2,0},{1,3},{3,1},{4,6},{6,4},{5,7},{7,5},{8,10},{10,8},{9,1... | collective-permute-start | bytes 995336 | tf_op jit(solution)/shard_map/ppermute | solution.py:315
  7.7 19.8 %all-to-all-start = ((f32[64,3,128]{2,1,0:T(4,128)}), f32[64,3,128]{2,1,0:T(4,128)S(1)}, u32[]{:S(2)}, u32[]{:S(2)}) async-start(f32[64,3,128]{2,1,0:T(4,128)} %get-tuple-element.20), calls=%async_computation | async-start | bytes 262144 | tf_op jit(solution)/shard_map/all_to_all | solution.py:312
  27.5 0.0 copy-start.1
  27.5 1.0 %copy-done.1 = f32[648,128]{1,0:T(8,128)S(1)} copy-done((f32[648,128]{1,0:T(8,128)S(1)}, f32[648,128]{1,0:T(8,128)}, u32[]{:S(2)}) %copy-start.1) | copy-done | bytes 331800
  28.5 0.0 copy-start.2
  28.5 0.9 %copy-done.2 = f32[2,256,128]{2,1,0:T(8,128)S(1)} copy-done((f32[2,256,128]{2,1,0:T(8,128)S(1)}, f32[2,256,128]{2,1,0:T(8,128)}, u32[]{:S(2)}) %copy-start.2) | copy-done | bytes 262168
  29.4 0.0 copy-start.3
  29.4 0.7 copy-done.3
  30.2 0.0 copy-start.5
  30.2 0.8 copy-done.5
  30.9 0.7 shard_map.84
  31.6 3.1 %all-gather = f32[1296,128]{1,0:T(8,128)S(1)} all-gather(f32[648,128]{1,0:T(8,128)S(1)} %get-tuple-element.29), channel_id=2, replica_groups=mesh['bins'=64,'zb'=2,'za'=2,'core'=2] {'core'}, dimensions={0}, use_global_device_ids=true | all-gather | bytes 995328 | tf_op jit(solution)/shard_map/all_gather | solution.py:322
  34.8 0.0 collective-permute-done
  34.8 2.3 %all-gather.1 = f32[1296,128]{1,0:T(8,128)S(1)} all-gather(f32[648,128]{1,0:T(8,128)S(1)} %collective-permute-done), channel_id=3, replica_groups=mesh['bins'=64,'zb'=2,'za'=2,'core'=2] {'core'}, dimensions={0}, use_global_device_ids=true | all-gather | bytes 995328 | tf_op jit(solution)/shard_map/all_gather | solution.py:322
  37.1 0.3 shard_map.85.both
  37.4 0.0 copy-start.4
  37.4 0.0 all-to-all-done.got
  37.4 0.0 copy-start
  37.4 2.2 %shard_map.86 = (f32[256,128]{1,0:T(8,128)S(1)}, f32[128,1,128]{2,1,0:T(1,128)}) custom-call(s32[1]{0:T(128)} %bitcast.1.here, f32[64,3,128]{2,1,0:T(4,128)S(1)} %all-to-all-done.got, f32[256,128]{1,0:T(8,128)S(1)} %get-tuple-element.25.latent_ref, f32[256,128]{1,0:T(8,128)S(1)} %get-tuple-element.26.moved_ref, ...), custom_call_target="tpu_custom_call" | custom-call | tf_op jit(solution)/shard_map/pallas_call | solution.py:325
  39.6 4.0 %collective-permute-start.1 = (f32[256,128]{1,0:T(8,128)S(1)}, f32[256,128]{1,0:T(8,128)S(1)}, u32[]{:S(2)}, u32[]{:S(2)}) collective-permute-start(f32[256,128]{1,0:T(8,128)S(1)} %get-tuple-element.32.mine), channel_id=1, source_target_pairs={{0,4},{4,0},{1,5},{5,1},{2,6},{6,2},{3,7},{7,3},{8,12},{12,8},{9,1... | collective-permute-start | bytes 393224 | tf_op jit(solution)/shard_map/ppermute | solution.py:331
  43.6 7.5 %all-to-all-start.1 = ((f32[128,1,128]{2,1,0:T(1,128)}), f32[128,1,128]{2,1,0:T(1,128)S(1)}, u32[]{:S(2)}, u32[]{:S(2)}) async-start(f32[128,1,128]{2,1,0:T(1,128)} %get-tuple-element.30), calls=%async_computation.1 | async-start | bytes 131072 | tf_op jit(solution)/shard_map/all_to_all | solution.py:330
  51.2 0.0 copy-done.4
  51.2 0.8 shard_map.83
  52.0 12.1 %all-to-all-done.1 = f32[128,1,128]{2,1,0:T(1,128)S(1)} async-done(((f32[128,1,128]{2,1,0:T(1,128)}), f32[128,1,128]{2,1,0:T(1,128)S(1)}, u32[]{:S(2)}, u32[]{:S(2)}) %all-to-all-start.1) | async-done | bytes 65568 | tf_op jit(solution)/shard_map/all_to_all | solution.py:330
  64.1 0.0 collective-permute-done.1.other
  64.1 0.4 shard_map.87
  64.5 2.2 %collective-permute-start.2 = (f32[264,128]{1,0:T(8,128)S(1)}, f32[264,128]{1,0:T(8,128)S(1)}, u32[]{:S(2)}, u32[]{:S(2)}) collective-permute-start(f32[264,128]{1,0:T(8,128)S(1)} %shard_map.87), channel_id=1, source_target_pairs={{0,2},{2,0},{1,3},{3,1},{4,6},{6,4},{5,7},{7,5},{8,10},{10,8},{9,1... | collective-permute-start | bytes 405512 | tf_op jit(solution)/shard_map/ppermute | solution.py:341
  66.7 5.7 %all-gather.2 = f32[528,128]{1,0:T(8,128)S(1)} all-gather(f32[264,128]{1,0:T(8,128)S(1)} %shard_map.87), channel_id=4, replica_groups=mesh['bins'=64,'zb'=2,'za'=2,'core'=2] {'core'}, dimensions={0}, use_global_device_ids=true | all-gather | bytes 405504 | tf_op jit(solution)/shard_map/all_gather | solution.py:342
  72.4 0.0 collective-permute-done.2
  72.4 4.4 %all-gather.3 = f32[528,128]{1,0:T(8,128)S(1)} all-gather(f32[264,128]{1,0:T(8,128)S(1)} %collective-permute-done.2), channel_id=5, replica_groups=mesh['bins'=64,'zb'=2,'za'=2,'core'=2] {'core'}, dimensions={0}, use_global_device_ids=true | all-gather | bytes 405504 | tf_op jit(solution)/shard_map/all_gather | solution.py:343
  76.9 0.0 copy-done
  76.9 0.9 %shard_map.88 = f32[1024,128]{1,0:T(8,128)} custom-call(s32[1]{0:T(128)} %bitcast.za, bf16[1024,128]{1,0:T(8,128)(2,1)S(1)} %copy-done, f32[6,8,128]{2,1,0:T(8,128)S(1)} %copy-done.4, f32[1024,128]{1,0:T(8,128)S(1)} %get-tuple-element.21.suffix, f32[2,264,128]{2,1,0:T(8,128)S(1)} %bitcast.13, f32[2,264,128]{2,1,0:T(8,128)S(1)} %bitcast.14), custom_call_target="tpu_custom_call" | custom-call | tf_op jit(solution)/shard_map/pallas_call | solution.py:344
Async XLA Ops:
  2.9 31.9 %collective-permute-start = (f32[648,128]{1,0:T(8,128)}, f32[648,128]{1,0:T(8,128)S(1)}, u32[]{:S(2)}, u32[]{:S(2)}) collective-permute-start(f32[648,128]{1,0:T(8,128)} %get-tuple-element.24.shard), channel_id=1, source_target_pairs={{0,2},{2,0},{1,3},{3,1},{4,6},{6,4},{5,7},{7,5},{8,10},{10,8},{9,1... | collective-permute-start | bytes 995336 | tf_op jit(solution)/shard_map/ppermute | solution.py:315
  7.7 29.7 %all-to-all-start = ((f32[64,3,128]{2,1,0:T(4,128)}), f32[64,3,128]{2,1,0:T(4,128)S(1)}, u32[]{:S(2)}, u32[]{:S(2)}) async-start(f32[64,3,128]{2,1,0:T(4,128)} %get-tuple-element.20), calls=%async_computation | async-start | bytes 262144 | tf_op jit(solution)/shard_map/all_to_all | solution.py:312
  27.5 1.0 %copy-start.1 = (f32[648,128]{1,0:T(8,128)S(1)}, f32[648,128]{1,0:T(8,128)}, u32[]{:S(2)}) copy-start(f32[648,128]{1,0:T(8,128)} %get-tuple-element.24.shard) | copy-start | bytes 995332
  28.5 0.9 %copy-start.2 = (f32[2,256,128]{2,1,0:T(8,128)S(1)}, f32[2,256,128]{2,1,0:T(8,128)}, u32[]{:S(2)}) copy-start(f32[2,256,128]{2,1,0:T(8,128)} %get-tuple-element.23.scaled) | copy-start | bytes 786436
  29.4 0.7 copy-start.3
  30.2 0.8 copy-start.5
  37.4 13.8 %copy-start.4 = (f32[6,8,128]{2,1,0:T(8,128)S(1)}, f32[6,8,128]{2,1,0:T(8,128)}, u32[]{:S(2)}) copy-start(f32[6,8,128]{2,1,0:T(8,128)} %get-tuple-element.19.chunk) | copy-start | bytes 73732
  37.4 39.5 %copy-start = (bf16[1024,128]{1,0:T(8,128)(2,1)S(1)}, bf16[1024,128]{1,0:T(8,128)(2,1)}, u32[]{:S(2)}) copy-start(bf16[1024,128]{1,0:T(8,128)(2,1)} %d.1) | copy-start | bytes 786436
  39.6 24.5 %collective-permute-start.1 = (f32[256,128]{1,0:T(8,128)S(1)}, f32[256,128]{1,0:T(8,128)S(1)}, u32[]{:S(2)}, u32[]{:S(2)}) collective-permute-start(f32[256,128]{1,0:T(8,128)S(1)} %get-tuple-element.32.mine), channel_id=1, source_target_pairs={{0,4},{4,0},{1,5},{5,1},{2,6},{6,2},{3,7},{7,3},{8,12},{12,8},{9,1... | collective-permute-start | bytes 393224 | tf_op jit(solution)/shard_map/ppermute | solution.py:331
  43.6 20.4 %all-to-all-start.1 = ((f32[128,1,128]{2,1,0:T(1,128)}), f32[128,1,128]{2,1,0:T(1,128)S(1)}, u32[]{:S(2)}, u32[]{:S(2)}) async-start(f32[128,1,128]{2,1,0:T(1,128)} %get-tuple-element.30), calls=%async_computation.1 | async-start | bytes 131072 | tf_op jit(solution)/shard_map/all_to_all | solution.py:330
  64.5 7.9 %collective-permute-start.2 = (f32[264,128]{1,0:T(8,128)S(1)}, f32[264,128]{1,0:T(8,128)S(1)}, u32[]{:S(2)}, u32[]{:S(2)}) collective-permute-start(f32[264,128]{1,0:T(8,128)S(1)} %shard_map.87), channel_id=1, source_target_pairs={{0,2},{2,0},{1,3},{3,1},{4,6},{6,4},{5,7},{7,5},{8,10},{10,8},{9,1... | collective-permute-start | bytes 405512 | tf_op jit(solution)/shard_map/ppermute | solution.py:341

commit v8 on v7

--- a/solution.py
+++ b/solution.py
@@ -9,6 +9,7 @@
 PEERS, NVIEW, TRACKS = 64, 8, 640
 SHARD = TRACKS + 8
 FINE = 32
+WIDE = FINE + 8
 PAD = STEPS + 8
 PART = QUARTER + 8
 BINS, VIEW = "bins", ("zb", "za", "core")
@@ -58,8 +59,8 @@
 
 
 def ends_kernel(
-    here, za, core, begin_hbm, span_hbm, carry_hbm, assay_hbm, coupling_hbm, x_hbm, d_hbm,
-    chunk, sent, shard_hbm, scaled_hbm,
+    here, begin_hbm, span_hbm, carry_hbm, assay_hbm, coupling_hbm, x_hbm, d_hbm,
+    chunk, sent, shard_hbm,
     begin, span, carry_ref, assay, coupling, x, d, shard, xs, ds, sems,
 ):
     pairs = [
@@ -79,8 +80,8 @@
     rest = jnp.zeros((SHARD - TRACKS - TRACKS // K, K), jnp.int32)
     shard[0:TRACKS, :] = coupling[...].astype(F32)
     shard[TRACKS:SHARD, :] = jnp.concatenate([assay[...], rest], axis=0).astype(F32)
-    leaves = [pltpu.make_async_copy(shard, shard_hbm, sems.at[len(pairs)])]
-    leaves[0].start()
+    leave = pltpu.make_async_copy(shard, shard_hbm, sems.at[len(pairs)])
+    leave.start()
     for copy in copies[2:]:
         copy.wait()
     keep, gain = gains(span[...])
@@ -89,13 +90,6 @@
         at, to = pl.ds(j * STEPS, STEPS), pl.ds(j * PAD, STEPS)
         xs[to, :] = gain * x[at, :].astype(F32)
         ds[to, :] = gain * d[at, :].astype(F32)
-    for j in range(2):
-        at = pl.multiple_of((core[0] * 4 + za[0] * 2 + j) * PAD, 8)
-        for k, ref in enumerate((xs, ds)):
-            to = scaled_hbm.at[k, pl.ds(j * STEPS, STEPS), :]
-            sem = sems.at[len(pairs) + len(leaves)]
-            leaves.append(pltpu.make_async_copy(ref.at[pl.ds(at, STEPS), :], to, sem))
-            leaves[-1].start()
     chunk[3] = carry
     chunk[4] = jnp.broadcast_to(keep, (CHUNKS, K))
     chunk[5] = jnp.broadcast_to(gain, (CHUNKS, K))
@@ -120,21 +114,21 @@
         mj = m[j : j + 1]
         mt, zt, vt = mj * mt, mj * zt + z[j : j + 1], mj * vt + v[j : j + 1]
     sent[...] = jnp.broadcast_to(jnp.concatenate([mt, zt, vt], axis=0)[None], sent.shape)
-    for copy in leaves:
-        copy.wait()
+    leave.wait()
 
 
 def prepare_kernel(
-    za, core, chunk, scaled, shift, shard, latent, moved, product, shift_t, mine
+    za, core, chunk, x, d, shift, shard, latent, moved, product, shift_t, mine, xs, ds
 ):
     mine[...] = shard[...]
     at = core[0] * 4 + za[0] * 2
     start = pl.multiple_of(at * STEPS, QUARTER)
-    pair, keep = chunk[3, pl.ds(at, 2), :], chunk[4, 0:1, :]
+    pair, keep, gain = chunk[3, pl.ds(at, 2), :], chunk[4, 0:1, :], chunk[5, 0:1, :]
     carry = jnp.concatenate(
         [pair[j : j + 1, i : i + FINE] for j in range(2) for i in range(0, STEPS, FINE)], axis=0
     )
-    xs, ds = scaled.at[0], scaled.at[1]
+    xs[...] = gain * x[pl.ds(start, QUARTER), :].astype(F32)
+    ds[...] = gain * d[pl.ds(start, QUARTER), :].astype(F32)
     z, v = rows(xs, 0, FINE), rows(ds, 0, FINE)
     m = column(carry, 0) * keep
     for i in range(1, FINE):
@@ -206,15 +200,12 @@
     latent = (latent_ref[...] + product * ez).astype(BF16)
     latent = jnp.concatenate([latent, shift_t[...]], axis=1)
     moved = (moved_ref[...] + product * ev).astype(BF16)
-    p = jnp.zeros((QUARTER, K), F32)
-    for side in range(4):
-        at = pl.ds(side * TRACKS, TRACKS)
-        log_rate = jnp.dot(latent, both[0 : 2 * K, at], preferred_element_type=F32)
-        along = jnp.dot(moved, both[0:K, at], preferred_element_type=F32)
-        weighted = (jnp.exp(log_rate) * along).astype(BF16)
-        blocks = both[2 * K : 3 * K, at]
-        coupling = jnp.concatenate([blocks[:, i : i + K] for i in range(0, TRACKS, K)], axis=0)
-        p = p + jnp.dot(weighted, coupling, preferred_element_type=F32)
+    log_rate = jnp.dot(latent, both[0 : 2 * K, :], preferred_element_type=F32)
+    along = jnp.dot(moved, both[0:K, :], preferred_element_type=F32)
+    weighted = (jnp.exp(log_rate) * along).astype(BF16)
+    blocks = both[2 * K : 3 * K, :]
+    coupling = jnp.concatenate([blocks[:, i : i + K] for i in range(0, 4 * TRACKS, K)], axis=0)
+    p = jnp.dot(weighted, coupling, preferred_element_type=F32)
     pulled[...] = p
     total = jnp.sum(product * p, axis=0, keepdims=True)
     sent[...] = jnp.broadcast_to(total[None], sent.shape)
@@ -235,16 +226,19 @@
         decays[to, :] = decay
         f = decay * f
     start = pl.multiple_of((core[0] * 4 + za[0] * 2) * STEPS, QUARTER)
-    own_decay[...] = decays[pl.ds(start, QUARTER), :]
+    for j in range(CHUNKS):
+        own_decay[pl.ds(j * WIDE, FINE), :] = decays[pl.ds(start + j * FINE, FINE), :]
 
 
 def sum_kernel(weights, late, own_decay, mine, other, out, p):
-    p[...] = mine[...] + other[...]
+    for j in range(CHUNKS):
+        at = pl.ds(j * FINE, FINE)
+        p[pl.ds(j * WIDE, FINE), :] = mine[at, :] + other[at, :]
     r = jnp.zeros((CHUNKS, K), F32)
     m = jnp.ones((CHUNKS, K), F32)
     for i in reversed(range(FINE)):
-        decay = rows(own_decay, i, FINE)
-        r = decay * (rows(p, i, FINE) + r)
+        decay = rows(own_decay, i, WIDE)
+        r = decay * (rows(p, i, WIDE) + r)
         m = decay * m
     entries = [jnp.zeros((1, K), F32)]
     for j in reversed(range(CHUNKS)):
@@ -252,9 +246,9 @@
     total = entries.pop()
     r = jnp.concatenate(entries[::-1], axis=0)
     for i in reversed(range(FINE)):
-        adjoint = rows(p, i, FINE) + r
+        adjoint = rows(p, i, WIDE) + r
         out[pl.ds(i, CHUNKS, stride=FINE), :] = adjoint
-        r = rows(own_decay, i, FINE) * adjoint
+        r = rows(own_decay, i, WIDE) * adjoint
     late = late[...]
     entry = jnp.sum(weights[...] * (late[:, 0:1, :] + late[:, 1:2, :]), axis=0)
     out[QUARTER:PART, :] = jnp.concatenate(
@@ -289,10 +283,10 @@
     carry = carry.reshape(CHUNKS, STEPS)
     wide, quarter = ((ROWS, K), F32), ((QUARTER, K), F32)
     pad = VMEM((CHUNKS * PAD, K), F32)
-    chunk, sent, shard, scaled = call(
+    chunk, sent, shard = call(
         ends_kernel,
-        [SMEM] * 3 + [HBM] * 7,
-        [((6, CHUNKS, K), F32), ((PEERS, 3, K), F32), ((SHARD, K), F32), ((2, QUARTER, K), F32)],
+        [SMEM] + [HBM] * 7,
+        [((6, CHUNKS, K), F32), ((PEERS, 3, K), F32), ((SHARD, K), F32)],
         [
             SMEM((3,), jnp.int32),
             VMEM((1, K), F32),
@@ -304,20 +298,21 @@
             VMEM((SHARD, K), F32),
             pad,
             pad,
-            pltpu.SemaphoreType.DMA((12,)),
+            pltpu.SemaphoreType.DMA((8,)),
         ],
         vmem=60,
-        spaces=[VMEM, VMEM, HBM, HBM],
-    )(here, za, core, begin, span, carry, assay.reshape(TRACKS // K, K), coupling, x, d)
+        spaces=[VMEM, VMEM, HBM],
+    )(here, begin, span, carry, assay.reshape(TRACKS // K, K), coupling, x, d)
     got = lax.all_to_all(sent, BINS, 0, 0, axis_index_groups=[ORDER], tiled=True)
 
     swap = [(0, 1), (1, 0)]
     other = lax.ppermute(shard, "za", swap)
     latent, moved, product, shift_t, mine = call(
         prepare_kernel,
-        [SMEM] * 2 + [VMEM] * 4,
+        [SMEM] * 2 + [VMEM] * 5,
         [quarter, quarter, quarter, ((QUARTER, K), BF16), ((SHARD, K), F32)],
-    )(za, core, chunk, scaled, shift, shard)
+        [VMEM(*quarter)] * 2,
+    )(za, core, chunk, x, d, shift, shard)
     (both,) = call(couple_kernel, [VMEM] * 2, [((3 * K, 4 * TRACKS), BF16)])(
         *(lax.all_gather(s, "core") for s in (mine, other))
     )
@@ -326,16 +321,17 @@
         tracks_kernel,
         [SMEM] + [VMEM] * 6,
         [quarter, ((2 * PEERS, 1, K), F32)],
+        vmem=32,
     )(here, got, latent, moved, product, shift_t, both)
     late = lax.all_to_all(sent, (BINS, "zb"), 0, 0, tiled=True)
     received = lax.ppermute(pulled, "zb", swap)
     weights, suffix, own_decay = call(
         later_kernel,
         [SMEM] * 3 + [VMEM] * 2,
-        [((PEERS, 1, K), F32), wide, quarter],
+        [((PEERS, 1, K), F32), wide, ((CHUNKS * WIDE, K), F32)],
         [VMEM(*wide)],
     )(here, za, core, chunk, got)
-    (part,) = call(sum_kernel, [VMEM] * 5, [((PART, K), F32)], [VMEM(*quarter)])(
+    (part,) = call(sum_kernel, [VMEM] * 5, [((PART, K), F32)], [VMEM((CHUNKS * WIDE, K), F32)])(
         weights, late.reshape(PEERS, 2, K), own_decay, pulled, received
     )
     other = lax.ppermute(part, "za", swap)

time: 78.3 us -> 77.5 us (0.990)
  Pallas kernels: 8.24 us -> 7.22 us
  local copies, waits for them, and re-layouts: 3.42 us -> 4.37 us
  starting transfers between devices: 38.3 us -> 37.5 us
    unnamed x12 -> x14, local copies, waits for them, and re-layouts: 3.42 us -> 4.37 us
    pallas_call x3, Pallas kernels: 4.02 us -> 3.18 us  [the longest x1 2.41 us: local(): call(ends_kernel, [SMEM] + [HBM] * 7, [((6, CHUNKS, K), F32), ((PEERS, 3,...]
    all_to_all x1, starting transfers between devices: 7.52 us -> 6.7 us  [local(): late = lax.all_to_all(sent, (BINS, 'zb'), 0, 0, tiled=True)]
where the time goes in v8:
time: 77.5 us; the launch traced here: 76.9 us
  starting transfers between devices  37.5 us (48%)
  blocking collectives  15.6 us (20%)
  waiting for transfers between devices  12.1 us (16%)
  Pallas kernels  7.22 us (9%)
  local copies, waits for them, and re-layouts  4.37 us (6%)
    all_to_all x1, starting transfers between devices, local(): lax.all_to_all(sent, BINS, 0, 0, axis_index_groups=[ORDER], tiled=True)  19.8 us
    all_to_all x1, waiting for transfers between devices, local(): late = lax.all_to_all(sent, (BINS, 'zb'), 0, 0, tiled=True)  12.1 us
    all_to_all x1, starting transfers between devices, local(): late = lax.all_to_all(sent, (BINS, 'zb'), 0, 0, tiled=True)  6.7 us
    all_gather x1, blocking collectives, local(): mine = lax.all_gather(part, 'core')  5.72 us
    all_gather x2, blocking collectives, local(): lax.all_gather(s, 'core')  5.41 us
    ppermute x1, starting transfers between devices, local(): other = lax.ppermute(shard, 'za', swap)  4.83 us
    all_gather x1, blocking collectives, local(): other = lax.all_gather(other, 'core')  4.42 us
    unnamed x14, local copies, waits for them, and re-layouts  4.37 us
  transfers between devices with their start and end apart: 5, of which 1 were waited for; matrix products, arithmetic and copies ran while one was open for 0% of the time, Pallas kernels for 2%

profile of v8, /device:TPU:1, one launch (start us, length us, event | category | flops | bytes accessed | tf_op | source)
XLA Modules:
  0.0 76.9 jit_solution(14088126208289011263)
XLA Ops:
  0.0 2.4 %shard_map.82 = (f32[6,8,128]{2,1,0:T(8,128)}, f32[64,3,128]{2,1,0:T(4,128)}, f32[648,128]{1,0:T(8,128)}) custom-call(s32[1]{0:T(128)} %bitcast.1.here, s32[3]{0:T(128)} %begin_hbm.1, f32[1,128]{1,0:T(1,128)} %bitcast.18, f32[8,128]{1,0:T(8,128)} %bitcast.16, s32[5,128]{1,0:T(8,128)} %bitcast.17, bf16[640,128]{1,0:T(8,128)(2,1)} %coupling_hbm.1, ...), custom_call_target="tpu_custom_call" | custom-call | tf_op jit(solution)/shard_map/pallas_call | solution.py:286
  2.4 4.8 %collective-permute-start = (f32[648,128]{1,0:T(8,128)}, f32[648,128]{1,0:T(8,128)S(1)}, u32[]{:S(2)}, u32[]{:S(2)}) collective-permute-start(f32[648,128]{1,0:T(8,128)} %get-tuple-element.22.shard), channel_id=1, source_target_pairs={{0,2},{2,0},{1,3},{3,1},{4,6},{6,4},{5,7},{7,5},{8,10},{10,8},{9,1... | collective-permute-start | bytes 995336 | tf_op jit(solution)/shard_map/ppermute | solution.py:309
  7.3 19.8 %all-to-all-start = ((f32[64,3,128]{2,1,0:T(4,128)}), f32[64,3,128]{2,1,0:T(4,128)S(1)}, u32[]{:S(2)}, u32[]{:S(2)}) async-start(f32[64,3,128]{2,1,0:T(4,128)} %get-tuple-element.19), calls=%async_computation | async-start | bytes 262144 | tf_op jit(solution)/shard_map/all_to_all | solution.py:306
  27.0 0.0 copy-start
  27.1 0.9 %copy-done = bf16[1024,128]{1,0:T(8,128)(2,1)S(1)} copy-done((bf16[1024,128]{1,0:T(8,128)(2,1)S(1)}, bf16[1024,128]{1,0:T(8,128)(2,1)}, u32[]{:S(2)}) %copy-start) | copy-done | bytes 262168
  28.0 0.0 copy-start.2
  28.0 0.9 %copy-done.2 = bf16[1024,128]{1,0:T(8,128)(2,1)S(1)} copy-done((bf16[1024,128]{1,0:T(8,128)(2,1)S(1)}, bf16[1024,128]{1,0:T(8,128)(2,1)}, u32[]{:S(2)}) %copy-start.2) | copy-done | bytes 262168
  29.0 0.0 copy-start.3
  29.0 1.0 %copy-done.3 = f32[648,128]{1,0:T(8,128)S(1)} copy-done((f32[648,128]{1,0:T(8,128)S(1)}, f32[648,128]{1,0:T(8,128)}, u32[]{:S(2)}) %copy-start.3) | copy-done | bytes 331800
  29.9 0.0 copy-start.4
  29.9 0.7 copy-done.4
  30.7 0.0 copy-start.6
  30.7 0.8 copy-done.6
  31.4 0.6 shard_map.84
  32.0 3.1 %all-gather = f32[1296,128]{1,0:T(8,128)S(1)} all-gather(f32[648,128]{1,0:T(8,128)S(1)} %get-tuple-element.27), channel_id=2, replica_groups=mesh['bins'=64,'zb'=2,'za'=2,'core'=2] {'core'}, dimensions={0}, use_global_device_ids=true | all-gather | bytes 995328 | tf_op jit(solution)/shard_map/all_gather | solution.py:317
  35.2 0.0 collective-permute-done
  35.2 2.3 %all-gather.1 = f32[1296,128]{1,0:T(8,128)S(1)} all-gather(f32[648,128]{1,0:T(8,128)S(1)} %collective-permute-done), channel_id=3, replica_groups=mesh['bins'=64,'zb'=2,'za'=2,'core'=2] {'core'}, dimensions={0}, use_global_device_ids=true | all-gather | bytes 995328 | tf_op jit(solution)/shard_map/all_gather | solution.py:317
  37.4 0.3 shard_map.85.both
  37.7 0.0 copy-start.5
  37.7 0.0 all-to-all-done.got
  37.7 0.0 copy-start.1
  37.8 2.1 %shard_map.86 = (f32[256,128]{1,0:T(8,128)S(1)}, f32[128,1,128]{2,1,0:T(1,128)}) custom-call(s32[1]{0:T(128)} %bitcast.1.here, f32[64,3,128]{2,1,0:T(4,128)S(1)} %all-to-all-done.got, f32[256,128]{1,0:T(8,128)S(1)} %get-tuple-element.23.latent_ref, f32[256,128]{1,0:T(8,128)S(1)} %get-tuple-element.24.moved_ref, ...), custom_call_target="tpu_custom_call" | custom-call | tf_op jit(solution)/shard_map/pallas_call | solution.py:320
  39.8 4.0 %collective-permute-start.1 = (f32[256,128]{1,0:T(8,128)S(1)}, f32[256,128]{1,0:T(8,128)S(1)}, u32[]{:S(2)}, u32[]{:S(2)}) collective-permute-start(f32[256,128]{1,0:T(8,128)S(1)} %get-tuple-element.30.mine), channel_id=1, source_target_pairs={{0,4},{4,0},{1,5},{5,1},{2,6},{6,2},{3,7},{7,3},{8,12},{12,8},{9,1... | collective-permute-start | bytes 393224 | tf_op jit(solution)/shard_map/ppermute | solution.py:327
  43.8 6.7 %all-to-all-start.1 = ((f32[128,1,128]{2,1,0:T(1,128)}), f32[128,1,128]{2,1,0:T(1,128)S(1)}, u32[]{:S(2)}, u32[]{:S(2)}) async-start(f32[128,1,128]{2,1,0:T(1,128)} %get-tuple-element.28), calls=%async_computation.1 | async-start | bytes 131072 | tf_op jit(solution)/shard_map/all_to_all | solution.py:326
  50.5 0.0 copy-done.5
  50.5 0.8 shard_map.83
  51.3 12.1 %all-to-all-done.1 = f32[128,1,128]{2,1,0:T(1,128)S(1)} async-done(((f32[128,1,128]{2,1,0:T(1,128)}), f32[128,1,128]{2,1,0:T(1,128)S(1)}, u32[]{:S(2)}, u32[]{:S(2)}) %all-to-all-start.1) | async-done | bytes 65568 | tf_op jit(solution)/shard_map/all_to_all | solution.py:326
  63.4 0.0 collective-permute-done.1.other
  63.4 0.2 shard_map.87
  63.7 2.2 %collective-permute-start.2 = (f32[264,128]{1,0:T(8,128)S(1)}, f32[264,128]{1,0:T(8,128)S(1)}, u32[]{:S(2)}, u32[]{:S(2)}) collective-permute-start(f32[264,128]{1,0:T(8,128)S(1)} %shard_map.87), channel_id=1, source_target_pairs={{0,2},{2,0},{1,3},{3,1},{4,6},{6,4},{5,7},{7,5},{8,10},{10,8},{9,1... | collective-permute-start | bytes 405512 | tf_op jit(solution)/shard_map/ppermute | solution.py:337
  65.8 5.7 %all-gather.2 = f32[528,128]{1,0:T(8,128)S(1)} all-gather(f32[264,128]{1,0:T(8,128)S(1)} %shard_map.87), channel_id=4, replica_groups=mesh['bins'=64,'zb'=2,'za'=2,'core'=2] {'core'}, dimensions={0}, use_global_device_ids=true | all-gather | bytes 405504 | tf_op jit(solution)/shard_map/all_gather | solution.py:338
  71.6 0.0 collective-permute-done.2
  71.6 4.4 %all-gather.3 = f32[528,128]{1,0:T(8,128)S(1)} all-gather(f32[264,128]{1,0:T(8,128)S(1)} %collective-permute-done.2), channel_id=5, replica_groups=mesh['bins'=64,'zb'=2,'za'=2,'core'=2] {'core'}, dimensions={0}, use_global_device_ids=true | all-gather | bytes 405504 | tf_op jit(solution)/shard_map/all_gather | solution.py:339
  76.0 0.0 copy-done.1
  76.0 0.9 %shard_map.88 = f32[1024,128]{1,0:T(8,128)} custom-call(s32[1]{0:T(128)} %bitcast.za, bf16[1024,128]{1,0:T(8,128)(2,1)S(1)} %copy-done.1, f32[6,8,128]{2,1,0:T(8,128)S(1)} %copy-done.5, f32[1024,128]{1,0:T(8,128)S(1)} %get-tuple-element.20.suffix, f32[2,264,128]{2,1,0:T(8,128)S(1)} %bitcast.13, f32[2,264,128]{2,1,0:T(8,128)S(1)} %bitcast.14), custom_call_target="tpu_custom_call" | custom-call | tf_op jit(solution)/shard_map/pallas_call | solution.py:340
Async XLA Ops:
  2.4 32.7 %collective-permute-start = (f32[648,128]{1,0:T(8,128)}, f32[648,128]{1,0:T(8,128)S(1)}, u32[]{:S(2)}, u32[]{:S(2)}) collective-permute-start(f32[648,128]{1,0:T(8,128)} %get-tuple-element.22.shard), channel_id=1, source_target_pairs={{0,2},{2,0},{1,3},{3,1},{4,6},{6,4},{5,7},{7,5},{8,10},{10,8},{9,1... | collective-permute-start | bytes 995336 | tf_op jit(solution)/shard_map/ppermute | solution.py:309
  7.3 30.5 %all-to-all-start = ((f32[64,3,128]{2,1,0:T(4,128)}), f32[64,3,128]{2,1,0:T(4,128)S(1)}, u32[]{:S(2)}, u32[]{:S(2)}) async-start(f32[64,3,128]{2,1,0:T(4,128)} %get-tuple-element.19), calls=%async_computation | async-start | bytes 262144 | tf_op jit(solution)/shard_map/all_to_all | solution.py:306
  27.0 1.0 %copy-start = (bf16[1024,128]{1,0:T(8,128)(2,1)S(1)}, bf16[1024,128]{1,0:T(8,128)(2,1)}, u32[]{:S(2)}) copy-start(bf16[1024,128]{1,0:T(8,128)(2,1)} %d.3) | copy-start | bytes 786436
  28.0 0.9 %copy-start.2 = (bf16[1024,128]{1,0:T(8,128)(2,1)S(1)}, bf16[1024,128]{1,0:T(8,128)(2,1)}, u32[]{:S(2)}) copy-start(bf16[1024,128]{1,0:T(8,128)(2,1)} %x.1) | copy-start | bytes 786436
  29.0 1.0 %copy-start.3 = (f32[648,128]{1,0:T(8,128)S(1)}, f32[648,128]{1,0:T(8,128)}, u32[]{:S(2)}) copy-start(f32[648,128]{1,0:T(8,128)} %get-tuple-element.22.shard) | copy-start | bytes 995332
  29.9 0.7 copy-start.4
  30.7 0.8 copy-start.6
  37.7 12.8 %copy-start.5 = (f32[6,8,128]{2,1,0:T(8,128)S(1)}, f32[6,8,128]{2,1,0:T(8,128)}, u32[]{:S(2)}) copy-start(f32[6,8,128]{2,1,0:T(8,128)} %get-tuple-element.18.chunk) | copy-start | bytes 73732
  37.7 38.2 %copy-start.1 = (bf16[1024,128]{1,0:T(8,128)(2,1)S(1)}, bf16[1024,128]{1,0:T(8,128)(2,1)}, u32[]{:S(2)}) copy-start(bf16[1024,128]{1,0:T(8,128)(2,1)} %d.3) | copy-start | bytes 786436
  39.8 23.6 %collective-permute-start.1 = (f32[256,128]{1,0:T(8,128)S(1)}, f32[256,128]{1,0:T(8,128)S(1)}, u32[]{:S(2)}, u32[]{:S(2)}) collective-permute-start(f32[256,128]{1,0:T(8,128)S(1)} %get-tuple-element.30.mine), channel_id=1, source_target_pairs={{0,4},{4,0},{1,5},{5,1},{2,6},{6,2},{3,7},{7,3},{8,12},{12,8},{9,1... | collective-permute-start | bytes 393224 | tf_op jit(solution)/shard_map/ppermute | solution.py:327
  43.8 19.6 %all-to-all-start.1 = ((f32[128,1,128]{2,1,0:T(1,128)}), f32[128,1,128]{2,1,0:T(1,128)S(1)}, u32[]{:S(2)}, u32[]{:S(2)}) async-start(f32[128,1,128]{2,1,0:T(1,128)} %get-tuple-element.28), calls=%async_computation.1 | async-start | bytes 131072 | tf_op jit(solution)/shard_map/all_to_all | solution.py:326
  63.7 7.9 %collective-permute-start.2 = (f32[264,128]{1,0:T(8,128)S(1)}, f32[264,128]{1,0:T(8,128)S(1)}, u32[]{:S(2)}, u32[]{:S(2)}) collective-permute-start(f32[264,128]{1,0:T(8,128)S(1)} %shard_map.87), channel_id=1, source_target_pairs={{0,2},{2,0},{1,3},{3,1},{4,6},{6,4},{5,7},{7,5},{8,10},{10,8},{9,1... | collective-permute-start | bytes 405512 | tf_op jit(solution)/shard_map/ppermute | solution.py:337

commit v9 on v8

--- a/solution.py
+++ b/solution.py
@@ -73,7 +73,7 @@
         (d_hbm, d),
     ]
     copies = [pltpu.make_async_copy(a, b, sems.at[i]) for i, (a, b) in enumerate(pairs)]
-    for copy in copies:
+    for copy in copies[5:] + copies[:5]:
         copy.start()
     copies[0].wait()
     copies[1].wait()
@@ -256,12 +256,13 @@
     )
 
 
-def finish_kernel(za, d, chunk, suffix, mine, other, out):
+def finish_kernel(za, d, chunk, suffix, mine, other, out_hbm, out, sems):
     gain = chunk[5, 0:1, :]
     tail = (mine[0, QUARTER:PART, :] + mine[1, QUARTER:PART, :]) + (
         other[0, QUARTER:PART, :] + other[1, QUARTER:PART, :]
     )
     entry = tail[1:2]
+    copies = []
     for quarter in reversed(range(4)):
         own = za[0] == quarter % 2
 
@@ -273,7 +274,12 @@
             entering = entry if j else chunk[0, quarter * 2 + 1 : quarter * 2 + 2, :] * entry
             adjoint = part(pl.ds(j * STEPS, STEPS)) + suffix[at, :] * entering
             out[at, :] = gain * adjoint + d[at, :].astype(F32)
+            sem = sems.at[quarter * 2 + j]
+            copies.append(pltpu.make_async_copy(out.at[at, :], out_hbm.at[at, :], sem))
+            copies[-1].start()
         entry = chunk[0, quarter * 2 : quarter * 2 + 1, :] * entering + part(pl.ds(QUARTER, 8))[0:1]
+    for copy in copies:
+        copy.wait()
 
 
 def local(x, d, coupling, assay, shift, span, carry, begin):
@@ -337,7 +343,8 @@
     other = lax.ppermute(part, "za", swap)
     mine = lax.all_gather(part, "core")
     other = lax.all_gather(other, "core")
-    (out,) = call(finish_kernel, [SMEM] + [VMEM] * 5, [wide])(
+    scratch = [VMEM(*wide), pltpu.SemaphoreType.DMA((CHUNKS,))]
+    (out,) = call(finish_kernel, [SMEM] + [VMEM] * 5, [wide], scratch, spaces=[HBM])(
         za, d, chunk, suffix, mine, other
     )
     return out

time: 77.5 us -> 77.6 us (level)
  no operation moved by 1% of the time
where the time goes in v9:
time: 77.6 us; the launch traced here: 77 us
  starting transfers between devices  37.5 us (48%)
  blocking collectives  15.6 us (20%)
  waiting for transfers between devices  12.1 us (16%)
  Pallas kernels  7.32 us (9%)
  local copies, waits for them, and re-layouts  4.37 us (6%)
    all_to_all x1, starting transfers between devices, local(): lax.all_to_all(sent, BINS, 0, 0, axis_index_groups=[ORDER], tiled=True)  19.8 us
    all_to_all x1, waiting for transfers between devices, local(): late = lax.all_to_all(sent, (BINS, 'zb'), 0, 0, tiled=True)  12.1 us
    all_to_all x1, starting transfers between devices, local(): late = lax.all_to_all(sent, (BINS, 'zb'), 0, 0, tiled=True)  6.7 us
    all_gather x1, blocking collectives, local(): mine = lax.all_gather(part, 'core')  5.72 us
    all_gather x2, blocking collectives, local(): lax.all_gather(s, 'core')  5.41 us
    ppermute x1, starting transfers between devices, local(): other = lax.ppermute(shard, 'za', swap)  4.83 us
    all_gather x1, blocking collectives, local(): other = lax.all_gather(other, 'core')  4.42 us
    unnamed x14, local copies, waits for them, and re-layouts  4.37 us
  transfers between devices with their start and end apart: 5, of which 1 were waited for; matrix products, arithmetic and copies ran while one was open for 0% of the time, Pallas kernels for 2%

profile of v9, /device:TPU:1, one launch (start us, length us, event | category | flops | bytes accessed | tf_op | source)
XLA Modules:
  0.0 77.0 jit_solution(11029796585101642781)
XLA Ops:
  0.0 2.6 %shard_map.82 = (f32[6,8,128]{2,1,0:T(8,128)}, f32[64,3,128]{2,1,0:T(4,128)}, f32[648,128]{1,0:T(8,128)}) custom-call(s32[1]{0:T(128)} %bitcast.1.here, s32[3]{0:T(128)} %begin_hbm.1, f32[1,128]{1,0:T(1,128)} %bitcast.18, f32[8,128]{1,0:T(8,128)} %bitcast.16, s32[5,128]{1,0:T(8,128)} %bitcast.17, bf16[640,128]{1,0:T(8,128)(2,1)} %coupling_hbm.1, ...), custom_call_target="tpu_custom_call" | custom-call | tf_op jit(solution)/shard_map/pallas_call | solution.py:292
  2.6 4.8 %collective-permute-start = (f32[648,128]{1,0:T(8,128)}, f32[648,128]{1,0:T(8,128)S(1)}, u32[]{:S(2)}, u32[]{:S(2)}) collective-permute-start(f32[648,128]{1,0:T(8,128)} %get-tuple-element.22.shard), channel_id=1, source_target_pairs={{0,2},{2,0},{1,3},{3,1},{4,6},{6,4},{5,7},{7,5},{8,10},{10,8},{9,1... | collective-permute-start | bytes 995336 | tf_op jit(solution)/shard_map/ppermute | solution.py:315
  7.4 19.8 %all-to-all-start = ((f32[64,3,128]{2,1,0:T(4,128)}), f32[64,3,128]{2,1,0:T(4,128)S(1)}, u32[]{:S(2)}, u32[]{:S(2)}) async-start(f32[64,3,128]{2,1,0:T(4,128)} %get-tuple-element.19), calls=%async_computation | async-start | bytes 262144 | tf_op jit(solution)/shard_map/all_to_all | solution.py:312
  27.2 0.0 copy-start
  27.2 0.9 %copy-done = bf16[1024,128]{1,0:T(8,128)(2,1)S(1)} copy-done((bf16[1024,128]{1,0:T(8,128)(2,1)S(1)}, bf16[1024,128]{1,0:T(8,128)(2,1)}, u32[]{:S(2)}) %copy-start) | copy-done | bytes 262168
  28.2 0.0 copy-start.2
  28.2 0.9 %copy-done.2 = bf16[1024,128]{1,0:T(8,128)(2,1)S(1)} copy-done((bf16[1024,128]{1,0:T(8,128)(2,1)S(1)}, bf16[1024,128]{1,0:T(8,128)(2,1)}, u32[]{:S(2)}) %copy-start.2) | copy-done | bytes 262168
  29.1 0.0 copy-start.3
  29.1 1.0 %copy-done.3 = f32[648,128]{1,0:T(8,128)S(1)} copy-done((f32[648,128]{1,0:T(8,128)S(1)}, f32[648,128]{1,0:T(8,128)}, u32[]{:S(2)}) %copy-start.3) | copy-done | bytes 331800
  30.1 0.0 copy-start.4
  30.1 0.7 copy-done.4
  30.8 0.0 copy-start.6
  30.8 0.8 copy-done.6
  31.6 0.6 shard_map.84
  32.2 3.1 %all-gather = f32[1296,128]{1,0:T(8,128)S(1)} all-gather(f32[648,128]{1,0:T(8,128)S(1)} %get-tuple-element.27), channel_id=2, replica_groups=mesh['bins'=64,'zb'=2,'za'=2,'core'=2] {'core'}, dimensions={0}, use_global_device_ids=true | all-gather | bytes 995328 | tf_op jit(solution)/shard_map/all_gather | solution.py:323
  35.3 0.0 collective-permute-done
  35.3 2.3 %all-gather.1 = f32[1296,128]{1,0:T(8,128)S(1)} all-gather(f32[648,128]{1,0:T(8,128)S(1)} %collective-permute-done), channel_id=3, replica_groups=mesh['bins'=64,'zb'=2,'za'=2,'core'=2] {'core'}, dimensions={0}, use_global_device_ids=true | all-gather | bytes 995328 | tf_op jit(solution)/shard_map/all_gather | solution.py:323
  37.6 0.3 shard_map.85.both
  37.9 0.0 copy-start.5
  37.9 0.0 all-to-all-done.got
  37.9 0.0 copy-start.1
  37.9 2.1 %shard_map.86 = (f32[256,128]{1,0:T(8,128)S(1)}, f32[128,1,128]{2,1,0:T(1,128)}) custom-call(s32[1]{0:T(128)} %bitcast.1.here, f32[64,3,128]{2,1,0:T(4,128)S(1)} %all-to-all-done.got, f32[256,128]{1,0:T(8,128)S(1)} %get-tuple-element.23.latent_ref, f32[256,128]{1,0:T(8,128)S(1)} %get-tuple-element.24.moved_ref, ...), custom_call_target="tpu_custom_call" | custom-call | tf_op jit(solution)/shard_map/pallas_call | solution.py:326
  40.0 4.0 %collective-permute-start.1 = (f32[256,128]{1,0:T(8,128)S(1)}, f32[256,128]{1,0:T(8,128)S(1)}, u32[]{:S(2)}, u32[]{:S(2)}) collective-permute-start(f32[256,128]{1,0:T(8,128)S(1)} %get-tuple-element.30.mine), channel_id=1, source_target_pairs={{0,4},{4,0},{1,5},{5,1},{2,6},{6,2},{3,7},{7,3},{8,12},{12,8},{9,1... | collective-permute-start | bytes 393224 | tf_op jit(solution)/shard_map/ppermute | solution.py:333
  44.0 6.7 %all-to-all-start.1 = ((f32[128,1,128]{2,1,0:T(1,128)}), f32[128,1,128]{2,1,0:T(1,128)S(1)}, u32[]{:S(2)}, u32[]{:S(2)}) async-start(f32[128,1,128]{2,1,0:T(1,128)} %get-tuple-element.28), calls=%async_computation.1 | async-start | bytes 131072 | tf_op jit(solution)/shard_map/all_to_all | solution.py:332
  50.7 0.0 copy-done.5
  50.7 0.8 shard_map.83
  51.5 12.1 %all-to-all-done.1 = f32[128,1,128]{2,1,0:T(1,128)S(1)} async-done(((f32[128,1,128]{2,1,0:T(1,128)}), f32[128,1,128]{2,1,0:T(1,128)S(1)}, u32[]{:S(2)}, u32[]{:S(2)}) %all-to-all-start.1) | async-done | bytes 65568 | tf_op jit(solution)/shard_map/all_to_all | solution.py:332
  63.6 0.0 collective-permute-done.1.other
  63.6 0.2 shard_map.87
  63.8 2.2 %collective-permute-start.2 = (f32[264,128]{1,0:T(8,128)S(1)}, f32[264,128]{1,0:T(8,128)S(1)}, u32[]{:S(2)}, u32[]{:S(2)}) collective-permute-start(f32[264,128]{1,0:T(8,128)S(1)} %shard_map.87), channel_id=1, source_target_pairs={{0,2},{2,0},{1,3},{3,1},{4,6},{6,4},{5,7},{7,5},{8,10},{10,8},{9,1... | collective-permute-start | bytes 405512 | tf_op jit(solution)/shard_map/ppermute | solution.py:343
  66.0 5.7 %all-gather.2 = f32[528,128]{1,0:T(8,128)S(1)} all-gather(f32[264,128]{1,0:T(8,128)S(1)} %shard_map.87), channel_id=4, replica_groups=mesh['bins'=64,'zb'=2,'za'=2,'core'=2] {'core'}, dimensions={0}, use_global_device_ids=true | all-gather | bytes 405504 | tf_op jit(solution)/shard_map/all_gather | solution.py:344
  71.7 0.0 collective-permute-done.2
  71.7 4.4 %all-gather.3 = f32[528,128]{1,0:T(8,128)S(1)} all-gather(f32[264,128]{1,0:T(8,128)S(1)} %collective-permute-done.2), channel_id=5, replica_groups=mesh['bins'=64,'zb'=2,'za'=2,'core'=2] {'core'}, dimensions={0}, use_global_device_ids=true | all-gather | bytes 405504 | tf_op jit(solution)/shard_map/all_gather | solution.py:345
  76.1 0.0 copy-done.1
  76.1 0.9 %shard_map.88 = f32[1024,128]{1,0:T(8,128)} custom-call(s32[1]{0:T(128)} %bitcast.za, bf16[1024,128]{1,0:T(8,128)(2,1)S(1)} %copy-done.1, f32[6,8,128]{2,1,0:T(8,128)S(1)} %copy-done.5, f32[1024,128]{1,0:T(8,128)S(1)} %get-tuple-element.20.suffix, f32[2,264,128]{2,1,0:T(8,128)S(1)} %bitcast.13, f32[2,264,128]{2,1,0:T(8,128)S(1)} %bitcast.14), custom_call_target="tpu_custom_call" | custom-call | tf_op jit(solution)/shard_map/pallas_call | solution.py:347
Async XLA Ops:
  2.6 32.7 %collective-permute-start = (f32[648,128]{1,0:T(8,128)}, f32[648,128]{1,0:T(8,128)S(1)}, u32[]{:S(2)}, u32[]{:S(2)}) collective-permute-start(f32[648,128]{1,0:T(8,128)} %get-tuple-element.22.shard), channel_id=1, source_target_pairs={{0,2},{2,0},{1,3},{3,1},{4,6},{6,4},{5,7},{7,5},{8,10},{10,8},{9,1... | collective-permute-start | bytes 995336 | tf_op jit(solution)/shard_map/ppermute | solution.py:315
  7.4 30.5 %all-to-all-start = ((f32[64,3,128]{2,1,0:T(4,128)}), f32[64,3,128]{2,1,0:T(4,128)S(1)}, u32[]{:S(2)}, u32[]{:S(2)}) async-start(f32[64,3,128]{2,1,0:T(4,128)} %get-tuple-element.19), calls=%async_computation | async-start | bytes 262144 | tf_op jit(solution)/shard_map/all_to_all | solution.py:312
  27.2 1.0 %copy-start = (bf16[1024,128]{1,0:T(8,128)(2,1)S(1)}, bf16[1024,128]{1,0:T(8,128)(2,1)}, u32[]{:S(2)}) copy-start(bf16[1024,128]{1,0:T(8,128)(2,1)} %d.3) | copy-start | bytes 786436
  28.2 0.9 %copy-start.2 = (bf16[1024,128]{1,0:T(8,128)(2,1)S(1)}, bf16[1024,128]{1,0:T(8,128)(2,1)}, u32[]{:S(2)}) copy-start(bf16[1024,128]{1,0:T(8,128)(2,1)} %x.1) | copy-start | bytes 786436
  29.1 1.0 %copy-start.3 = (f32[648,128]{1,0:T(8,128)S(1)}, f32[648,128]{1,0:T(8,128)}, u32[]{:S(2)}) copy-start(f32[648,128]{1,0:T(8,128)} %get-tuple-element.22.shard) | copy-start | bytes 995332
  30.1 0.7 copy-start.4
  30.8 0.8 copy-start.6
  37.9 12.8 %copy-start.5 = (f32[6,8,128]{2,1,0:T(8,128)S(1)}, f32[6,8,128]{2,1,0:T(8,128)}, u32[]{:S(2)}) copy-start(f32[6,8,128]{2,1,0:T(8,128)} %get-tuple-element.18.chunk) | copy-start | bytes 73732
  37.9 38.2 %copy-start.1 = (bf16[1024,128]{1,0:T(8,128)(2,1)S(1)}, bf16[1024,128]{1,0:T(8,128)(2,1)}, u32[]{:S(2)}) copy-start(bf16[1024,128]{1,0:T(8,128)(2,1)} %d.3) | copy-start | bytes 786436
  40.0 23.6 %collective-permute-start.1 = (f32[256,128]{1,0:T(8,128)S(1)}, f32[256,128]{1,0:T(8,128)S(1)}, u32[]{:S(2)}, u32[]{:S(2)}) collective-permute-start(f32[256,128]{1,0:T(8,128)S(1)} %get-tuple-element.30.mine), channel_id=1, source_target_pairs={{0,4},{4,0},{1,5},{5,1},{2,6},{6,2},{3,7},{7,3},{8,12},{12,8},{9,1... | collective-permute-start | bytes 393224 | tf_op jit(solution)/shard_map/ppermute | solution.py:333
  44.0 19.6 %all-to-all-start.1 = ((f32[128,1,128]{2,1,0:T(1,128)}), f32[128,1,128]{2,1,0:T(1,128)S(1)}, u32[]{:S(2)}, u32[]{:S(2)}) async-start(f32[128,1,128]{2,1,0:T(1,128)} %get-tuple-element.28), calls=%async_computation.1 | async-start | bytes 131072 | tf_op jit(solution)/shard_map/all_to_all | solution.py:332
  63.8 7.9 %collective-permute-start.2 = (f32[264,128]{1,0:T(8,128)S(1)}, f32[264,128]{1,0:T(8,128)S(1)}, u32[]{:S(2)}, u32[]{:S(2)}) collective-permute-start(f32[264,128]{1,0:T(8,128)S(1)} %shard_map.87), channel_id=1, source_target_pairs={{0,2},{2,0},{1,3},{3,1},{4,6},{6,4},{5,7},{7,5},{8,10},{10,8},{9,1... | collective-permute-start | bytes 405512 | tf_op jit(solution)/shard_map/ppermute | solution.py:343

commit v10 on v8

--- a/solution.py
+++ b/solution.py
@@ -13,7 +13,7 @@
 PAD = STEPS + 8
 PART = QUARTER + 8
 BINS, VIEW = "bins", ("zb", "za", "core")
-FIRST = 38
+FIRST = 34
 ORDER = [(FIRST + i) % PEERS for i in range(PEERS)]
 VMEM, SMEM, HBM = pltpu.VMEM, pltpu.SMEM, pltpu.HBM
 F32, BF16 = jnp.float32, jnp.bfloat16

time: 77.5 us -> 77.3 us (level)
  blocking collectives: 15.6 us -> 14.3 us
  starting transfers between devices: 37.5 us -> 38.6 us
    all_to_all x1, starting transfers between devices: 6.7 us -> 8.82 us  [local(): late = lax.all_to_all(sent, (BINS, 'zb'), 0, 0, tiled=True)]
    all_gather x1, blocking collectives: 5.72 us -> 4.2 us  [local(): mine = lax.all_gather(part, 'core')]
    all_to_all x1, starting transfers between devices: 19.8 us -> 18.7 us  [local(): lax.all_to_all(sent, BINS, 0, 0, axis_index_groups=[ORDER], tiled=True)]
where the time goes in v10:
time: 77.3 us; the launch traced here: 76.8 us
  starting transfers between devices  38.6 us (50%)
  blocking collectives  14.3 us (18%)
  waiting for transfers between devices  12.1 us (16%)
  Pallas kernels  7.22 us (9%)
  local copies, waits for them, and re-layouts  4.37 us (6%)
    all_to_all x1, starting transfers between devices, local(): lax.all_to_all(sent, BINS, 0, 0, axis_index_groups=[ORDER], tiled=True)  18.7 us
    all_to_all x1, waiting for transfers between devices, local(): late = lax.all_to_all(sent, (BINS, 'zb'), 0, 0, tiled=True)  12.1 us
    all_to_all x1, starting transfers between devices, local(): late = lax.all_to_all(sent, (BINS, 'zb'), 0, 0, tiled=True)  8.82 us
    all_gather x2, blocking collectives, local(): lax.all_gather(s, 'core')  5.69 us
    ppermute x1, starting transfers between devices, local(): other = lax.ppermute(shard, 'za', swap)  4.83 us
    all_gather x1, blocking collectives, local(): other = lax.all_gather(other, 'core')  4.42 us
    unnamed x14, local copies, waits for them, and re-layouts  4.37 us
    all_gather x1, blocking collectives, local(): mine = lax.all_gather(part, 'core')  4.2 us
  transfers between devices with their start and end apart: 5, of which 1 were waited for; matrix products, arithmetic and copies ran while one was open for 0% of the time, Pallas kernels for 2%

profile of v10, /device:TPU:1, one launch (start us, length us, event | category | flops | bytes accessed | tf_op | source)
XLA Modules:
  0.0 76.8 jit_solution(10845984158222243044)
XLA Ops:
  0.0 2.4 %shard_map.82 = (f32[6,8,128]{2,1,0:T(8,128)}, f32[64,3,128]{2,1,0:T(4,128)}, f32[648,128]{1,0:T(8,128)}) custom-call(s32[1]{0:T(128)} %bitcast.1.here, s32[3]{0:T(128)} %begin_hbm.1, f32[1,128]{1,0:T(1,128)} %bitcast.18, f32[8,128]{1,0:T(8,128)} %bitcast.16, s32[5,128]{1,0:T(8,128)} %bitcast.17, bf16[640,128]{1,0:T(8,128)(2,1)} %coupling_hbm.1, ...), custom_call_target="tpu_custom_call" | custom-call | tf_op jit(solution)/shard_map/pallas_call | solution.py:286
  2.4 4.8 %collective-permute-start = (f32[648,128]{1,0:T(8,128)}, f32[648,128]{1,0:T(8,128)S(1)}, u32[]{:S(2)}, u32[]{:S(2)}) collective-permute-start(f32[648,128]{1,0:T(8,128)} %get-tuple-element.22.shard), channel_id=1, source_target_pairs={{0,2},{2,0},{1,3},{3,1},{4,6},{6,4},{5,7},{7,5},{8,10},{10,8},{9,1... | collective-permute-start | bytes 995336 | tf_op jit(solution)/shard_map/ppermute | solution.py:309
  7.3 18.7 %all-to-all-start = ((f32[64,3,128]{2,1,0:T(4,128)}), f32[64,3,128]{2,1,0:T(4,128)S(1)}, u32[]{:S(2)}, u32[]{:S(2)}) async-start(f32[64,3,128]{2,1,0:T(4,128)} %get-tuple-element.19), calls=%async_computation | async-start | bytes 262144 | tf_op jit(solution)/shard_map/all_to_all | solution.py:306
  26.0 0.0 copy-start
  26.0 0.9 %copy-done = bf16[1024,128]{1,0:T(8,128)(2,1)S(1)} copy-done((bf16[1024,128]{1,0:T(8,128)(2,1)S(1)}, bf16[1024,128]{1,0:T(8,128)(2,1)}, u32[]{:S(2)}) %copy-start) | copy-done | bytes 262168
  27.0 0.0 copy-start.2
  27.0 0.9 %copy-done.2 = bf16[1024,128]{1,0:T(8,128)(2,1)S(1)} copy-done((bf16[1024,128]{1,0:T(8,128)(2,1)S(1)}, bf16[1024,128]{1,0:T(8,128)(2,1)}, u32[]{:S(2)}) %copy-start.2) | copy-done | bytes 262168
  27.9 0.0 copy-start.3
  27.9 1.0 %copy-done.3 = f32[648,128]{1,0:T(8,128)S(1)} copy-done((f32[648,128]{1,0:T(8,128)S(1)}, f32[648,128]{1,0:T(8,128)}, u32[]{:S(2)}) %copy-start.3) | copy-done | bytes 331800
  28.9 0.0 copy-start.4
  28.9 0.7 copy-done.4
  29.6 0.0 copy-start.6
  29.6 0.8 copy-done.6
  30.4 0.6 shard_map.84
  31.0 3.4 %all-gather = f32[1296,128]{1,0:T(8,128)S(1)} all-gather(f32[648,128]{1,0:T(8,128)S(1)} %get-tuple-element.27), channel_id=2, replica_groups=mesh['bins'=64,'zb'=2,'za'=2,'core'=2] {'core'}, dimensions={0}, use_global_device_ids=true | all-gather | bytes 995328 | tf_op jit(solution)/shard_map/all_gather | solution.py:317
  34.4 0.0 collective-permute-done
  34.4 2.3 %all-gather.1 = f32[1296,128]{1,0:T(8,128)S(1)} all-gather(f32[648,128]{1,0:T(8,128)S(1)} %collective-permute-done), channel_id=3, replica_groups=mesh['bins'=64,'zb'=2,'za'=2,'core'=2] {'core'}, dimensions={0}, use_global_device_ids=true | all-gather | bytes 995328 | tf_op jit(solution)/shard_map/all_gather | solution.py:317
  36.7 0.3 shard_map.85.both
  37.0 0.0 copy-start.5
  37.0 0.0 all-to-all-done.got
  37.0 0.0 copy-start.1
  37.0 2.1 %shard_map.86 = (f32[256,128]{1,0:T(8,128)S(1)}, f32[128,1,128]{2,1,0:T(1,128)}) custom-call(s32[1]{0:T(128)} %bitcast.1.here, f32[64,3,128]{2,1,0:T(4,128)S(1)} %all-to-all-done.got, f32[256,128]{1,0:T(8,128)S(1)} %get-tuple-element.23.latent_ref, f32[256,128]{1,0:T(8,128)S(1)} %get-tuple-element.24.moved_ref, ...), custom_call_target="tpu_custom_call" | custom-call | tf_op jit(solution)/shard_map/pallas_call | solution.py:320
  39.0 4.0 %collective-permute-start.1 = (f32[256,128]{1,0:T(8,128)S(1)}, f32[256,128]{1,0:T(8,128)S(1)}, u32[]{:S(2)}, u32[]{:S(2)}) collective-permute-start(f32[256,128]{1,0:T(8,128)S(1)} %get-tuple-element.30.mine), channel_id=1, source_target_pairs={{0,4},{4,0},{1,5},{5,1},{2,6},{6,2},{3,7},{7,3},{8,12},{12,8},{9,1... | collective-permute-start | bytes 393224 | tf_op jit(solution)/shard_map/ppermute | solution.py:327
  43.1 8.8 %all-to-all-start.1 = ((f32[128,1,128]{2,1,0:T(1,128)}), f32[128,1,128]{2,1,0:T(1,128)S(1)}, u32[]{:S(2)}, u32[]{:S(2)}) async-start(f32[128,1,128]{2,1,0:T(1,128)} %get-tuple-element.28), calls=%async_computation.1 | async-start | bytes 131072 | tf_op jit(solution)/shard_map/all_to_all | solution.py:326
  51.9 0.0 copy-done.5
  51.9 0.8 shard_map.83
  52.7 12.1 %all-to-all-done.1 = f32[128,1,128]{2,1,0:T(1,128)S(1)} async-done(((f32[128,1,128]{2,1,0:T(1,128)}), f32[128,1,128]{2,1,0:T(1,128)S(1)}, u32[]{:S(2)}, u32[]{:S(2)}) %all-to-all-start.1) | async-done | bytes 65568 | tf_op jit(solution)/shard_map/all_to_all | solution.py:326
  64.8 0.0 collective-permute-done.1.other
  64.8 0.2 shard_map.87
  65.0 2.2 %collective-permute-start.2 = (f32[264,128]{1,0:T(8,128)S(1)}, f32[264,128]{1,0:T(8,128)S(1)}, u32[]{:S(2)}, u32[]{:S(2)}) collective-permute-start(f32[264,128]{1,0:T(8,128)S(1)} %shard_map.87), channel_id=1, source_target_pairs={{0,2},{2,0},{1,3},{3,1},{4,6},{6,4},{5,7},{7,5},{8,10},{10,8},{9,1... | collective-permute-start | bytes 405512 | tf_op jit(solution)/shard_map/ppermute | solution.py:337
  67.2 4.2 %all-gather.2 = f32[528,128]{1,0:T(8,128)S(1)} all-gather(f32[264,128]{1,0:T(8,128)S(1)} %shard_map.87), channel_id=4, replica_groups=mesh['bins'=64,'zb'=2,'za'=2,'core'=2] {'core'}, dimensions={0}, use_global_device_ids=true | all-gather | bytes 405504 | tf_op jit(solution)/shard_map/all_gather | solution.py:338
  71.4 0.0 collective-permute-done.2
  71.4 4.4 %all-gather.3 = f32[528,128]{1,0:T(8,128)S(1)} all-gather(f32[264,128]{1,0:T(8,128)S(1)} %collective-permute-done.2), channel_id=5, replica_groups=mesh['bins'=64,'zb'=2,'za'=2,'core'=2] {'core'}, dimensions={0}, use_global_device_ids=true | all-gather | bytes 405504 | tf_op jit(solution)/shard_map/all_gather | solution.py:339
  75.8 0.0 copy-done.1
  75.8 0.9 %shard_map.88 = f32[1024,128]{1,0:T(8,128)} custom-call(s32[1]{0:T(128)} %bitcast.za, bf16[1024,128]{1,0:T(8,128)(2,1)S(1)} %copy-done.1, f32[6,8,128]{2,1,0:T(8,128)S(1)} %copy-done.5, f32[1024,128]{1,0:T(8,128)S(1)} %get-tuple-element.20.suffix, f32[2,264,128]{2,1,0:T(8,128)S(1)} %bitcast.13, f32[2,264,128]{2,1,0:T(8,128)S(1)} %bitcast.14), custom_call_target="tpu_custom_call" | custom-call | tf_op jit(solution)/shard_map/pallas_call | solution.py:340
Async XLA Ops:
  2.4 32.0 %collective-permute-start = (f32[648,128]{1,0:T(8,128)}, f32[648,128]{1,0:T(8,128)S(1)}, u32[]{:S(2)}, u32[]{:S(2)}) collective-permute-start(f32[648,128]{1,0:T(8,128)} %get-tuple-element.22.shard), channel_id=1, source_target_pairs={{0,2},{2,0},{1,3},{3,1},{4,6},{6,4},{5,7},{7,5},{8,10},{10,8},{9,1... | collective-permute-start | bytes 995336 | tf_op jit(solution)/shard_map/ppermute | solution.py:309
  7.3 29.7 %all-to-all-start = ((f32[64,3,128]{2,1,0:T(4,128)}), f32[64,3,128]{2,1,0:T(4,128)S(1)}, u32[]{:S(2)}, u32[]{:S(2)}) async-start(f32[64,3,128]{2,1,0:T(4,128)} %get-tuple-element.19), calls=%async_computation | async-start | bytes 262144 | tf_op jit(solution)/shard_map/all_to_all | solution.py:306
  26.0 1.0 %copy-start = (bf16[1024,128]{1,0:T(8,128)(2,1)S(1)}, bf16[1024,128]{1,0:T(8,128)(2,1)}, u32[]{:S(2)}) copy-start(bf16[1024,128]{1,0:T(8,128)(2,1)} %d.3) | copy-start | bytes 786436
  27.0 0.9 %copy-start.2 = (bf16[1024,128]{1,0:T(8,128)(2,1)S(1)}, bf16[1024,128]{1,0:T(8,128)(2,1)}, u32[]{:S(2)}) copy-start(bf16[1024,128]{1,0:T(8,128)(2,1)} %x.1) | copy-start | bytes 786436
  27.9 1.0 %copy-start.3 = (f32[648,128]{1,0:T(8,128)S(1)}, f32[648,128]{1,0:T(8,128)}, u32[]{:S(2)}) copy-start(f32[648,128]{1,0:T(8,128)} %get-tuple-element.22.shard) | copy-start | bytes 995332
  28.9 0.7 copy-start.4
  29.6 0.8 copy-start.6
  37.0 14.9 %copy-start.5 = (f32[6,8,128]{2,1,0:T(8,128)S(1)}, f32[6,8,128]{2,1,0:T(8,128)}, u32[]{:S(2)}) copy-start(f32[6,8,128]{2,1,0:T(8,128)} %get-tuple-element.18.chunk) | copy-start | bytes 73732
  37.0 38.9 %copy-start.1 = (bf16[1024,128]{1,0:T(8,128)(2,1)S(1)}, bf16[1024,128]{1,0:T(8,128)(2,1)}, u32[]{:S(2)}) copy-start(bf16[1024,128]{1,0:T(8,128)(2,1)} %d.3) | copy-start | bytes 786436
  39.0 25.8 %collective-permute-start.1 = (f32[256,128]{1,0:T(8,128)S(1)}, f32[256,128]{1,0:T(8,128)S(1)}, u32[]{:S(2)}, u32[]{:S(2)}) collective-permute-start(f32[256,128]{1,0:T(8,128)S(1)} %get-tuple-element.30.mine), channel_id=1, source_target_pairs={{0,4},{4,0},{1,5},{5,1},{2,6},{6,2},{3,7},{7,3},{8,12},{12,8},{9,1... | collective-permute-start | bytes 393224 | tf_op jit(solution)/shard_map/ppermute | solution.py:327
  43.1 21.7 %all-to-all-start.1 = ((f32[128,1,128]{2,1,0:T(1,128)}), f32[128,1,128]{2,1,0:T(1,128)S(1)}, u32[]{:S(2)}, u32[]{:S(2)}) async-start(f32[128,1,128]{2,1,0:T(1,128)} %get-tuple-element.28), calls=%async_computation.1 | async-start | bytes 131072 | tf_op jit(solution)/shard_map/all_to_all | solution.py:326
  65.0 6.4 %collective-permute-start.2 = (f32[264,128]{1,0:T(8,128)S(1)}, f32[264,128]{1,0:T(8,128)S(1)}, u32[]{:S(2)}, u32[]{:S(2)}) collective-permute-start(f32[264,128]{1,0:T(8,128)S(1)} %shard_map.87), channel_id=1, source_target_pairs={{0,2},{2,0},{1,3},{3,1},{4,6},{6,4},{5,7},{7,5},{8,10},{10,8},{9,1... | collective-permute-start | bytes 405512 | tf_op jit(solution)/shard_map/ppermute | solution.py:337
